TPU v7x, 32 devices: a whole 2x2x4 slice. The times are simulated.
32 devices in a mesh: stream: 4 (over y, x), span: 8 (over z, core).
Axes of the slice: x: 2, y: 2, z: 4, core: 2. Of those that a mesh axis runs over, the one named last changes fastest.
Arguments:
- forcing: float32 [5, 256, 128, 128], P(None, 'span', 'stream'), may hold values from -6 to 6
- initial_state: float32 [128, 5, 2, 128, 128], P('span', None, None, 'stream'), may hold values from -4 to 4
- diagonal: float32 [5, 128, 128], replicated, may hold values from 1.5 to 4
- span_speed: float32 [5], replicated, may hold values from 0.3 to 3
- coupling: float32 [4, 5, 5], replicated, may hold values from -1.25 to 1.25
- stiffener_mask: int32 [128, 128], replicated, may hold values 0 or 1
- face_index: int32 [2, 4096], P(None, ('stream', 'span')), may hold values from 0 to 1023
- mode_shapes: float32 [2, 2, 4096], P(None, None, ('stream', 'span')), may hold values from -12 to 12
Outputs:
- flow: float32 [128, 5, 2, 128, 128], P('span', None, None, 'stream')
- forces: float32 [2, 2], replicated
All inputs are finite; a program needn't handle non-finite values.
Results may differ from a plain program's by a relative error of at most 0.00025.
Values sent between devices are 32-bit elements; how exact they have to be, the bound alone decides.
No kernel may reach another device: no remote copies, remote signals or barrier semaphores. Data moves between devices by JAX's collectives and lax.ppermute only.
A program may use at most 192 MiB of HBM per device.

v0:
```python
import functools
import math

import jax
import jax.numpy as jnp
from jax import lax
from jax.experimental import pallas as pl
from jax.experimental.pallas import tpu as pltpu
from jax.sharding import PartitionSpec as P

HI = lax.Precision.HIGHEST


def swap(value, axis, dist):
    count = lax.axis_size(axis)
    return lax.ppermute(value, axis, [(i, i ^ dist) for i in range(count)])


def halo(head, tail, axis):
    ends = lax.axis_size(axis) - 1
    left = lax.ppermute(tail, axis, [(i, i + 1) for i in range(ends)])
    right = lax.ppermute(head, axis, [(i + 1, i) for i in range(ends)])
    return left, right


def wave_rows(owners, blocks, me, waves, cells, span_total):
    k = (jnp.stack([me ^ d for d in owners])[:, None] * waves + jnp.arange(waves, dtype=jnp.int32)).reshape(-1)
    z = (jnp.stack([me ^ d for d in blocks])[:, None] * cells + jnp.arange(cells, dtype=jnp.int32)).reshape(-1)
    index = (k[:, None] * z[None, :]) % span_total
    phase = index.astype(jnp.float32) * (2.0 * math.pi / span_total)
    tab = jnp.stack([jnp.cos(phase), -jnp.sin(phase)], axis=1) * (1.0 / math.sqrt(span_total))
    return tab.reshape(len(owners), waves, 2, len(blocks) * cells)


def near_terms(ext, cpl, r, row, comps, normal):
    lane = lax.broadcasted_iota(jnp.int32, (8, normal), 1)
    parts = []
    for c in range(comps):
        mid = ext[c, r, pl.ds(row, 8), :]
        up = jnp.where(lane < normal - 1, pltpu.roll(mid, normal - 1, 1), 0.0)
        down = jnp.where(lane > 0, pltpu.roll(mid, 1, 1), 0.0)
        parts.append((ext[c, r, pl.ds(row + 1, 8), :], ext[c, r, pl.ds(row - 1, 8), :], up, down))
    out = []
    for c in range(comps):
        acc = None
        for e in range(comps):
            for d in range(4):
                term = cpl[d, c, e] * parts[e][d]
                acc = term if acc is None else acc + term
        out.append(acc)
    return out


def near_kernel(cpl, state, left, right, near, ext):
    waves, comps, _, rows, normal = state.shape

    def one(k, carry):
        ext[:, :, 8 : 8 + rows, :] = state[k]
        ext[:, :, 7:8, :] = left[k]
        ext[:, :, 8 + rows : 9 + rows, :] = right[k]
        for r in range(2):
            for t in range(rows // 8):
                sums = near_terms(ext, cpl, r, 8 + 8 * t, comps, normal)
                for c in range(comps):
                    near[k, c, r, 8 * t : 8 * t + 8, :] = sums[c]
        return carry

    lax.fori_loop(0, waves, one, 0)


def rotate(re, im, a, b, keep):
    scale = keep / (a * a + b * b)
    return (a * re + b * im) * scale, (a * im - b * re) * scale


def edge_kernel(speed, rhs, near, diag, keep, first):
    waves, comps, _, rows, _ = rhs.shape
    cells = near.shape[3]
    half = rows // 2
    base = pl.program_id(0) * waves

    def one(k, carry):
        for c in range(comps):
            b = speed[base + k, c]
            for lo, at in ((0, 0), (half, cells - half)):
                for t in range(0, half, 8):
                    src, dst = slice(at + t, at + t + 8), slice(lo + t, lo + t + 8)
                    re = rhs[k, c, 0, dst, :] - near[k, c, 0, src, :]
                    im = rhs[k, c, 1, dst, :] - near[k, c, 1, src, :]
                    out = rotate(re, im, diag[c, src, :], b, keep[src, :])
                    first[k, c, 0, dst, :], first[k, c, 1, dst, :] = out
        return carry

    lax.fori_loop(0, waves, one, 0)


def last_kernel(start, cpl, speed, edge_rhs, edge_first, mid_own, mid_far, near, left, right, diag, keep, *rest):
    flow, ext = rest[-2:]
    waves, comps, _, rows, normal = flow.shape
    half = edge_rhs.shape[3] // 2
    base = (start + pl.program_id(0)) * waves

    def one(k, carry):
        ext[:, :, 7:8, :] = left[k]
        ext[:, :, 8 : 8 + half, :] = edge_first[k, :, :, :half, :]
        ext[:, :, 8 + rows - half : 8 + rows, :] = edge_first[k, :, :, half:, :]
        ext[:, :, 8 + rows : 9 + rows, :] = right[k]
        for c in range(comps):
            b = speed[base + k, c]
            for t in range(half, rows - half, 8):
                at = slice(t - half, t - half + 8)
                src = slice(t, t + 8)
                re = mid_own[k, c, 0, at, :] + mid_far[k, c, 0, at, :] - near[k, c, 0, src, :]
                im = mid_own[k, c, 1, at, :] + mid_far[k, c, 1, at, :] - near[k, c, 1, src, :]
                out = rotate(re, im, diag[c, src, :], b, keep[src, :])
                ext[c, 0, 8 + t : 16 + t, :], ext[c, 1, 8 + t : 16 + t, :] = out
        for t in range(0, rows, 8):
            src = slice(t, t + 8)
            sums = [near_terms(ext, cpl, r, 8 + t, comps, normal) for r in range(2)]
            for c in range(comps):
                if t < half or t >= rows - half:
                    lo = t if t < half else t - (rows - 2 * half)
                    rhs = [edge_rhs[k, c, r, lo : lo + 8, :] for r in range(2)]
                else:
                    at = slice(t - half, t - half + 8)
                    rhs = [mid_own[k, c, r, at, :] + mid_far[k, c, r, at, :] for r in range(2)]
                b = speed[base + k, c]
                out = rotate(rhs[0] - sums[0][c], rhs[1] - sums[1][c], diag[c, src, :], b, keep[src, :])
                flow[k, c, 0, src, :], flow[k, c, 1, src, :] = out
        return carry

    lax.fori_loop(0, waves, one, 0)


def by_wave(shape, step, offset=0):
    rest = len(shape) - 1
    return pl.BlockSpec((step,) + tuple(shape[1:]), lambda i: (i + offset,) + (0,) * rest)


def whole(shape):
    return pl.BlockSpec(tuple(shape), lambda i: (0,) * len(shape))


SMEM = pl.BlockSpec(memory_space=pltpu.SMEM)
PARAMS = pltpu.CompilerParams(vmem_limit_bytes=48 * 1024 * 1024)


def cost(flops, moved):
    return pl.CostEstimate(flops=int(flops), bytes_accessed=int(moved), transcendentals=0)


def shards(forcing, initial_state, diagonal, span_speed, coupling, stiffener_mask, face_index, mode_shapes):
    span_count = lax.axis_size("span")
    stream_count = lax.axis_size("stream")
    me = lax.axis_index("span")
    comps, cells, rows, normal = forcing.shape
    waves = initial_state.shape[0]
    span_total = cells * span_count
    half_span = span_count // 2
    modes = face_index.shape[0]
    edge = rows // 4
    table = functools.partial(wave_rows, me=me, waves=waves, cells=cells, span_total=span_total)
    inner = [d for d in (1 << i for i in range(20)) if d < half_span]

    edges = jnp.concatenate([forcing[:, :, :edge], forcing[:, :, rows - edge :]], axis=2)
    middle = forcing[:, :, edge : rows - edge]
    edges_far = swap(edges, "span", half_span)
    blocks, held = [0], middle
    for d in reversed(inner):
        held = jnp.concatenate([held, swap(held, "span", d)], axis=1)
        blocks = blocks + [b ^ d for b in blocks]
    both = jnp.einsum("czxy,dkrz->dkcrxy", held, table([half_span, 0], blocks), precision=HI)
    mid_own = both[1]
    mid_far = swap(both[0], "span", half_span)

    first_cell = lax.axis_index("stream") * rows
    keep = lax.dynamic_slice_in_dim((1 - stiffener_mask).astype(jnp.float32), first_cell, rows, 0)
    diag = lax.dynamic_slice_in_dim(diagonal, first_cell, rows, 1)
    k_mine = me * waves + jnp.arange(waves, dtype=jnp.int32)
    speed = (k_mine.astype(jnp.float32) * (2.0 * math.pi / span_total))[:, None] * span_speed[None, :]
    left0, right0 = halo(initial_state[:, :, :, :1], initial_state[:, :, :, rows - 1 :], "stream")
    step = 2
    grid = (waves // step,)
    state_shape = initial_state.shape
    side_shape = left0.shape
    ext_shape = (comps, 2, rows + 16, normal)
    size = initial_state.size
    near0 = pl.pallas_call(
        near_kernel,
        grid=grid,
        in_specs=[SMEM, by_wave(state_shape, step), by_wave(side_shape, step), by_wave(side_shape, step)],
        out_specs=by_wave(state_shape, step),
        out_shape=jax.ShapeDtypeStruct(state_shape, jnp.float32),
        scratch_shapes=[pltpu.VMEM(ext_shape, jnp.float32)],
        compiler_params=PARAMS,
        cost_estimate=cost(40 * size, 8 * size),
        name="near",
    )(coupling, initial_state, left0, right0)

    pair = jnp.concatenate([edges, edges_far], axis=1)
    owners = [0]
    for d in inner:
        owners = owners + [o ^ d for o in owners]
    part = jnp.einsum("czxy,dkrz->dkcrxy", pair, table(owners, [0, half_span]), precision=HI)
    held_owners = owners
    for d in inner:
        mine = [i for i, o in enumerate(held_owners) if not o & d]
        other = [held_owners.index(held_owners[i] ^ d) for i in mine]
        sent = jnp.stack([part[i] for i in other]) if len(other) > 1 else part[other[0]][None]
        got = swap(sent, "span", d)
        part = jnp.stack([part[i] + got[n] for n, i in enumerate(mine)])
        held_owners = [held_owners[i] for i in mine]
    edge_rhs = part[0]
    edge_shape = edge_rhs.shape
    edge_first = pl.pallas_call(
        edge_kernel,
        grid=grid,
        in_specs=[SMEM, by_wave(edge_shape, step), by_wave(state_shape, step), whole(diag.shape), whole(keep.shape)],
        out_specs=by_wave(edge_shape, step),
        out_shape=jax.ShapeDtypeStruct(edge_shape, jnp.float32),
        compiler_params=PARAMS,
        cost_estimate=cost(10 * size, 8 * size),
        name="edge",
    )(speed, edge_rhs, near0, diag, keep)
    left1, right1 = halo(edge_first[:, :, :, :1], edge_first[:, :, :, 2 * edge - 1 :], "stream")

    flow = pl.pallas_call(
        functools.partial(last_kernel, 0),
        grid=grid,
        in_specs=[SMEM, SMEM]
        + [by_wave(edge_shape, step)] * 2
        + [by_wave(mid_own.shape, step)] * 2
        + [by_wave(state_shape, step)]
        + [by_wave(side_shape, step)] * 2
        + [whole(diag.shape), whole(keep.shape)],
        out_specs=by_wave(state_shape, step),
        out_shape=jax.ShapeDtypeStruct(state_shape, jnp.float32),
        scratch_shapes=[pltpu.VMEM(ext_shape, jnp.float32)],
        compiler_params=PARAMS,
        cost_estimate=cost(50 * size, 16 * size),
        name="last",
    )(coupling, speed, edge_rhs, edge_first, mid_own, mid_far, near0, left1, right1, diag, keep)

    hot = (face_index[:, :, None] == jnp.arange(cells * rows, dtype=jnp.int32)).astype(jnp.float32)
    grid_modes = jnp.einsum("mrf,mfl->mrl", mode_shapes, hot, precision=HI)
    held = grid_modes.reshape(modes * 2, cells, rows)
    blocks = [0]
    for d in [half_span] + inner[::-1]:
        held = jnp.concatenate([held, swap(held, "span", d)], axis=1)
        blocks = blocks + [b ^ d for b in blocks]
    weight = jnp.where(k_mine == 0, 1.0, 2.0).astype(jnp.float32)
    gains = jnp.einsum("mzx,krz->mkrx", held, table([0], blocks)[0], precision=HI) * weight[:, None, None]
    wall = flow[:, comps - 1, :, :, 0]
    total = jnp.sum(gains * wall[None], axis=(1, 2, 3)).reshape(modes, 2)
    for axis, count in (("span", span_count), ("stream", stream_count)):
        d = 1
        while d < count:
            total = total + swap(total, axis, d)
            d *= 2
    faces = face_index.shape[1] * stream_count * span_count
    return flow, total / math.sqrt(faces)


def solution(mesh):
    return jax.shard_map(
        shards,
        mesh=mesh,
        in_specs=(
            P(None, "span", "stream", None),
            P("span", None, None, "stream", None),
            P(),
            P(),
            P(),
            P(),
            P(None, ("stream", "span")),
            P(None, None, ("stream", "span")),
        ),
        out_specs=(P("span", None, None, "stream", None), P()),
        check_vma=False,
    )
```

profile of v0, /device:TPU:0, one launch (start us, length us, event | category | flops | bytes accessed | tf_op | source)
XLA Modules:
  0.0 201.5 jit_solution(13549653692776730077)
XLA Ops:
  0.6 1.4 fusion.55
  2.4 4.1 %collective-permute-start = (f32[5,32,16,128]{3,1,2,0:T(8,128)S(1)}, f32[5,32,16,128]{3,1,2,0:T(8,128)S(1)}, u32[]{:S(2)}, u32[]{:S(2)}) collective-permute-start(f32[5,32,16,128]{3,1,2,0:T(8,128)S(1)} %copy_dynamic-update-slice_fusion), channel_id=1, source_target_pairs={{0,4},{1,5},{2,6},{3,7},{4,0},{5,1},{6,2},{7,3},{8,12},{9,13},{10,... | collective-permute-start | bytes 3932168 | tf_op jit(solution)/shard_map/ppermute | solution.py:16
  6.5 1.5 copy.41
  7.9 1.6 collective-permute-start.5
  10.1 53.3 %collective-permute-done = f32[5,32,16,128]{3,1,2,0:T(8,128)S(1)} collective-permute-done((f32[5,32,16,128]{3,1,2,0:T(8,128)S(1)}, f32[5,32,16,128]{3,1,2,0:T(8,128)S(1)}, u32[]{:S(2)}, u32[]{:S(2)}) %collective-permute-start) | collective-permute-done | bytes 1310752 | tf_op jit(solution)/shard_map/ppermute | solution.py:16
  63.4 4.4 %fusion.5 = f32[4,16,2,5,16,128]{5,1,4,3,2,0:T(8,128)S(1)} fusion(f32[5,32,16,128]{3,1,2,0:T(8,128)S(1)} %collective-permute-done, f32[5,32,16,128]{3,1,2,0:T(8,128)S(1)} %copy_dynamic-update-slice_fusion, f32[4,16,1,64]{3,1,2,0:T(8,128)S(1)} %get-tuple-element.13, f32[4,16,1,64]{3,1,2,0:T(8,128)S(1)} %get-tuple-element.12), kind=kOutput, calls=%fused_computation.8 | convolution fusion | flops 1007304704 | bytes 7897088 | tf_op jit(solution)/shard_map/czxy,dkrz->dkcrxy/dot_general | solution.py:204
  67.8 1.6 copy.46
  69.7 2.1 %copy-done.3 = f32[4,16,2,5,16,128]{5,4,2,3,1,0:T(8,128)} copy-done((f32[4,16,2,5,16,128]{5,4,2,3,1,0:T(8,128)}, f32[4,16,2,5,16,128]{5,4,2,3,1,0:T(8,128)S(1)}, u32[]{:S(2)}) %copy-start.3) | copy-done | bytes 5242904
  71.8 1.8 pad_maximum_fusion
  73.5 3.7 %pad_maximum_fusion.1 = f32[5,64,16,128]{3,1,2,0:T(8,128)} fusion(f32[5,32,16,128]{3,1,2,0:T(8,128)} %collective-permute-done.5, f32[5,32,16,128]{3,1,2,0:T(8,128)} %copy.41), kind=kLoop, calls=%fused_computation.12 | loop fusion | flops 655360 | bytes 5242880 | tf_op jit(solution)/shard_map/concatenate | solution.py:170
  77.7 3.4 %collective-permute-start.3 = (f32[16,5,2,1,128]{4,3,2,1,0:T(1,128)S(1)}, f32[16,5,2,1,128]{4,3,2,1,0:T(1,128)S(1)}, u32[]{:S(2)}, u32[]{:S(2)}) collective-permute-start(f32[16,5,2,1,128]{4,3,2,1,0:T(1,128)S(1)} %get-tuple-element.7), channel_id=1, source_target_pairs={{0,8},{8,16},{16,24},{1,9},{9,17},{17,25},{2,10},{10,18},{18,26},{... | collective-permute-start | bytes 245768 | tf_op jit(solution)/shard_map/ppermute | solution.py:21
  81.2 1.5 collective-permute-start.4
  84.1 3.0 %slice_add_fusion = f32[1,16,5,2,16,128]{5,4,3,2,1,0:T(8,128)} fusion(f32[2,16,5,2,16,128]{5,4,3,2,1,0:T(8,128)} %collective-permute-done.1, f32[4,16,5,2,16,128]{5,4,3,2,1,0:T(8,128)} %bitcast.53), kind=kLoop, calls=%fused_computation.16 | loop fusion | flops 327680 | bytes 3932160 | tf_op jit(solution)/shard_map/add | solution.py:211
  87.2 4.3 %collective-permute-start.2 = (f32[1,16,5,2,16,128]{5,4,3,2,1,0:T(8,128)}, f32[1,16,5,2,16,128]{5,4,3,2,1,0:T(8,128)}, u32[]{:S(2)}, u32[]{:S(2)}) collective-permute-start(f32[1,16,5,2,16,128]{5,4,3,2,1,0:T(8,128)} %slice_add_fusion), channel_id=1, source_target_pairs={{0,2},{1,3},{2,0},{3,1},{4,6},{5,7},{6,4},{7,5},{8,10},{9,11},{10,... | collective-permute-start | bytes 3932168 | tf_op jit(solution)/shard_map/ppermute | solution.py:16
  92.2 4.7 %fusion = f32[2,16,2,5,16,128]{5,1,4,3,2,0:T(8,128)S(1)} fusion(f32[5,64,16,128]{3,1,2,0:T(8,128)} %collective-permute-done.6, f32[5,32,16,128]{3,1,2,0:T(8,128)} %collective-permute-done.5, f32[5,32,16,128]{3,1,2,0:T(8,128)} %copy.41, f32[2,16,1,128]{3,1,2,0:T(8,128)S(1)} %get-tuple-element.17, f32[2,16,1,128]{3,1,2,0:T(8,128)S(1)} %get-tuple-element.16), kind=kOutput, calls=%fused_computation.1 | convolution fusion | flops 1009270784 | bytes 7897088 | tf_op jit(solution)/shard_map/czxy,dkrz->dkcrxy/dot_general | solution.py:172
  99.7 49.2 %collective-permute-done.11 = f32[4,64,32]{1,2,0:T(8,128)S(1)} collective-permute-done((f32[4,64,32]{1,2,0:T(8,128)S(1)}, f32[4,64,32]{1,2,0:T(8,128)S(1)}, u32[]{:S(2)}, u32[]{:S(2)}) %collective-permute-start.11) | collective-permute-done | bytes 32800 | tf_op jit(solution)/shard_map/ppermute | solution.py:16
  149.1 6.2 %near.1 = f32[16,5,2,32,128]{4,3,2,1,0:T(8,128)S(1)} custom-call(f32[4,5,5]{2,1,0:T(8,128)S(1)} %copy.28.cpl, f32[16,5,2,32,128]{4,3,2,1,0:T(8,128)S(1)} %copy-done.2, f32[16,5,2,1,128]{4,3,2,1,0:T(1,128)S(1)} %collective-permute-done.3.left, f32[16,5,2,1,128]{4,3,2,1,0:T(1,128)S(1)} %collective-permute-done.4.right), custom_call_target="tpu_custom_call" | custom-call | flops 26214400 | bytes 5242880 | tf_op jit(solution)/shard_map/near/pallas_call | solution.py:188
  155.3 3.5 %fusion.9.rhs.edge_rhs = f32[16,5,2,16,128]{4,3,2,1,0:T(8,128)S(1)} fusion(f32[1,16,5,2,16,128]{5,4,3,2,1,0:T(8,128)} %collective-permute-done.2, f32[2,16,5,2,16,128]{5,4,3,2,1,0:T(8,128)} %collective-permute-done.1, f32[4,16,5,2,16,128]{5,4,3,2,1,0:T(8,128)} %bitcast.54), kind=kLoop, calls=%fused_computation.19 | loop fusion | flops 655360 | bytes 5242880 | tf_op jit(solution)/shard_map/add | solution.py:211
  158.8 1.3 edge.1.edge_first
  160.3 4.3 %collective-permute-start.8 = (f32[16,5,2,1,128]{4,3,2,1,0:T(1,128)S(1)}, f32[16,5,2,1,128]{4,3,2,1,0:T(1,128)S(1)}, u32[]{:S(2)}, u32[]{:S(2)}) collective-permute-start(f32[16,5,2,1,128]{4,3,2,1,0:T(1,128)S(1)} %get-tuple-element.11), channel_id=1, source_target_pairs={{0,8},{8,16},{16,24},{1,9},{9,17},{17,25},{2,10},{10,18},{18,26},{... | collective-permute-start | bytes 245768 | tf_op jit(solution)/shard_map/ppermute | solution.py:21
  164.5 1.3 collective-permute-start.9
  166.9 4.8 %collective-permute-done.9.right = f32[16,5,2,1,128]{4,3,2,1,0:T(1,128)S(1)} collective-permute-done((f32[16,5,2,1,128]{4,3,2,1,0:T(1,128)S(1)}, f32[16,5,2,1,128]{4,3,2,1,0:T(1,128)S(1)}, u32[]{:S(2)}, u32[]{:S(2)}) %collective-permute-start.9) | collective-permute-done | bytes 81952 | tf_op jit(solution)/shard_map/ppermute | solution.py:22
  171.6 9.0 %last.1 = f32[16,5,2,32,128]{4,3,2,1,0:T(8,128)} custom-call(f32[4,5,5]{2,1,0:T(8,128)S(1)} %copy.28.cpl, f32[16,5]{1,0:T(8,128)S(1)} %broadcast_multiply_fusion.speed, f32[16,5,2,16,128]{4,3,2,1,0:T(8,128)S(1)} %fusion.9.rhs.edge_rhs, f32[16,5,2,16,128]{4,3,2,1,0:T(8,128)S(1)} %edge.1.edge_first, f32[16,5,2,16,128]{4,3,2,1,0:T(8,128)S(1)} %get-tuple-element.5.mid_own, ...), custom_call_target="tpu_custom_call" | custom-call | flops 32768000 | bytes 10485760 | tf_op jit(solution)/shard_map/last/pallas_call | solution.py:227
  180.7 1.1 slice.74
  182.0 1.4 fusion.11
  183.5 1.1 collective-permute-done.13
  184.7 2.5 %collective-permute-start.14 = (f32[2,2]{1,0:T(2,128)S(1)}, f32[2,2]{1,0:T(2,128)S(1)}, u32[]{:S(2)}, u32[]{:S(2)}) collective-permute-start(f32[2,2]{1,0:T(2,128)S(1)} %add.235), channel_id=1, source_target_pairs={{0,2},{1,3},{2,0},{3,1},{4,6},{5,7},{6,4},{7,5},{8,10},{9,11},{10,... | collective-permute-start | bytes 56 | tf_op jit(solution)/shard_map/ppermute | solution.py:16
  187.2 1.5 collective-permute-done.14
  189.5 3.7 %collective-permute-done.15 = f32[2,2]{1,0:T(2,128)S(1)} collective-permute-done((f32[2,2]{1,0:T(2,128)S(1)}, f32[2,2]{1,0:T(2,128)S(1)}, u32[]{:S(2)}, u32[]{:S(2)}) %collective-permute-start.15) | collective-permute-done | bytes 48 | tf_op jit(solution)/shard_map/ppermute | solution.py:16
  193.2 2.6 %collective-permute-start.16 = (f32[2,2]{1,0:T(2,128)S(1)}, f32[2,2]{1,0:T(2,128)S(1)}, u32[]{:S(2)}, u32[]{:S(2)}) collective-permute-start(f32[2,2]{1,0:T(2,128)S(1)} %add.237), channel_id=1, source_target_pairs={{0,8},{8,0},{16,24},{24,16},{1,9},{9,1},{17,25},{25,17},{2,10},{10... | collective-permute-start | bytes 56 | tf_op jit(solution)/shard_map/ppermute | solution.py:16
  195.8 1.5 collective-permute-done.16
  197.6 3.3 %collective-permute-done.17 = f32[2,2]{1,0:T(2,128)S(1)} collective-permute-done((f32[2,2]{1,0:T(2,128)S(1)}, f32[2,2]{1,0:T(2,128)S(1)}, u32[]{:S(2)}, u32[]{:S(2)}) %collective-permute-start.17) | collective-permute-done | bytes 48 | tf_op jit(solution)/shard_map/ppermute | solution.py:16
  (79 shorter events, 9.7 us)
Async XLA Ops:
  0.6 97.8 %copy-start = (f32[5,128,128]{2,1,0:T(8,128)S(1)}, f32[5,128,128]{2,1,0:T(8,128)}, u32[]{:S(2)}) copy-start(f32[5,128,128]{2,1,0:T(8,128)} %param.10) | copy-start | bytes 983044
  2.3 4.1 %slice-start = ((f32[5,32,32,128]{3,2,1,0:T(8,128)}), f32[5,32,16,128]{3,2,1,0:T(8,128)S(1)}, s32[]{:S(2)}) async-start(f32[5,32,32,128]{3,2,1,0:T(8,128)} %param.8), calls=%async_computation | async-start | bytes 2621440 | tf_op jit(solution)/shard_map/slice | solution.py:166
  2.4 61.1 %collective-permute-start = (f32[5,32,16,128]{3,1,2,0:T(8,128)S(1)}, f32[5,32,16,128]{3,1,2,0:T(8,128)S(1)}, u32[]{:S(2)}, u32[]{:S(2)}) collective-permute-start(f32[5,32,16,128]{3,1,2,0:T(8,128)S(1)} %copy_dynamic-update-slice_fusion), channel_id=1, source_target_pairs={{0,4},{1,5},{2,6},{3,7},{4,0},{5,1},{6,2},{7,3},{8,12},{9,13},{10,... | collective-permute-start | bytes 3932168 | tf_op jit(solution)/shard_map/ppermute | solution.py:16
  7.9 65.6 %collective-permute-start.5 = (f32[5,32,16,128]{3,1,2,0:T(8,128)}, f32[5,32,16,128]{3,1,2,0:T(8,128)}, u32[]{:S(2)}, u32[]{:S(2)}) collective-permute-start(f32[5,32,16,128]{3,1,2,0:T(8,128)} %copy.41), channel_id=1, source_target_pairs={{0,2},{1,3},{2,0},{3,1},{4,6},{5,7},{6,4},{7,5},{8,10},{9,11},{10,... | collective-permute-start | bytes 3932168 | tf_op jit(solution)/shard_map/ppermute | solution.py:16
  69.4 2.3 %copy-start.3 = (f32[4,16,2,5,16,128]{5,4,2,3,1,0:T(8,128)}, f32[4,16,2,5,16,128]{5,4,2,3,1,0:T(8,128)S(1)}, u32[]{:S(2)}) copy-start(f32[4,16,2,5,16,128]{5,4,2,3,1,0:T(8,128)S(1)} %copy.46) | copy-start | bytes 15728644
  73.5 4.1 %copy-start.2 = (f32[16,5,2,32,128]{4,3,2,1,0:T(8,128)S(1)}, f32[16,5,2,32,128]{4,3,2,1,0:T(8,128)}, u32[]{:S(2)}) copy-start(f32[16,5,2,32,128]{4,3,2,1,0:T(8,128)} %state.1) | copy-start | bytes 7864324
  73.5 9.2 %copy-start.7 = (f32[2,2,128]{2,1,0:T(2,128)S(1)}, f32[2,2,128]{2,1,0:T(2,128)}, u32[]{:S(2)}) copy-start(f32[2,2,128]{2,1,0:T(2,128)} %param.15) | copy-start | bytes 6148
  73.5 9.2 %copy-start.8 = (s32[2,128]{1,0:T(2,128)S(1)}, s32[2,128]{1,0:T(2,128)}, u32[]{:S(2)}) copy-start(s32[2,128]{1,0:T(2,128)} %param.14) | copy-start | bytes 3076
  73.5 10.6 %collective-permute-start.1 = (f32[2,16,5,2,16,128]{5,4,3,2,1,0:T(8,128)}, f32[2,16,5,2,16,128]{5,4,3,2,1,0:T(8,128)}, u32[]{:S(2)}, u32[]{:S(2)}) collective-permute-start(f32[2,16,5,2,16,128]{5,4,3,2,1,0:T(8,128)} %pad_maximum_fusion), channel_id=1, source_target_pairs={{0,1},{1,0},{2,3},{3,2},{4,5},{5,4},{6,7},{7,6},{8,9},{9,8},{10,11... | collective-permute-start | bytes 7864328 | tf_op jit(solution)/shard_map/ppermute | solution.py:16
  77.3 14.9 %collective-permute-start.6 = (f32[5,64,16,128]{3,1,2,0:T(8,128)}, f32[5,64,16,128]{3,1,2,0:T(8,128)}, u32[]{:S(2)}, u32[]{:S(2)}) collective-permute-start(f32[5,64,16,128]{3,1,2,0:T(8,128)} %pad_maximum_fusion.1), channel_id=1, source_target_pairs={{0,1},{1,0},{2,3},{3,2},{4,5},{5,4},{6,7},{7,6},{8,9},{9,8},{10,11... | collective-permute-start | bytes 7864328 | tf_op jit(solution)/shard_map/ppermute | solution.py:16
  77.7 71.3 %collective-permute-start.3 = (f32[16,5,2,1,128]{4,3,2,1,0:T(1,128)S(1)}, f32[16,5,2,1,128]{4,3,2,1,0:T(1,128)S(1)}, u32[]{:S(2)}, u32[]{:S(2)}) collective-permute-start(f32[16,5,2,1,128]{4,3,2,1,0:T(1,128)S(1)} %get-tuple-element.7), channel_id=1, source_target_pairs={{0,8},{8,16},{16,24},{1,9},{9,17},{17,25},{2,10},{10,18},{18,26},{... | collective-permute-start | bytes 245768 | tf_op jit(solution)/shard_map/ppermute | solution.py:21
  81.2 67.8 %collective-permute-start.4 = (f32[16,5,2,1,128]{4,3,2,1,0:T(1,128)S(1)}, f32[16,5,2,1,128]{4,3,2,1,0:T(1,128)S(1)}, u32[]{:S(2)}, u32[]{:S(2)}) collective-permute-start(f32[16,5,2,1,128]{4,3,2,1,0:T(1,128)S(1)} %get-tuple-element.6), channel_id=1, source_target_pairs={{8,0},{16,8},{24,16},{9,1},{17,9},{25,17},{10,2},{18,10},{26,18},{... | collective-permute-start | bytes 245768 | tf_op jit(solution)/shard_map/ppermute | solution.py:22
  83.4 15.1 %collective-permute-start.10 = (f32[4,32,32]{1,2,0:T(8,128)S(1)}, f32[4,32,32]{1,2,0:T(8,128)S(1)}, u32[]{:S(2)}, u32[]{:S(2)}) collective-permute-start(f32[4,32,32]{1,2,0:T(8,128)S(1)} %copy.32), channel_id=1, source_target_pairs={{0,4},{1,5},{2,6},{3,7},{4,0},{5,1},{6,2},{7,3},{8,12},{9,13},{10,... | collective-permute-start | bytes 49160 | tf_op jit(solution)/shard_map/ppermute | solution.py:16
  87.2 68.1 %collective-permute-start.2 = (f32[1,16,5,2,16,128]{5,4,3,2,1,0:T(8,128)}, f32[1,16,5,2,16,128]{5,4,3,2,1,0:T(8,128)}, u32[]{:S(2)}, u32[]{:S(2)}) collective-permute-start(f32[1,16,5,2,16,128]{5,4,3,2,1,0:T(8,128)} %slice_add_fusion), channel_id=1, source_target_pairs={{0,2},{1,3},{2,0},{3,1},{4,6},{5,7},{6,4},{7,5},{8,10},{9,11},{10,... | collective-permute-start | bytes 3932168 | tf_op jit(solution)/shard_map/ppermute | solution.py:16
  97.7 0.7 copy-start.6
  97.7 2.0 copy-start.5
  98.0 67.9 %collective-permute-start.7 = (f32[16,5,2,16,128]{4,3,2,1,0:T(8,128)S(1)}, f32[16,5,2,16,128]{4,3,2,1,0:T(8,128)S(1)}, u32[]{:S(2)}, u32[]{:S(2)}) collective-permute-start(f32[16,5,2,16,128]{4,3,2,1,0:T(8,128)S(1)} %get-tuple-element.4), channel_id=1, source_target_pairs={{0,4},{1,5},{2,6},{3,7},{4,0},{5,1},{6,2},{7,3},{8,12},{9,13},{10,... | collective-permute-start | bytes 3932168 | tf_op jit(solution)/shard_map/ppermute | solution.py:16
  98.5 50.3 %collective-permute-start.11 = (f32[4,64,32]{1,2,0:T(8,128)S(1)}, f32[4,64,32]{1,2,0:T(8,128)S(1)}, u32[]{:S(2)}, u32[]{:S(2)}) collective-permute-start(f32[4,64,32]{1,2,0:T(8,128)S(1)} %pad_maximum_fusion.2), channel_id=1, source_target_pairs={{0,2},{1,3},{2,0},{3,1},{4,6},{5,7},{6,4},{7,5},{8,10},{9,11},{10,... | collective-permute-start | bytes 98312 | tf_op jit(solution)/shard_map/ppermute | solution.py:16
  148.9 33.1 %collective-permute-start.12 = (f32[4,128,32]{1,2,0:T(8,128)S(1)}, f32[4,128,32]{1,2,0:T(8,128)}, u32[]{:S(2)}, u32[]{:S(2)}) collective-permute-start(f32[4,128,32]{1,2,0:T(8,128)S(1)} %pad_maximum_fusion.3), channel_id=1, source_target_pairs={{0,1},{1,0},{2,3},{3,2},{4,5},{5,4},{6,7},{7,6},{8,9},{9,8},{10,11... | collective-permute-start | bytes 196616 | tf_op jit(solution)/shard_map/ppermute | solution.py:16
  155.3 3.5 %copy-start.1 = (f32[16,5,2,32,128]{4,3,2,1,0:T(8,128)}, f32[16,5,2,32,128]{4,3,2,1,0:T(8,128)S(1)}, u32[]{:S(2)}) copy-start(f32[16,5,2,32,128]{4,3,2,1,0:T(8,128)S(1)} %near.1) | copy-start | bytes 7864324
  160.3 6.6 %collective-permute-start.8 = (f32[16,5,2,1,128]{4,3,2,1,0:T(1,128)S(1)}, f32[16,5,2,1,128]{4,3,2,1,0:T(1,128)S(1)}, u32[]{:S(2)}, u32[]{:S(2)}) collective-permute-start(f32[16,5,2,1,128]{4,3,2,1,0:T(1,128)S(1)} %get-tuple-element.11), channel_id=1, source_target_pairs={{0,8},{8,16},{16,24},{1,9},{9,17},{17,25},{2,10},{10,18},{18,26},{... | collective-permute-start | bytes 245768 | tf_op jit(solution)/shard_map/ppermute | solution.py:21
  164.5 7.1 %collective-permute-start.9 = (f32[16,5,2,1,128]{4,3,2,1,0:T(1,128)S(1)}, f32[16,5,2,1,128]{4,3,2,1,0:T(1,128)S(1)}, u32[]{:S(2)}, u32[]{:S(2)}) collective-permute-start(f32[16,5,2,1,128]{4,3,2,1,0:T(1,128)S(1)} %get-tuple-element.10), channel_id=1, source_target_pairs={{8,0},{16,8},{24,16},{9,1},{17,9},{25,17},{10,2},{18,10},{26,18},{... | collective-permute-start | bytes 245768 | tf_op jit(solution)/shard_map/ppermute | solution.py:22
  180.7 1.4 copy-start.4
  183.5 1.1 collective-permute-start.13
  184.7 4.0 %collective-permute-start.14 = (f32[2,2]{1,0:T(2,128)S(1)}, f32[2,2]{1,0:T(2,128)S(1)}, u32[]{:S(2)}, u32[]{:S(2)}) collective-permute-start(f32[2,2]{1,0:T(2,128)S(1)} %add.235), channel_id=1, source_target_pairs={{0,2},{1,3},{2,0},{3,1},{4,6},{5,7},{6,4},{7,5},{8,10},{9,11},{10,... | collective-permute-start | bytes 56 | tf_op jit(solution)/shard_map/ppermute | solution.py:16
  188.7 4.5 %collective-permute-start.15 = (f32[2,2]{1,0:T(2,128)S(1)}, f32[2,2]{1,0:T(2,128)S(1)}, u32[]{:S(2)}, u32[]{:S(2)}) collective-permute-start(f32[2,2]{1,0:T(2,128)S(1)} %add.236), channel_id=1, source_target_pairs={{0,4},{1,5},{2,6},{3,7},{4,0},{5,1},{6,2},{7,3},{8,12},{9,13},{10,... | collective-permute-start | bytes 56 | tf_op jit(solution)/shard_map/ppermute | solution.py:16
  193.2 4.2 %collective-permute-start.16 = (f32[2,2]{1,0:T(2,128)S(1)}, f32[2,2]{1,0:T(2,128)S(1)}, u32[]{:S(2)}, u32[]{:S(2)}) collective-permute-start(f32[2,2]{1,0:T(2,128)S(1)} %add.237), channel_id=1, source_target_pairs={{0,8},{8,0},{16,24},{24,16},{1,9},{9,1},{17,25},{25,17},{2,10},{10... | collective-permute-start | bytes 56 | tf_op jit(solution)/shard_map/ppermute | solution.py:16
  197.4 3.6 %collective-permute-start.17 = (f32[2,2]{1,0:T(2,128)S(1)}, f32[2,2]{1,0:T(2,128)S(1)}, u32[]{:S(2)}, u32[]{:S(2)}) collective-permute-start(f32[2,2]{1,0:T(2,128)S(1)} %add.238), channel_id=1, source_target_pairs={{0,16},{8,24},{16,0},{24,8},{1,17},{9,25},{17,1},{25,9},{2,18},{10... | collective-permute-start | bytes 56 | tf_op jit(solution)/shard_map/ppermute | solution.py:16
where the time goes:
time: 202 us
  waiting for transfers between devices  119 us (59%)
  starting transfers between devices  27.6 us (14%)
  Pallas kernels  16.6 us (8%)
  other arithmetic  15.2 us (8%)
  matrix products  11 us (5%)
  local copies, waits for them, and re-layouts  10.6 us (5%)
    ppermute x14, waiting for transfers between devices, swap(): return lax.ppermute(value, axis, [(i, i ^ dist) for i in range(count)])  114 us
    ppermute x14, starting transfers between devices, swap(): return lax.ppermute(value, axis, [(i, i ^ dist) for i in range(count)])  17.1 us
    pallas_call x1, Pallas kernels, shards(): pl.pallas_call(functools.partial(last_kernel, 0), grid=grid, in_specs=[SM...  9.04 us
    ppermute x2, starting transfers between devices, halo(): left = lax.ppermute(tail, axis, [(i, i + 1) for i in range(ends)])  7.72 us
    add x2, other arithmetic, shards(): part = jnp.stack([part[i] + got[n] for n, i in enumerate(mine)])  6.54 us
    pallas_call x1, Pallas kernels, shards(): pl.pallas_call(near_kernel, grid=grid, in_specs=[SMEM, by_wave(state_shap...  6.23 us
    ppermute x2, waiting for transfers between devices, halo(): right = lax.ppermute(head, axis, [(i + 1, i) for i in range(ends)])  4.78 us
    dot_general x1, matrix products, shards(): jnp.einsum('czxy,dkrz->dkcrxy', held, table([half_span, 0], blocks), prec...  4.69 us
  transfers between devices with their start and end apart: 18, of which 9 were waited for; matrix products, arithmetic and copies ran while one was open for 15% of the time, Pallas kernels for 8%

commit v1 on v0

v1 whole, which is shorter than its diff:
```python
import functools
import math

import jax
import jax.numpy as jnp
from jax import lax
from jax.experimental import pallas as pl
from jax.experimental.pallas import tpu as pltpu
from jax.sharding import PartitionSpec as P

HI = lax.Precision.HIGHEST


def swap(value, axis, dist):
    count = lax.axis_size(axis)
    return lax.ppermute(value, axis, [(i, i ^ dist) for i in range(count)])


def halo(head, tail, axis):
    ends = lax.axis_size(axis) - 1
    left = lax.ppermute(tail, axis, [(i, i + 1) for i in range(ends)])
    right = lax.ppermute(head, axis, [(i + 1, i) for i in range(ends)])
    return left, right


def gate(value, *after):
    return pl.pallas_call(
        lambda *refs: None,
        in_specs=[pl.BlockSpec(memory_space=pl.ANY)] * (1 + len(after)),
        out_specs=pl.BlockSpec(memory_space=pl.ANY),
        out_shape=jax.ShapeDtypeStruct(value.shape, value.dtype),
        input_output_aliases={0: 0},
        cost_estimate=FREE,
        name="gate",
    )(value, *after)


def split_kernel(start, end, faces, outer, between):
    @pl.when(pl.program_id(0) < pl.num_programs(0) - 1)
    def _():
        outer[:, :4, :] = start[0, :, :4, :]
        outer[:, 4:, :] = end[0, :, 4:, :]
        between[0, :, :4, :] = end[0, :, :4, :]
        between[0, :, 4:, :] = start[0, :, 4:, :]

    @pl.when(pl.program_id(0) == pl.num_programs(0) - 1)
    def _():
        outer[0] = faces[...]


def split(source, faces):
    comps, cells, rows, normal = source.shape
    last = comps - 1

    def spec(tile):
        return pl.BlockSpec((1, cells, 8, normal), lambda c: (jnp.minimum(c, last), 0, tile, 0))

    return pl.pallas_call(
        split_kernel,
        grid=(comps + 1,),
        in_specs=[spec(0), spec(rows // 8 - 1), pl.BlockSpec(faces.shape, lambda c: (0, 0))],
        out_specs=[pl.BlockSpec((cells, 8, normal), lambda c: (c, 0, 0)), spec(0)],
        out_shape=[
            jax.ShapeDtypeStruct((comps * cells + 1, 8, normal), jnp.float32),
            jax.ShapeDtypeStruct((comps, cells, 8, normal), jnp.float32),
        ],
        compiler_params=PARAMS,
        cost_estimate=FREE,
        name="split",
    )(source, source, faces)


def wave_rows(owners, blocks, me, waves, cells, span_total):
    k = (jnp.stack([me ^ d for d in owners])[:, None] * waves + jnp.arange(waves, dtype=jnp.int32)).reshape(-1)
    z = jnp.concatenate([(me ^ d) * cells + start + jnp.arange(size, dtype=jnp.int32) for d, start, size in blocks])
    index = (k[:, None] * z[None, :]) % span_total
    phase = index.astype(jnp.float32) * (2.0 * math.pi / span_total)
    tab = jnp.stack([jnp.cos(phase), -jnp.sin(phase)], axis=1) * (1.0 / math.sqrt(span_total))
    return tab.reshape(len(owners) * waves * 2, z.shape[0])


def halves(value):
    high = value.astype(jnp.bfloat16)
    return high, (value - high.astype(jnp.float32)).astype(jnp.bfloat16)


def table_halves(value):
    high = lax.reduce_precision(value, 8, 7)
    return high.astype(jnp.bfloat16), (value - high).astype(jnp.bfloat16)


def transform_kernel(count, outs_at, sizes, rows, comps, *refs):
    high, low = refs[0], refs[1]
    raws, outs = refs[2 : 2 + count], refs[outs_at:]
    normal = raws[0].shape[-1]
    wide = 2

    @pl.when(pl.program_id(0) < comps)
    def _():
        for x in range(0, rows, wide):
            cols = []
            for j in range(wide):
                cols.append(jnp.concatenate([r[pl.ds(x + j, n, stride=rows), :] for r, n in zip(raws, sizes)], axis=0))
            data = jnp.concatenate(cols, axis=1)
            dh, dl = halves(data)
            dot = functools.partial(jnp.dot, preferred_element_type=jnp.float32)
            val = dot(high[...], dh) + (dot(low[...], dh) + dot(high[...], dl))
            at = 0
            for out in outs:
                lines = out.shape[0] // rows
                for j in range(wide):
                    out[pl.ds(x + j, lines, stride=rows), :] = val[at : at + lines, j * normal : (j + 1) * normal]
                at += lines

    @pl.when(pl.program_id(0) == comps)
    def _():
        for n, raw in enumerate(raws):
            outs[-1][8 * n : 8 * n + 8, :] = raw[:8, :]


def transform(table, raws, lines, after, name, comps, tail=False):
    rows, normal = raws[0].shape[-2:]
    flat = [raw.reshape(-1, normal) for raw in raws]
    sizes = [f.shape[0] // (comps * rows) for f in flat]
    high, low = table_halves(table)
    counts = [comps * n * rows for n in lines]
    if tail:
        counts[-1] += 8 * len(raws)
    first_outs = [pl.BlockSpec((n * rows, normal), lambda c: (jnp.minimum(c, comps - 1), 0)) for n in lines[:-1]]
    outs = pl.pallas_call(
        functools.partial(transform_kernel, len(raws), 2 + len(raws) + len(after), sizes, rows, comps),
        grid=(comps + tail,),
        in_specs=[pl.BlockSpec(table.shape, lambda c: (0, 0))] * 2
        + [pl.BlockSpec((n * rows, normal), lambda c: (c, 0)) for n in sizes]
        + [ANY] * len(after),
        out_specs=first_outs + [pl.BlockSpec((lines[-1] * rows, normal), lambda c: (c, 0))],
        out_shape=[jax.ShapeDtypeStruct((n, normal), jnp.float32) for n in counts],
        compiler_params=PARAMS,
        cost_estimate=FREE,
        name=name,
    )(high, low, *flat, *after)
    return [o if tail and o is outs[-1] else o.reshape(comps, n, rows, normal) for o, n in zip(outs, lines)]


def near_terms(ext, cpl, r, row, comps, normal, wanted):
    lane = lax.broadcasted_iota(jnp.int32, (8, normal), 1)
    parts = []
    for c in range(comps):
        mid = ext[c, r, pl.ds(row, 8), :]
        up = jnp.where(lane < normal - 1, pltpu.roll(mid, normal - 1, 1), 0.0)
        down = jnp.where(lane > 0, pltpu.roll(mid, 1, 1), 0.0)
        parts.append((ext[c, r, pl.ds(row + 1, 8), :], ext[c, r, pl.ds(row - 1, 8), :], up, down))
    out = []
    for c in wanted:
        acc = None
        for e in range(comps):
            for d in range(4):
                term = cpl[d, c, e] * parts[e][d]
                acc = term if acc is None else acc + term
        out.append(acc)
    return out


def near_kernel(cpl, state, left, right, after, near, ext):
    waves, comps, _, rows, normal = state.shape

    def one(k, carry):
        ext[:, :, 8 : 8 + rows, :] = state[k]
        ext[:, :, 7:8, :] = left[k]
        ext[:, :, 8 + rows : 9 + rows, :] = right[k]
        for r in range(2):
            for t in range(rows // 8):
                sums = near_terms(ext, cpl, r, 8 + 8 * t, comps, normal, range(comps))
                for c in range(comps):
                    near[k, c, r, 8 * t : 8 * t + 8, :] = sums[c]
        return carry

    lax.fori_loop(0, waves, one, 0)


def rotate(re, im, a, b, keep):
    scale = keep / (a * a + b * b)
    return (a * re + b * im) * scale, (a * im - b * re) * scale


def edge_kernel(speed, own, far, near_start, near_end, diag, keep, after, first):
    waves, comps, _, _, normal = near_start.shape
    rows = keep.shape[0]
    base = pl.program_id(0) * waves
    low = lax.broadcasted_iota(jnp.int32, (8, normal), 0) < 4

    def one(k, carry):
        for c in range(comps):
            defect = []
            for r in range(2):
                old = jnp.where(low, near_start[k, c, r], near_end[k, c, r])
                defect.append(own[c, 2 * k + r] + far[c, 2 * k + r] - old)
            a = jnp.where(low, diag[c, :8, :], diag[c, rows - 8 :, :])
            out = rotate(*defect, a, speed[base + k, c], jnp.where(low, keep[:8, :], keep[rows - 8 :, :]))
            first[k, c, 0], first[k, c, 1] = out
        return carry

    lax.fori_loop(0, waves, one, 0)


def tile_sums(owns, fars, low, rows, c, at):
    outer, between, *middle = [own[c, at] + far[c, at] for own, far in zip(owns, fars)]
    return [jnp.where(low, outer, between)] + middle + [jnp.where(low, between, outer)]


def last_kernel(pieces, cpl, speed, left, right, diag, keep, near, *rest):
    owns, fars = rest[:pieces], rest[pieces : 2 * pieces]
    flow, ext = rest[2 * pieces :]
    waves, comps, _, rows, normal = flow.shape
    base = pl.program_id(0) * waves
    low = lax.broadcasted_iota(jnp.int32, (8, normal), 0) < 4

    def one(k, carry):
        ext[:, :, 7:8, :] = left[k]
        ext[:, :, 8 + rows : 9 + rows, :] = right[k]
        for c in range(comps):
            b = speed[base + k, c]
            rhs = [tile_sums(owns, fars, low, rows, c, 2 * k + r) for r in range(2)]
            for n in range(rows // 8):
                src = slice(8 * n, 8 * n + 8)
                re, im = (rhs[r][n] - near[k, c, r, src, :] for r in range(2))
                re, im = rotate(re, im, diag[c, src, :], b, keep[src, :])
                ext[c, 0, 8 + 8 * n : 16 + 8 * n, :], ext[c, 1, 8 + 8 * n : 16 + 8 * n, :] = re, im
                flow[k, c, 0, src, :], flow[k, c, 1, src, :] = rhs[0][n], rhs[1][n]
        for n in range(rows // 8):
            src = slice(8 * n, 8 * n + 8)
            sums = [near_terms(ext, cpl, r, 8 + 8 * n, comps, normal, range(comps)) for r in range(2)]
            for c in range(comps):
                re, im = (flow[k, c, r, src, :] - sums[r][c] for r in range(2))
                out = rotate(re, im, diag[c, src, :], speed[base + k, c], keep[src, :])
                flow[k, c, 0, src, :], flow[k, c, 1, src, :] = out
        return carry

    lax.fori_loop(0, waves, one, 0)


def by_wave(shape, step, skip=0):
    rest = len(shape) - 1
    return pl.BlockSpec((step,) + tuple(shape[1:]), lambda i: (i + skip,) + (0,) * rest)


def by_wave2(shape, step, skip=0):
    return pl.BlockSpec((shape[0], 2 * step) + tuple(shape[2:]), lambda i: (0, i + skip, 0, 0))


def whole(shape):
    return pl.BlockSpec(tuple(shape), lambda i: (0,) * len(shape))


SMEM = pl.BlockSpec(memory_space=pltpu.SMEM)
ANY = pl.BlockSpec(memory_space=pl.ANY)
LARGE = pltpu.CompilerParams(vmem_limit_bytes=60 * 1024 * 1024)
PARAMS = pltpu.CompilerParams(vmem_limit_bytes=48 * 1024 * 1024)


BUSY = pl.CostEstimate(flops=0, bytes_accessed=60_000_000, transcendentals=0)
FREE = pl.CostEstimate(flops=0, bytes_accessed=0, transcendentals=0)


def shards(forcing, initial_state, diagonal, span_speed, coupling, stiffener_mask, face_index, mode_shapes):
    span_count = lax.axis_size("span")
    stream_count = lax.axis_size("stream")
    me = lax.axis_index("span")
    comps, cells, rows, normal = forcing.shape
    waves = initial_state.shape[0]
    span_total = cells * span_count
    half_span = span_count // 2
    modes = face_index.shape[0]
    inner = [d for d in (1 << i for i in range(20)) if d < half_span]

    k_mine = me * waves + jnp.arange(waves, dtype=jnp.int32)
    first_cell = lax.axis_index("stream") * rows
    keep = lax.dynamic_slice_in_dim((1 - stiffener_mask).astype(jnp.float32), first_cell, rows, 0)
    diag = lax.dynamic_slice_in_dim(diagonal, first_cell, rows, 1)
    speed = (k_mine.astype(jnp.float32) * (2.0 * math.pi / span_total))[:, None] * span_speed[None, :]
    left0, right0 = halo(initial_state[:, :, :, :1], initial_state[:, :, :, rows - 1 :], "stream")
    step = 2
    grid = (waves // step,)
    state_shape = initial_state.shape
    side_shape = left0.shape
    ext_shape = (comps, 2, rows + 16, normal)
    top, quarter = half_span, half_span // 2
    lower = [d for d in reversed(inner) if d < quarter]
    middle = [forcing[:, :, at : at + 8] for at in range(8, rows - 8, 8)]
    faces = [face_index.astype(jnp.float32), mode_shapes.reshape(2 * modes, -1)]
    faces = jnp.concatenate(faces + [jnp.zeros((8 - 3 * modes, face_index.shape[1]), jnp.float32)], axis=0)
    outer, between = split(forcing, faces)

    def gather(raw, got, hold, first, last):
        late = gate(got, *hold) if hold else got
        sets = [(raw, 0, 0), (late, first, 0)]
        for d in lower:
            more = []
            for value, block, start in sets:
                cuts = 4 if block & first and value.shape[1] == cells and value.ndim == 4 else 1
                size = value.shape[1] // cuts if value.ndim == 4 else cells
                for n in range(cuts):
                    part = value[:, n * size : (n + 1) * size] if cuts > 1 else value
                    more.append((swap(part, "span", d), block ^ d, start + n * size))
            sets = sets + more
        blocks = [(block, start, value.shape[1] if value.ndim == 4 else cells) for value, block, start in sets]
        return [value for value, _, _ in sets], wave_rows([0, last], blocks, me, waves, cells, span_total), [b for b, _, _ in blocks]

    e_got = swap(outer, "span", quarter)
    far_raw = swap(forcing[:, :, 8 : rows - 8], "span", top)
    raws, tab, face_blocks = gather(outer, e_got, [], quarter, top)
    lines = 2 * waves
    e_own, e_out = transform(tab, raws, (lines, lines), [keep, diag, speed], "gathered", comps, True)
    f_got = swap(gate(between, e_got), "span", quarter)
    f_got = swap(gate(between, e_got), "span", quarter)
    e_far = swap(e_out, "span", top)
    cut = comps * lines * 8
    face_sets = jnp.concatenate([e_out[cut:], e_far[cut:]]).reshape(span_count, 8, -1)
    face_blocks = face_blocks + [b ^ top for b in face_blocks]
    e_far = e_far[:cut].reshape(e_own.shape)

    def cross(n, hold):
        raws, tab, _ = gather(middle[n], far_raw[:, :, 8 * n : 8 * n + 8], hold[:1], top, quarter)
        own, out = transform(tab, raws, (lines, lines), hold, "crossing", comps)
        return own, out, swap(out, "span", quarter)

    raws, tab, _ = gather(between, f_got, [e_out], quarter, top)
    f_own, f_out = transform(tab, raws, (lines, lines), [], "gathered", comps)
    f_far = swap(f_out, "span", top)
    c_own, c_out, c_far = cross(0, [f_out])
    d_own, d_out, d_far = cross(1, [c_out])
    near0 = pl.pallas_call(
        near_kernel,
        grid=grid,
        in_specs=[SMEM, by_wave(state_shape, step), by_wave(side_shape, step), by_wave(side_shape, step), ANY],
        out_specs=by_wave(state_shape, step),
        out_shape=jax.ShapeDtypeStruct(state_shape, jnp.float32),
        scratch_shapes=[pltpu.VMEM(ext_shape, jnp.float32)],
        compiler_params=PARAMS,
        cost_estimate=FREE,
        name="near",
    )(coupling, initial_state, left0, right0, d_out)
    owns, fars = [e_own, f_own, c_own, d_own], [e_far, f_far, c_far, d_far]
    pieces = len(owns)

    first_shape = (waves, comps, 2, 8, normal)
    ends = pl.pallas_call(
        edge_kernel,
        grid=(2,),
        in_specs=[SMEM]
        + [by_wave2(e_own.shape, waves // 2)] * 2
        + [pl.BlockSpec((waves // 2,) + first_shape[1:], lambda i, n=n: (i, 0, 0, n, 0)) for n in (0, rows // 8 - 1)]
        + [whole(diag.shape), whole(keep.shape), ANY],
        out_specs=by_wave(first_shape, waves // 2),
        out_shape=jax.ShapeDtypeStruct(first_shape, jnp.float32),
        compiler_params=LARGE,
        cost_estimate=FREE,
        name="edge",
    )(speed, e_own, e_far, near0, near0, diag, keep, c_far)
    left1, right1 = halo(ends[:, :, :, :1], ends[:, :, :, 7:], "stream")

    hot = (face_sets[:, :modes, :, None] == jnp.arange(cells * rows, dtype=jnp.float32)).astype(jnp.float32)
    shapes = face_sets[:, modes : 3 * modes].reshape(span_count, modes, 2, -1)
    held = jnp.einsum("bmrf,bmfl->mrbl", shapes, hot, precision=HI).reshape(2 * modes, span_total, rows)
    tab = wave_rows([0], [(b, 0, cells) for b in face_blocks], me, waves, cells, span_total)
    weight = jnp.where(k_mine == 0, 1.0, 2.0).astype(jnp.float32)
    gains = jnp.einsum("mzx,kz->mkx", held, tab, precision=HI).reshape(2 * modes, waves, 2, rows)
    gains = gains * weight[:, None, None]

    flow = pl.pallas_call(
        functools.partial(last_kernel, pieces),
        grid=grid,
        in_specs=[SMEM, SMEM]
        + [by_wave(side_shape, step)] * 2
        + [whole(diag.shape), whole(keep.shape), by_wave(state_shape, step)]
        + [by_wave2(e_own.shape, step)] * (2 * pieces),
        out_specs=by_wave(state_shape, step),
        out_shape=jax.ShapeDtypeStruct(state_shape, jnp.float32),
        scratch_shapes=[pltpu.VMEM(ext_shape, jnp.float32)],
        compiler_params=LARGE,
        cost_estimate=FREE,
        name="last",
    )(coupling, speed, left1, right1, diag, keep, near0, *owns, *fars)

    wall = flow[:, comps - 1, :, :, 0]
    total = jnp.sum(gains * wall[None], axis=(1, 2, 3)).reshape(modes, 2)
    for axis, count in (("span", span_count), ("stream", stream_count)):
        d = 1
        while d < count:
            total = total + swap(total, axis, d)
            d *= 2
    faces = face_index.shape[1] * stream_count * span_count
    return flow, total / math.sqrt(faces)


def solution(mesh):
    return jax.shard_map(
        shards,
        mesh=mesh,
        in_specs=(
            P(None, "span", "stream", None),
            P("span", None, None, "stream", None),
            P(),
            P(),
            P(),
            P(),
            P(None, ("stream", "span")),
            P(None, None, ("stream", "span")),
        ),
        out_specs=(P("span", None, None, "stream", None), P()),
        check_vma=False,
    )
```

time: 202 us -> 183 us (0.906)
  waiting for transfers between devices: 119 us -> 68.7 us
  Pallas kernels: 16.6 us -> 39.2 us
  local copies, waits for them, and re-layouts: 10.6 us -> 32.4 us
  other arithmetic: 15.2 us -> 3.78 us
  matrix products: 11 us -> 3 us
  starting transfers between devices: 27.6 us -> 33.5 us
    ppermute x14 -> x29, waiting for transfers between devices: 114 us -> 68.7 us  [swap(): return lax.ppermute(value, axis, [(i, i ^ dist) for i in range(count)])]
    pallas_call x2 -> x11, Pallas kernels: 10.4 us -> 32.8 us  [the longest x4 17.5 us: transform(): pl.pallas_call(functools.partial(transform_kernel, len(raws), 2 + len(raw...]
    slice x5 -> x13, local copies, waits for them, and re-layouts: 1.82 us -> 14.3 us  [the longest x3 4.63 us: gather(): part = value[:, n * size:(n + 1) * size] if cuts > 1 else value]
    unnamed x21 -> x49, local copies, waits for them, and re-layouts: 4 us -> 13.6 us
    dot_general x4 -> x2, matrix products: 11 us -> 3 us  [the longest x1 2.49 us: shards(): jnp.einsum('bmrf,bmfl->mrbl', shapes, hot, precision=HI)]
    add x5 -> x8, other arithmetic: 6.76 us -> 0.03 us  [wave_rows(): (me ^ d) * cells + start + jnp.arange(size, dtype=jnp.int32)]
    ppermute x2, waiting for transfers between devices: 4.78 us -> 0.01 us  [halo(): right = lax.ppermute(head, axis, [(i + 1, i) for i in range(ends)])]
    ppermute x14 -> x29, starting transfers between devices: 17.1 us -> 21.2 us  [swap(): return lax.ppermute(value, axis, [(i, i ^ dist) for i in range(count)])]
  transfers between devices with their start and end apart: 18 -> 33, of which waited for: 9 -> 13; matrix products, arithmetic and copies ran while one was open for 15% -> 13% of each run, Pallas kernels for 8% -> 15%
where the time goes in v1:
time: 183 us; the launch traced here: 182 us
  waiting for transfers between devices  68.7 us (38%)
  Pallas kernels  39.2 us (21%)
  starting transfers between devices  33.5 us (18%)
  local copies, waits for them, and re-layouts  32.4 us (18%)
  other arithmetic  3.78 us (2%)
  matrix products  3 us (2%)
    ppermute x29, waiting for transfers between devices, swap(): return lax.ppermute(value, axis, [(i, i ^ dist) for i in range(count)])  68.7 us
    ppermute x29, starting transfers between devices, swap(): return lax.ppermute(value, axis, [(i, i ^ dist) for i in range(count)])  21.2 us
    pallas_call x4, Pallas kernels, transform(): pl.pallas_call(functools.partial(transform_kernel, len(raws), 2 + len(raw...  17.5 us
    unnamed x49, local copies, waits for them, and re-layouts  13.6 us
    pallas_call x1, Pallas kernels, shards(): pl.pallas_call(functools.partial(last_kernel, pieces), grid=grid, in_spec...  10.2 us
    ppermute x2, starting transfers between devices, halo(): left = lax.ppermute(tail, axis, [(i, i + 1) for i in range(ends)])  9.73 us
    pallas_call x1, Pallas kernels, shards(): pl.pallas_call(near_kernel, grid=grid, in_specs=[SMEM, by_wave(state_shap...  6.39 us
    slice x3, local copies, waits for them, and re-layouts, gather(): part = value[:, n * size:(n + 1) * size] if cuts > 1 else value  4.63 us
  transfers between devices with their start and end apart: 33, of which 13 were waited for; matrix products, arithmetic and copies ran while one was open for 13% of the time, Pallas kernels for 15%

profile of v1, /device:TPU:0, one launch (start us, length us, event | category | flops | bytes accessed | tf_op | source)
XLA Modules:
  0.0 181.7 jit_solution(14028297505281331584)
XLA Ops:
  2.2 1.7 copy-done.2
  3.9 2.5 %split.1 = (f32[161,8,128]{2,1,0:T(8,128)}, f32[5,32,8,128]{3,2,1,0:T(8,128)}) custom-call(f32[5,32,32,128]{3,2,1,0:T(8,128)S(1)} %copy-done.2, f32[5,32,32,128]{3,2,1,0:T(8,128)S(1)} %copy-done.2, f32[8,128]{1,0:T(8,128)S(1)} %maximum_maximum_fusion.faces), custom_call_target="tpu_custom_call" | custom-call | tf_op jit(solution)/shard_map/split/pallas_call | solution.py:58
  6.9 2.6 %collective-permute-start = (f32[161,8,128]{2,1,0:T(8,128)}, f32[161,8,128]{2,1,0:T(8,128)}, u32[]{:S(2)}, u32[]{:S(2)}) collective-permute-start(f32[161,8,128]{2,1,0:T(8,128)} %get-tuple-element.12), channel_id=1, source_target_pairs={{0,2},{1,3},{2,0},{3,1},{4,6},{5,7},{6,4},{7,5},{8,10},{9,11},{10,... | collective-permute-start | bytes 1978376 | tf_op jit(solution)/shard_map/ppermute | solution.py:16
  10.9 2.6 %collective-permute-start.6 = (f32[5,32,16,128]{3,2,1,0:T(8,128)}, f32[5,32,16,128]{3,2,1,0:T(8,128)}, u32[]{:S(2)}, u32[]{:S(2)}) collective-permute-start(f32[5,32,16,128]{3,2,1,0:T(8,128)} %slice.85), channel_id=1, source_target_pairs={{0,4},{1,5},{2,6},{3,7},{4,0},{5,1},{6,2},{7,3},{8,12},{9,13},{10,... | collective-permute-start | bytes 3932168 | tf_op jit(solution)/shard_map/ppermute | solution.py:16
  14.6 2.1 %fusion.25 = (f32[16,5,2,1,128]{4,3,2,1,0:T(1,128)}, f32[16,5,2,1,128]{4,3,2,1,0:T(1,128)}) fusion(f32[16,5,2,32,128]{4,3,2,1,0:T(8,128)} %state.1), kind=kLoop, calls=%fused_computation.93 | loop fusion | bytes 327680 | tf_op jit(solution)/shard_map/slice | solution.py:281
  16.7 2.0 %copy.49.refs_0_ = f32[5,32,8,128]{3,2,1,0:T(8,128)} copy(f32[5,32,8,128]{3,2,1,0:T(8,128)} %get-tuple-element.15) | data formatting | bytes 1310720
  18.7 19.1 %collective-permute-done.refs_1_ = f32[161,8,128]{2,1,0:T(8,128)} collective-permute-done((f32[161,8,128]{2,1,0:T(8,128)}, f32[161,8,128]{2,1,0:T(8,128)}, u32[]{:S(2)}, u32[]{:S(2)}) %collective-permute-start) | collective-permute-done | bytes 659488 | tf_op jit(solution)/shard_map/ppermute | solution.py:16
  40.4 5.0 %gathered.2 = (f32[1280,128]{1,0:T(8,128)S(1)}, f32[1312,128]{1,0:T(8,128)}) custom-call(bf16[64,128]{1,0:T(8,128)(2,1)S(1)} %get-tuple-element.47.refs_0_, bf16[64,128]{1,0:T(8,128)(2,1)S(1)} %get-tuple-element.46.refs_1_, f32[1288,128]{1,0:T(8,128)} %bitcast.4.refs_2_, f32[1288,128]{1,0:T(8,128)} %bitcast.5.refs_3_, f32[1288,128]{1,0:T(8,128)} %bitcast.6.refs_4_, ...), custom_call_target="tpu_custom_call" | custom-call | tf_op jit(solution)/shard_map/gathered/pallas_call | solution.py:130
  46.3 20.4 %collective-permute-done.7.refs_0_ = f32[5,32,8,128]{3,2,1,0:T(8,128)} collective-permute-done((f32[5,32,8,128]{3,2,1,0:T(8,128)}, f32[5,32,8,128]{3,2,1,0:T(8,128)}, u32[]{:S(2)}, u32[]{:S(2)}) %collective-permute-start.7) | collective-permute-done | bytes 655392 | tf_op jit(solution)/shard_map/ppermute | solution.py:16
  68.6 2.6 %collective-permute-done.6 = f32[5,32,16,128]{3,2,1,0:T(8,128)} collective-permute-done((f32[5,32,16,128]{3,2,1,0:T(8,128)}, f32[5,32,16,128]{3,2,1,0:T(8,128)}, u32[]{:S(2)}, u32[]{:S(2)}) %collective-permute-start.6) | collective-permute-done | bytes 1310752 | tf_op jit(solution)/shard_map/ppermute | solution.py:16
  71.2 2.4 %fusion.26 = (f32[5,32,8,128]{3,2,1,0:T(8,128)}, f32[5,32,8,128]{3,2,1,0:T(8,128)}) fusion(f32[5,32,16,128]{3,2,1,0:T(8,128)} %collective-permute-done.6), kind=kLoop, calls=%fused_computation.94 | loop fusion | bytes 2621440 | tf_op jit(solution)/shard_map/slice | solution.py:323
  74.2 4.1 %gathered.3 = (f32[1280,128]{1,0:T(8,128)S(1)}, f32[1280,128]{1,0:T(8,128)S(1)}) custom-call(bf16[64,128]{1,0:T(8,128)(2,1)S(1)} %get-tuple-element.43.refs_0_, bf16[64,128]{1,0:T(8,128)(2,1)S(1)} %get-tuple-element.42.refs_1_, f32[1280,128]{1,0:T(8,128)} %bitcast.15.refs_2_, f32[1280,128]{1,0:T(8,128)} %bitcast.16.refs_3_, f32[1280,128]{1,0:T(8,128)} %bitcast.17.refs_4_, ...), custom_call_target="tpu_custom_call" | custom-call | tf_op jit(solution)/shard_map/gathered/pallas_call | solution.py:130
  84.8 3.7 %crossing.2 = (f32[1280,128]{1,0:T(8,128)S(1)}, f32[1280,128]{1,0:T(8,128)S(1)}) custom-call(bf16[64,128]{1,0:T(8,128)(2,1)S(1)} %get-tuple-element.45.refs_0_, bf16[64,128]{1,0:T(8,128)(2,1)S(1)} %get-tuple-element.44.refs_1_, f32[1280,128]{1,0:T(8,128)} %bitcast.13.refs_2_, f32[1280,128]{1,0:T(8,128)S(1)} %bitcast.51, f32[1280,128]{1,0:T(8,128)S(1)} %bitcast.63, ...), custom_call_target="tpu_custom_call" | custom-call | tf_op jit(solution)/shard_map/crossing/pallas_call | solution.py:130
  90.2 2.2 %fusion.28 = (f32[5,8,8,128]{3,2,1,0:T(8,128)}, f32[5,8,8,128]{3,2,1,0:T(8,128)}, f32[5,8,8,128]{3,2,1,0:T(8,128)}, f32[5,8,8,128]{3,2,1,0:T(8,128)}) fusion(f32[5,32,8,128]{3,2,1,0:T(8,128)} %gate.7), kind=kLoop, calls=%fused_computation.96 | loop fusion | bytes 1310720 | tf_op jit(solution)/shard_map/slice | solution.py:303
  92.5 4.2 %collective-permute-start.23 = (f32[5,32,8,128]{3,2,1,0:T(8,128)}, f32[5,32,8,128]{3,2,1,0:T(8,128)}, u32[]{:S(2)}, u32[]{:S(2)}) collective-permute-start(f32[5,32,8,128]{3,2,1,0:T(8,128)} %bitcast.58), channel_id=1, source_target_pairs={{0,2},{1,3},{2,0},{3,1},{4,6},{5,7},{6,4},{7,5},{8,10},{9,11},{10,... | collective-permute-start | bytes 1966088 | tf_op jit(solution)/shard_map/ppermute | solution.py:16
  99.8 5.2 %collective-permute-start.4 = (f32[16,5,2,1,128]{4,3,2,1,0:T(1,128)}, f32[16,5,2,1,128]{4,3,2,1,0:T(1,128)}, u32[]{:S(2)}, u32[]{:S(2)}) collective-permute-start(f32[16,5,2,1,128]{4,3,2,1,0:T(1,128)} %get-tuple-element.25), channel_id=1, source_target_pairs={{0,8},{8,16},{16,24},{1,9},{9,17},{17,25},{2,10},{10,18},{18,26},{... | collective-permute-start | bytes 245768 | tf_op jit(solution)/shard_map/ppermute | solution.py:21
  108.2 4.7 %crossing.3 = (f32[1280,128]{1,0:T(8,128)S(1)}, f32[1280,128]{1,0:T(8,128)}) custom-call(bf16[64,128]{1,0:T(8,128)(2,1)S(1)} %get-tuple-element.45.refs_0_, bf16[64,128]{1,0:T(8,128)(2,1)S(1)} %get-tuple-element.44.refs_1_, f32[1280,128]{1,0:T(8,128)} %bitcast.12.refs_2_, f32[1280,128]{1,0:T(8,128)S(1)} %bitcast.50, f32[1280,128]{1,0:T(8,128)} %bitcast.31.refs_4_, ...), custom_call_target="tpu_custom_call" | custom-call | tf_op jit(solution)/shard_map/crossing/pallas_call | solution.py:130
  114.6 6.4 %near.1.near_start.near_end = f32[16,5,2,32,128]{4,3,2,1,0:T(8,128)S(1)} custom-call(f32[4,5,5]{2,1,0:T(8,128)S(1)} %copy.38.cpl, f32[16,5,2,32,128]{4,3,2,1,0:T(8,128)S(1)} %copy-done.6, f32[16,5,2,1,128]{4,3,2,1,0:T(1,128)} %collective-permute-done.4.left, f32[16,5,2,1,128]{4,3,2,1,0:T(1,128)} %collective-permute-done.5.right, f32[5,32,8,128]{3,2,1,0:T(8,128)} %bitcast.36.after), custom_call_target="tpu_custom_call" | custom-call | tf_op jit(solution)/shard_map/near/pallas_call | solution.py:332
  123.2 2.0 %slice.108 = f32[1280,128]{1,0:T(8,128)} slice(f32[1312,128]{1,0:T(8,128)} %collective-permute-done.3), slice={[0:1280], [0:128]} | slice | bytes 1310720 | tf_op jit(solution)/shard_map/slice | solution.py:320
  126.6 2.7 %edge.1 = f32[16,5,2,8,128]{4,3,2,1,0:T(8,128)} custom-call(f32[16,5]{1,0:T(8,128)} %copy-done.18, f32[5,32,8,128]{3,2,1,0:T(8,128)} %bitcast.52, f32[5,32,8,128]{3,2,1,0:T(8,128)} %bitcast.75, f32[16,5,2,32,128]{4,3,2,1,0:T(8,128)} %copy-done.1, f32[16,5,2,32,128]{4,3,2,1,0:T(8,128)} %copy-done.1, f32[5,32,128]{2,1,0:T(8,128)} %copy-done.12, ...), custom_call_target="tpu_custom_call" | custom-call | tf_op jit(solution)/shard_map/edge/pallas_call | solution.py:347
  132.0 4.6 %collective-permute-start.24 = (f32[16,5,2,1,128]{4,3,2,1,0:T(1,128)S(1)}, f32[16,5,2,1,128]{4,3,2,1,0:T(1,128)S(1)}, u32[]{:S(2)}, u32[]{:S(2)}) collective-permute-start(f32[16,5,2,1,128]{4,3,2,1,0:T(1,128)S(1)} %get-tuple-element.29), channel_id=1, source_target_pairs={{0,8},{8,16},{16,24},{1,9},{9,17},{17,25},{2,10},{10,18},{18,26},{... | collective-permute-start | bytes 245768 | tf_op jit(solution)/shard_map/ppermute | solution.py:21
  136.6 2.5 %fusion.2 = f32[2,2,8,1024]{3,1,2,0:T(2,128)S(1)} fusion(f32[8,2,128]{2,0,1:T(8,128)S(1)} %copy.40, f32[8,2,2,128]{3,0,2,1:T(8,128)S(1)} %bitcast.81), kind=kOutput, calls=%fused_computation.3 | convolution fusion | flops 52428800 | bytes 155648 | tf_op jit(solution)/shard_map/bmrf,bmfl->mrbl/dot_general | solution.py:364
  139.3 4.4 %collective-permute-done.26.rest_5_ = f32[5,32,8,128]{3,2,1,0:T(8,128)} collective-permute-done((f32[5,32,8,128]{3,2,1,0:T(8,128)}, f32[5,32,8,128]{3,2,1,0:T(8,128)}, u32[]{:S(2)}, u32[]{:S(2)}) %collective-permute-start.26) | collective-permute-done | bytes 655392 | tf_op jit(solution)/shard_map/ppermute | solution.py:16
  143.8 8.9 %collective-permute-done.27.rest_7_ = f32[5,32,8,128]{3,2,1,0:T(8,128)} collective-permute-done((f32[5,32,8,128]{3,2,1,0:T(8,128)}, f32[5,32,8,128]{3,2,1,0:T(8,128)}, u32[]{:S(2)}, u32[]{:S(2)}) %collective-permute-start.27) | collective-permute-done | bytes 655392 | tf_op jit(solution)/shard_map/ppermute | solution.py:16
  152.6 10.2 %last.1 = f32[16,5,2,32,128]{4,3,2,1,0:T(8,128)} custom-call(f32[4,5,5]{2,1,0:T(8,128)} %copy-done.17, f32[16,5]{1,0:T(8,128)} %copy-done.18, f32[16,5,2,1,128]{4,3,2,1,0:T(1,128)} %copy-done.20, f32[16,5,2,1,128]{4,3,2,1,0:T(1,128)} %copy-done.19, f32[5,32,128]{2,1,0:T(8,128)} %copy-done.12, f32[32,128]{1,0:T(8,128)} %copy-done.16, ...), custom_call_target="tpu_custom_call" | custom-call | tf_op jit(solution)/shard_map/last/pallas_call | solution.py:370
  165.9 3.6 %collective-permute-done.29 = f32[2,2]{1,0:T(2,128)S(1)} collective-permute-done((f32[2,2]{1,0:T(2,128)S(1)}, f32[2,2]{1,0:T(2,128)S(1)}, u32[]{:S(2)}, u32[]{:S(2)}) %collective-permute-start.29) | collective-permute-done | bytes 48 | tf_op jit(solution)/shard_map/ppermute | solution.py:16
  169.5 2.7 %collective-permute-start.30 = (f32[2,2]{1,0:T(2,128)S(1)}, f32[2,2]{1,0:T(2,128)S(1)}, u32[]{:S(2)}, u32[]{:S(2)}) collective-permute-start(f32[2,2]{1,0:T(2,128)S(1)} %add.368), channel_id=1, source_target_pairs={{0,4},{1,5},{2,6},{3,7},{4,0},{5,1},{6,2},{7,3},{8,12},{9,13},{10,... | collective-permute-start | bytes 56 | tf_op jit(solution)/shard_map/ppermute | solution.py:16
  172.1 1.8 collective-permute-done.30
  173.9 1.5 collective-permute-start.31
  175.4 2.1 %collective-permute-done.31 = f32[2,2]{1,0:T(2,128)S(1)} collective-permute-done((f32[2,2]{1,0:T(2,128)S(1)}, f32[2,2]{1,0:T(2,128)S(1)}, u32[]{:S(2)}, u32[]{:S(2)}) %collective-permute-start.31) | collective-permute-done | bytes 48 | tf_op jit(solution)/shard_map/ppermute | solution.py:16
  177.5 1.5 collective-permute-start.32
  179.0 2.1 %collective-permute-done.32 = f32[2,2]{1,0:T(2,128)S(1)} collective-permute-done((f32[2,2]{1,0:T(2,128)S(1)}, f32[2,2]{1,0:T(2,128)S(1)}, u32[]{:S(2)}, u32[]{:S(2)}) %collective-permute-start.32) | collective-permute-done | bytes 48 | tf_op jit(solution)/shard_map/ppermute | solution.py:16
  (165 shorter events, 36.8 us)
Async XLA Ops:
  6.4 33.5 %collective-permute-start.1 = (f32[161,8,128]{2,1,0:T(8,128)}, f32[161,8,128]{2,1,0:T(8,128)}, u32[]{:S(2)}, u32[]{:S(2)}) collective-permute-start(f32[161,8,128]{2,1,0:T(8,128)} %get-tuple-element.12), channel_id=1, source_target_pairs={{0,1},{1,0},{2,3},{3,2},{4,5},{5,4},{6,7},{7,6},{8,9},{9,8},{10,11... | collective-permute-start | bytes 1978376 | tf_op jit(solution)/shard_map/ppermute | solution.py:16
  6.9 30.9 %collective-permute-start = (f32[161,8,128]{2,1,0:T(8,128)}, f32[161,8,128]{2,1,0:T(8,128)}, u32[]{:S(2)}, u32[]{:S(2)}) collective-permute-start(f32[161,8,128]{2,1,0:T(8,128)} %get-tuple-element.12), channel_id=1, source_target_pairs={{0,2},{1,3},{2,0},{3,1},{4,6},{5,7},{6,4},{7,5},{8,10},{9,11},{10,... | collective-permute-start | bytes 1978376 | tf_op jit(solution)/shard_map/ppermute | solution.py:16
  9.5 59.0 %collective-permute-start.8 = (f32[5,32,8,128]{3,2,1,0:T(8,128)}, f32[5,32,8,128]{3,2,1,0:T(8,128)}, u32[]{:S(2)}, u32[]{:S(2)}) collective-permute-start(f32[5,32,8,128]{3,2,1,0:T(8,128)} %get-tuple-element.15), channel_id=1, source_target_pairs={{0,1},{1,0},{2,3},{3,2},{4,5},{5,4},{6,7},{7,6},{8,9},{9,8},{10,11... | collective-permute-start | bytes 1966088 | tf_op jit(solution)/shard_map/ppermute | solution.py:16
  10.9 60.3 %collective-permute-start.6 = (f32[5,32,16,128]{3,2,1,0:T(8,128)}, f32[5,32,16,128]{3,2,1,0:T(8,128)}, u32[]{:S(2)}, u32[]{:S(2)}) collective-permute-start(f32[5,32,16,128]{3,2,1,0:T(8,128)} %slice.85), channel_id=1, source_target_pairs={{0,4},{1,5},{2,6},{3,7},{4,0},{5,1},{6,2},{7,3},{8,12},{9,13},{10,... | collective-permute-start | bytes 3932168 | tf_op jit(solution)/shard_map/ppermute | solution.py:16
  37.8 28.9 %collective-permute-start.7 = (f32[5,32,8,128]{3,2,1,0:T(8,128)}, f32[5,32,8,128]{3,2,1,0:T(8,128)}, u32[]{:S(2)}, u32[]{:S(2)}) collective-permute-start(f32[5,32,8,128]{3,2,1,0:T(8,128)} %gate.4), channel_id=1, source_target_pairs={{0,2},{1,3},{2,0},{3,1},{4,6},{5,7},{6,4},{7,5},{8,10},{9,11},{10,... | collective-permute-start | bytes 1966088 | tf_op jit(solution)/shard_map/ppermute | solution.py:16
  37.8 2.6 %collective-permute-start.2 = (f32[161,8,128]{2,1,0:T(8,128)}, f32[161,8,128]{2,1,0:T(8,128)}, u32[]{:S(2)}, u32[]{:S(2)}) collective-permute-start(f32[161,8,128]{2,1,0:T(8,128)} %collective-permute-done.refs_1_), channel_id=1, source_target_pairs={{0,1},{1,0},{2,3},{3,2},{4,5},{5,4},{6,7},{7,6},{8,9},{9,8},{10,11... | collective-permute-start | bytes 1978376 | tf_op jit(solution)/shard_map/ppermute | solution.py:16
  39.9 42.0 %collective-permute-start.13 = (f32[5,32,8,128]{3,2,1,0:T(8,128)}, f32[5,32,8,128]{3,2,1,0:T(8,128)S(1)}, u32[]{:S(2)}, u32[]{:S(2)}) collective-permute-start(f32[5,32,8,128]{3,2,1,0:T(8,128)} %get-tuple-element.22), channel_id=1, source_target_pairs={{0,1},{1,0},{2,3},{3,2},{4,5},{5,4},{6,7},{7,6},{8,9},{9,8},{10,11... | collective-permute-start | bytes 1966088 | tf_op jit(solution)/shard_map/ppermute | solution.py:16
  67.9 5.7 %collective-permute-start.12 = (f32[5,8,8,128]{3,2,1,0:T(8,128)S(1)}, f32[5,8,8,128]{3,2,1,0:T(8,128)S(1)}, u32[]{:S(2)}, u32[]{:S(2)}) collective-permute-start(f32[5,8,8,128]{3,2,1,0:T(8,128)S(1)} %get-tuple-element.38), channel_id=1, source_target_pairs={{0,1},{1,0},{2,3},{3,2},{4,5},{5,4},{6,7},{7,6},{8,9},{9,8},{10,11... | collective-permute-start | bytes 491528 | tf_op jit(solution)/shard_map/ppermute | solution.py:16
  68.0 6.2 %collective-permute-start.11 = (f32[5,8,8,128]{3,2,1,0:T(8,128)S(1)}, f32[5,8,8,128]{3,2,1,0:T(8,128)S(1)}, u32[]{:S(2)}, u32[]{:S(2)}) collective-permute-start(f32[5,8,8,128]{3,2,1,0:T(8,128)S(1)} %get-tuple-element.39), channel_id=1, source_target_pairs={{0,1},{1,0},{2,3},{3,2},{4,5},{5,4},{6,7},{7,6},{8,9},{9,8},{10,11... | collective-permute-start | bytes 491528 | tf_op jit(solution)/shard_map/ppermute | solution.py:16
  68.5 5.7 %collective-permute-start.10 = (f32[5,8,8,128]{3,2,1,0:T(8,128)S(1)}, f32[5,8,8,128]{3,2,1,0:T(8,128)S(1)}, u32[]{:S(2)}, u32[]{:S(2)}) collective-permute-start(f32[5,8,8,128]{3,2,1,0:T(8,128)S(1)} %get-tuple-element.40), channel_id=1, source_target_pairs={{0,1},{1,0},{2,3},{3,2},{4,5},{5,4},{6,7},{7,6},{8,9},{9,8},{10,11... | collective-permute-start | bytes 491528 | tf_op jit(solution)/shard_map/ppermute | solution.py:16
  71.2 3.0 %collective-permute-start.9 = (f32[5,8,8,128]{3,2,1,0:T(8,128)S(1)}, f32[5,8,8,128]{3,2,1,0:T(8,128)S(1)}, u32[]{:S(2)}, u32[]{:S(2)}) collective-permute-start(f32[5,8,8,128]{3,2,1,0:T(8,128)S(1)} %get-tuple-element.41), channel_id=1, source_target_pairs={{0,1},{1,0},{2,3},{3,2},{4,5},{5,4},{6,7},{7,6},{8,9},{9,8},{10,11... | collective-permute-start | bytes 491528 | tf_op jit(solution)/shard_map/ppermute | solution.py:16
  73.7 23.2 %collective-permute-start.18 = (f32[5,32,8,128]{3,2,1,0:T(8,128)}, f32[5,32,8,128]{3,2,1,0:T(8,128)}, u32[]{:S(2)}, u32[]{:S(2)}) collective-permute-start(f32[5,32,8,128]{3,2,1,0:T(8,128)} %get-tuple-element.23), channel_id=1, source_target_pairs={{0,1},{1,0},{2,3},{3,2},{4,5},{5,4},{6,7},{7,6},{8,9},{9,8},{10,11... | collective-permute-start | bytes 1966088 | tf_op jit(solution)/shard_map/ppermute | solution.py:16
  81.3 1.5 collective-permute-start.17
  81.4 2.3 %collective-permute-start.16 = (f32[5,8,8,128]{3,2,1,0:T(8,128)S(1)}, f32[5,8,8,128]{3,2,1,0:T(8,128)S(1)}, u32[]{:S(2)}, u32[]{:S(2)}) collective-permute-start(f32[5,8,8,128]{3,2,1,0:T(8,128)S(1)} %get-tuple-element.35), channel_id=1, source_target_pairs={{0,1},{1,0},{2,3},{3,2},{4,5},{5,4},{6,7},{7,6},{8,9},{9,8},{10,11... | collective-permute-start | bytes 491528 | tf_op jit(solution)/shard_map/ppermute | solution.py:16
  81.9 1.8 %collective-permute-start.15 = (f32[5,8,8,128]{3,2,1,0:T(8,128)S(1)}, f32[5,8,8,128]{3,2,1,0:T(8,128)S(1)}, u32[]{:S(2)}, u32[]{:S(2)}) collective-permute-start(f32[5,8,8,128]{3,2,1,0:T(8,128)S(1)} %get-tuple-element.36), channel_id=1, source_target_pairs={{0,1},{1,0},{2,3},{3,2},{4,5},{5,4},{6,7},{7,6},{8,9},{9,8},{10,11... | collective-permute-start | bytes 491528 | tf_op jit(solution)/shard_map/ppermute | solution.py:16
  81.9 1.8 collective-permute-start.14
  82.7 39.7 %collective-permute-start.3 = (f32[1312,128]{1,0:T(8,128)}, f32[1312,128]{1,0:T(8,128)}, u32[]{:S(2)}, u32[]{:S(2)}) collective-permute-start(f32[1312,128]{1,0:T(8,128)} %get-tuple-element.14.refs_1_), channel_id=1, source_target_pairs={{0,4},{1,5},{2,6},{3,7},{4,0},{5,1},{6,2},{7,3},{8,12},{9,13},{10,... | collective-permute-start | bytes 2015240 | tf_op jit(solution)/shard_map/ppermute | solution.py:16
  92.4 4.9 %collective-permute-start.22 = (f32[5,8,8,128]{3,2,1,0:T(8,128)}, f32[5,8,8,128]{3,2,1,0:T(8,128)S(1)}, u32[]{:S(2)}, u32[]{:S(2)}) collective-permute-start(f32[5,8,8,128]{3,2,1,0:T(8,128)} %get-tuple-element.30), channel_id=1, source_target_pairs={{0,1},{1,0},{2,3},{3,2},{4,5},{5,4},{6,7},{7,6},{8,9},{9,8},{10,11... | collective-permute-start | bytes 491528 | tf_op jit(solution)/shard_map/ppermute | solution.py:16
  92.5 34.1 %collective-permute-start.23 = (f32[5,32,8,128]{3,2,1,0:T(8,128)}, f32[5,32,8,128]{3,2,1,0:T(8,128)}, u32[]{:S(2)}, u32[]{:S(2)}) collective-permute-start(f32[5,32,8,128]{3,2,1,0:T(8,128)} %bitcast.58), channel_id=1, source_target_pairs={{0,2},{1,3},{2,0},{3,1},{4,6},{5,7},{6,4},{7,5},{8,10},{9,11},{10,... | collective-permute-start | bytes 1966088 | tf_op jit(solution)/shard_map/ppermute | solution.py:16
  96.7 1.6 collective-permute-start.21
  96.9 2.9 %collective-permute-start.20 = (f32[5,8,8,128]{3,2,1,0:T(8,128)}, f32[5,8,8,128]{3,2,1,0:T(8,128)S(1)}, u32[]{:S(2)}, u32[]{:S(2)}) collective-permute-start(f32[5,8,8,128]{3,2,1,0:T(8,128)} %get-tuple-element.32), channel_id=1, source_target_pairs={{0,1},{1,0},{2,3},{3,2},{4,5},{5,4},{6,7},{7,6},{8,9},{9,8},{10,11... | collective-permute-start | bytes 491528 | tf_op jit(solution)/shard_map/ppermute | solution.py:16
  97.2 7.8 %collective-permute-start.19 = (f32[5,8,8,128]{3,2,1,0:T(8,128)}, f32[5,8,8,128]{3,2,1,0:T(8,128)}, u32[]{:S(2)}, u32[]{:S(2)}) collective-permute-start(f32[5,8,8,128]{3,2,1,0:T(8,128)} %get-tuple-element.33), channel_id=1, source_target_pairs={{0,1},{1,0},{2,3},{3,2},{4,5},{5,4},{6,7},{7,6},{8,9},{9,8},{10,11... | collective-permute-start | bytes 491528 | tf_op jit(solution)/shard_map/ppermute | solution.py:16
  98.3 15.4 %collective-permute-start.5 = (f32[16,5,2,1,128]{4,3,2,1,0:T(1,128)}, f32[16,5,2,1,128]{4,3,2,1,0:T(1,128)}, u32[]{:S(2)}, u32[]{:S(2)}) collective-permute-start(f32[16,5,2,1,128]{4,3,2,1,0:T(1,128)} %get-tuple-element.24), channel_id=1, source_target_pairs={{8,0},{16,8},{24,16},{9,1},{17,9},{25,17},{10,2},{18,10},{26,18},{... | collective-permute-start | bytes 245768 | tf_op jit(solution)/shard_map/ppermute | solution.py:22
  99.8 14.7 %collective-permute-start.4 = (f32[16,5,2,1,128]{4,3,2,1,0:T(1,128)}, f32[16,5,2,1,128]{4,3,2,1,0:T(1,128)}, u32[]{:S(2)}, u32[]{:S(2)}) collective-permute-start(f32[16,5,2,1,128]{4,3,2,1,0:T(1,128)} %get-tuple-element.25), channel_id=1, source_target_pairs={{0,8},{8,16},{16,24},{1,9},{9,17},{17,25},{2,10},{10,18},{18,26},{... | collective-permute-start | bytes 245768 | tf_op jit(solution)/shard_map/ppermute | solution.py:21
  105.0 38.7 %collective-permute-start.26 = (f32[5,32,8,128]{3,2,1,0:T(8,128)}, f32[5,32,8,128]{3,2,1,0:T(8,128)}, u32[]{:S(2)}, u32[]{:S(2)}) collective-permute-start(f32[5,32,8,128]{3,2,1,0:T(8,128)} %bitcast.55), channel_id=1, source_target_pairs={{0,4},{1,5},{2,6},{3,7},{4,0},{5,1},{6,2},{7,3},{8,12},{9,13},{10,... | collective-permute-start | bytes 1966088 | tf_op jit(solution)/shard_map/ppermute | solution.py:16
  113.7 38.9 %collective-permute-start.27 = (f32[5,32,8,128]{3,2,1,0:T(8,128)}, f32[5,32,8,128]{3,2,1,0:T(8,128)}, u32[]{:S(2)}, u32[]{:S(2)}) collective-permute-start(f32[5,32,8,128]{3,2,1,0:T(8,128)} %bitcast.36.after), channel_id=1, source_target_pairs={{0,2},{1,3},{2,0},{3,1},{4,6},{5,7},{6,4},{7,5},{8,10},{9,11},{10,... | collective-permute-start | bytes 1966088 | tf_op jit(solution)/shard_map/ppermute | solution.py:16
  130.7 13.0 %collective-permute-start.25 = (f32[16,5,2,1,128]{4,3,2,1,0:T(1,128)S(1)}, f32[16,5,2,1,128]{4,3,2,1,0:T(1,128)S(1)}, u32[]{:S(2)}, u32[]{:S(2)}) collective-permute-start(f32[16,5,2,1,128]{4,3,2,1,0:T(1,128)S(1)} %get-tuple-element.28), channel_id=1, source_target_pairs={{8,0},{16,8},{24,16},{9,1},{17,9},{25,17},{10,2},{18,10},{26,18},{... | collective-permute-start | bytes 245768 | tf_op jit(solution)/shard_map/ppermute | solution.py:22
  132.0 11.7 %collective-permute-start.24 = (f32[16,5,2,1,128]{4,3,2,1,0:T(1,128)S(1)}, f32[16,5,2,1,128]{4,3,2,1,0:T(1,128)S(1)}, u32[]{:S(2)}, u32[]{:S(2)}) collective-permute-start(f32[16,5,2,1,128]{4,3,2,1,0:T(1,128)S(1)} %get-tuple-element.29), channel_id=1, source_target_pairs={{0,8},{8,16},{16,24},{1,9},{9,17},{17,25},{2,10},{10,18},{18,26},{... | collective-permute-start | bytes 245768 | tf_op jit(solution)/shard_map/ppermute | solution.py:21
  165.9 3.6 %collective-permute-start.29 = (f32[2,2]{1,0:T(2,128)S(1)}, f32[2,2]{1,0:T(2,128)S(1)}, u32[]{:S(2)}, u32[]{:S(2)}) collective-permute-start(f32[2,2]{1,0:T(2,128)S(1)} %add.367), channel_id=1, source_target_pairs={{0,2},{1,3},{2,0},{3,1},{4,6},{5,7},{6,4},{7,5},{8,10},{9,11},{10,... | collective-permute-start | bytes 56 | tf_op jit(solution)/shard_map/ppermute | solution.py:16
  169.5 4.5 %collective-permute-start.30 = (f32[2,2]{1,0:T(2,128)S(1)}, f32[2,2]{1,0:T(2,128)S(1)}, u32[]{:S(2)}, u32[]{:S(2)}) collective-permute-start(f32[2,2]{1,0:T(2,128)S(1)} %add.368), channel_id=1, source_target_pairs={{0,4},{1,5},{2,6},{3,7},{4,0},{5,1},{6,2},{7,3},{8,12},{9,13},{10,... | collective-permute-start | bytes 56 | tf_op jit(solution)/shard_map/ppermute | solution.py:16
  173.9 3.6 %collective-permute-start.31 = (f32[2,2]{1,0:T(2,128)S(1)}, f32[2,2]{1,0:T(2,128)S(1)}, u32[]{:S(2)}, u32[]{:S(2)}) collective-permute-start(f32[2,2]{1,0:T(2,128)S(1)} %add.369), channel_id=1, source_target_pairs={{0,8},{8,0},{16,24},{24,16},{1,9},{9,1},{17,25},{25,17},{2,10},{10... | collective-permute-start | bytes 56 | tf_op jit(solution)/shard_map/ppermute | solution.py:16
  177.5 3.6 %collective-permute-start.32 = (f32[2,2]{1,0:T(2,128)S(1)}, f32[2,2]{1,0:T(2,128)S(1)}, u32[]{:S(2)}, u32[]{:S(2)}) collective-permute-start(f32[2,2]{1,0:T(2,128)S(1)} %add.370), channel_id=1, source_target_pairs={{0,16},{8,24},{16,0},{24,8},{1,17},{9,25},{17,1},{25,9},{2,18},{10... | collective-permute-start | bytes 56 | tf_op jit(solution)/shard_map/ppermute | solution.py:16
  (24 other events, 208.5 us)

commit v2 on v1

--- a/solution.py
+++ b/solution.py
@@ -35,7 +35,7 @@
     )(value, *after)
 
 
-def split_kernel(start, end, faces, outer, between):
+def split_kernel(start, end, faces, after, outer, between):
     @pl.when(pl.program_id(0) < pl.num_programs(0) - 1)
     def _():
         outer[:, :4, :] = start[0, :, :4, :]
@@ -48,7 +48,7 @@
         outer[0] = faces[...]
 
 
-def split(source, faces):
+def split(source, faces, after):
     comps, cells, rows, normal = source.shape
     last = comps - 1
 
@@ -58,7 +58,7 @@
     return pl.pallas_call(
         split_kernel,
         grid=(comps + 1,),
-        in_specs=[spec(0), spec(rows // 8 - 1), pl.BlockSpec(faces.shape, lambda c: (0, 0))],
+        in_specs=[spec(0), spec(rows // 8 - 1), pl.BlockSpec(faces.shape, lambda c: (0, 0)), ANY],
         out_specs=[pl.BlockSpec((cells, 8, normal), lambda c: (c, 0, 0)), spec(0)],
         out_shape=[
             jax.ShapeDtypeStruct((comps * cells + 1, 8, normal), jnp.float32),
@@ -67,7 +67,7 @@
         compiler_params=PARAMS,
         cost_estimate=FREE,
         name="split",
-    )(source, source, faces)
+    )(source, source, faces, after)
 
 
 def wave_rows(owners, blocks, me, waves, cells, span_total):
@@ -258,7 +258,6 @@
 PARAMS = pltpu.CompilerParams(vmem_limit_bytes=48 * 1024 * 1024)
 
 
-BUSY = pl.CostEstimate(flops=0, bytes_accessed=60_000_000, transcendentals=0)
 FREE = pl.CostEstimate(flops=0, bytes_accessed=0, transcendentals=0)
 
 
@@ -279,7 +278,7 @@
     diag = lax.dynamic_slice_in_dim(diagonal, first_cell, rows, 1)
     speed = (k_mine.astype(jnp.float32) * (2.0 * math.pi / span_total))[:, None] * span_speed[None, :]
     left0, right0 = halo(initial_state[:, :, :, :1], initial_state[:, :, :, rows - 1 :], "stream")
-    step = 2
+    step = 4
     grid = (waves // step,)
     state_shape = initial_state.shape
     side_shape = left0.shape
@@ -289,7 +288,9 @@
     middle = [forcing[:, :, at : at + 8] for at in range(8, rows - 8, 8)]
     faces = [face_index.astype(jnp.float32), mode_shapes.reshape(2 * modes, -1)]
     faces = jnp.concatenate(faces + [jnp.zeros((8 - 3 * modes, face_index.shape[1]), jnp.float32)], axis=0)
-    outer, between = split(forcing, faces)
+    inner_rows = forcing[:, :, 8 : rows - 8]
+    far_raw = swap(inner_rows, "span", half_span)
+    outer, between = split(forcing, faces, inner_rows)
 
     def gather(raw, got, hold, first, last):
         late = gate(got, *hold) if hold else got
@@ -307,11 +308,9 @@
         return [value for value, _, _ in sets], wave_rows([0, last], blocks, me, waves, cells, span_total), [b for b, _, _ in blocks]
 
     e_got = swap(outer, "span", quarter)
-    far_raw = swap(forcing[:, :, 8 : rows - 8], "span", top)
     raws, tab, face_blocks = gather(outer, e_got, [], quarter, top)
     lines = 2 * waves
-    e_own, e_out = transform(tab, raws, (lines, lines), [keep, diag, speed], "gathered", comps, True)
-    f_got = swap(gate(between, e_got), "span", quarter)
+    e_own, e_out = transform(tab, raws, (lines, lines), [keep, diag, speed, left0, right0], "gathered", comps, True)
     f_got = swap(gate(between, e_got), "span", quarter)
     e_far = swap(e_out, "span", top)
     cut = comps * lines * 8
@@ -367,6 +366,8 @@
     gains = jnp.einsum("mzx,kz->mkx", held, tab, precision=HI).reshape(2 * modes, waves, 2, rows)
     gains = gains * weight[:, None, None]
 
+    step = 4
+    grid = (waves // step,)
     flow = pl.pallas_call(
         functools.partial(last_kernel, pieces),
         grid=grid,

time: 183 us -> 181 us (0.989)
  waiting for transfers between devices: 68.7 us -> 74.6 us
  starting transfers between devices: 33.5 us -> 29.4 us
  local copies, waits for them, and re-layouts: 32.4 us -> 30.3 us
    ppermute x29, waiting for transfers between devices: 68.7 us -> 72.2 us  [swap(): return lax.ppermute(value, axis, [(i, i ^ dist) for i in range(count)])]
    unnamed x49, local copies, waits for them, and re-layouts: 13.6 us -> 10.8 us
    ppermute x29, starting transfers between devices: 21.2 us -> 18.7 us  [swap(): return lax.ppermute(value, axis, [(i, i ^ dist) for i in range(count)])]
    ppermute x2, waiting for transfers between devices: 0.01 us -> 2.34 us  [halo(): left = lax.ppermute(tail, axis, [(i, i + 1) for i in range(ends)])]
  transfers between devices with their start and end apart: 33 -> 33, of which waited for: 13 -> 16; matrix products, arithmetic and copies ran while one was open for 13% -> 12% of each run, Pallas kernels for 15% -> 15%
where the time goes in v2:
time: 181 us; the launch traced here: 179 us
  waiting for transfers between devices  74.6 us (41%)
  Pallas kernels  37.8 us (21%)
  local copies, waits for them, and re-layouts  30.3 us (17%)
  starting transfers between devices  29.4 us (16%)
  other arithmetic  3.2 us (2%)
  matrix products  3 us (2%)
    ppermute x29, waiting for transfers between devices, swap(): return lax.ppermute(value, axis, [(i, i ^ dist) for i in range(count)])  72.2 us
    ppermute x29, starting transfers between devices, swap(): return lax.ppermute(value, axis, [(i, i ^ dist) for i in range(count)])  18.7 us
    pallas_call x4, Pallas kernels, transform(): pl.pallas_call(functools.partial(transform_kernel, len(raws), 2 + len(raw...  18 us
    unnamed x49, local copies, waits for them, and re-layouts  10.8 us
    pallas_call x1, Pallas kernels, shards(): pl.pallas_call(functools.partial(last_kernel, pieces), grid=grid, in_spec...  8.82 us
    ppermute x2, starting transfers between devices, halo(): left = lax.ppermute(tail, axis, [(i, i + 1) for i in range(ends)])  8.11 us
    pallas_call x1, Pallas kernels, shards(): pl.pallas_call(near_kernel, grid=grid, in_specs=[SMEM, by_wave(state_shap...  6.1 us
    slice x3, local copies, waits for them, and re-layouts, gather(): part = value[:, n * size:(n + 1) * size] if cuts > 1 else value  4.63 us
  transfers between devices with their start and end apart: 33, of which 16 were waited for; matrix products, arithmetic and copies ran while one was open for 12% of the time, Pallas kernels for 15%

profile of v2, /device:TPU:0, one launch (start us, length us, event | category | flops | bytes accessed | tf_op | source)
XLA Modules:
  0.0 179.4 jit_solution(17982166286144923664)
XLA Ops:
  1.5 2.6 %slice.81.after = f32[5,32,16,128]{3,2,1,0:T(8,128)} slice(f32[5,32,32,128]{3,2,1,0:T(8,128)} %end.1), slice={[0:5], [0:32], [8:24], [0:128]} | slice | bytes 2621440 | tf_op jit(solution)/shard_map/slice | solution.py:291
  4.2 2.3 %split.1 = (f32[161,8,128]{2,1,0:T(8,128)}, f32[5,32,8,128]{3,2,1,0:T(8,128)S(1)}) custom-call(f32[5,32,32,128]{3,2,1,0:T(8,128)S(1)} %copy-done.2, f32[5,32,32,128]{3,2,1,0:T(8,128)S(1)} %copy-done.2, f32[8,128]{1,0:T(8,128)S(1)} %maximum_maximum_fusion.faces, f32[5,32,16,128]{3,2,1,0:T(8,128)} %slice.81.after), custom_call_target="tpu_custom_call" | custom-call | tf_op jit(solution)/shard_map/split/pallas_call | solution.py:58
  7.8 2.6 %collective-permute-start = (f32[161,8,128]{2,1,0:T(8,128)}, f32[161,8,128]{2,1,0:T(8,128)}, u32[]{:S(2)}, u32[]{:S(2)}) collective-permute-start(f32[161,8,128]{2,1,0:T(8,128)} %get-tuple-element.12), channel_id=1, source_target_pairs={{0,2},{1,3},{2,0},{3,1},{4,6},{5,7},{6,4},{7,5},{8,10},{9,11},{10,... | collective-permute-start | bytes 1978376 | tf_op jit(solution)/shard_map/ppermute | solution.py:16
  10.3 2.6 %collective-permute-start.6 = (f32[5,32,16,128]{3,2,1,0:T(8,128)}, f32[5,32,16,128]{3,2,1,0:T(8,128)}, u32[]{:S(2)}, u32[]{:S(2)}) collective-permute-start(f32[5,32,16,128]{3,2,1,0:T(8,128)} %slice.81.after), channel_id=1, source_target_pairs={{0,4},{1,5},{2,6},{3,7},{4,0},{5,1},{6,2},{7,3},{8,12},{9,13},{10,... | collective-permute-start | bytes 3932168 | tf_op jit(solution)/shard_map/ppermute | solution.py:16
  16.9 2.0 %copy.49.refs_0_ = f32[5,32,8,128]{3,2,1,0:T(8,128)} copy(f32[5,32,8,128]{3,2,1,0:T(8,128)} %copy-done.9) | data formatting | bytes 1310720
  18.8 21.3 %collective-permute-done.refs_1_ = f32[161,8,128]{2,1,0:T(8,128)} collective-permute-done((f32[161,8,128]{2,1,0:T(8,128)}, f32[161,8,128]{2,1,0:T(8,128)}, u32[]{:S(2)}, u32[]{:S(2)}) %collective-permute-start) | collective-permute-done | bytes 659488 | tf_op jit(solution)/shard_map/ppermute | solution.py:16
  40.3 3.6 %collective-permute-start.3 = (f32[16,5,2,1,128]{4,3,2,1,0:T(1,128)S(1)}, f32[16,5,2,1,128]{4,3,2,1,0:T(1,128)S(1)}, u32[]{:S(2)}, u32[]{:S(2)}) collective-permute-start(f32[16,5,2,1,128]{4,3,2,1,0:T(1,128)S(1)} %get-tuple-element.25), channel_id=1, source_target_pairs={{0,8},{8,16},{16,24},{1,9},{9,17},{17,25},{2,10},{10,18},{18,26},{... | collective-permute-start | bytes 245768 | tf_op jit(solution)/shard_map/ppermute | solution.py:21
  43.8 2.3 %collective-permute-done.3.refs_9_.left = f32[16,5,2,1,128]{4,3,2,1,0:T(1,128)S(1)} collective-permute-done((f32[16,5,2,1,128]{4,3,2,1,0:T(1,128)S(1)}, f32[16,5,2,1,128]{4,3,2,1,0:T(1,128)S(1)}, u32[]{:S(2)}, u32[]{:S(2)}) %collective-permute-start.3) | collective-permute-done | bytes 81952 | tf_op jit(solution)/shard_map/ppermute | solution.py:21
  48.7 5.0 %gathered.2 = (f32[1280,128]{1,0:T(8,128)S(1)}, f32[1312,128]{1,0:T(8,128)}) custom-call(bf16[64,128]{1,0:T(8,128)(2,1)S(1)} %get-tuple-element.47.refs_0_, bf16[64,128]{1,0:T(8,128)(2,1)S(1)} %get-tuple-element.46.refs_1_, f32[1288,128]{1,0:T(8,128)} %bitcast.4.refs_2_, f32[1288,128]{1,0:T(8,128)} %bitcast.5.refs_3_, f32[1288,128]{1,0:T(8,128)} %bitcast.6.refs_4_, ...), custom_call_target="tpu_custom_call" | custom-call | tf_op jit(solution)/shard_map/gathered/pallas_call | solution.py:130
  54.5 16.6 %collective-permute-done.7.refs_0_ = f32[5,32,8,128]{3,2,1,0:T(8,128)} collective-permute-done((f32[5,32,8,128]{3,2,1,0:T(8,128)}, f32[5,32,8,128]{3,2,1,0:T(8,128)}, u32[]{:S(2)}, u32[]{:S(2)}) %collective-permute-start.7) | collective-permute-done | bytes 655392 | tf_op jit(solution)/shard_map/ppermute | solution.py:16
  73.5 2.5 %fusion.26 = (f32[5,32,8,128]{3,2,1,0:T(8,128)}, f32[5,32,8,128]{3,2,1,0:T(8,128)}) fusion(f32[5,32,16,128]{3,2,1,0:T(8,128)} %collective-permute-done.6), kind=kLoop, calls=%fused_computation.94 | loop fusion | bytes 2621440 | tf_op jit(solution)/shard_map/slice | solution.py:322
  76.1 3.9 %gathered.3 = (f32[1280,128]{1,0:T(8,128)S(1)}, f32[1280,128]{1,0:T(8,128)S(1)}) custom-call(bf16[64,128]{1,0:T(8,128)(2,1)S(1)} %get-tuple-element.43.refs_0_, bf16[64,128]{1,0:T(8,128)(2,1)S(1)} %get-tuple-element.42.refs_1_, f32[1280,128]{1,0:T(8,128)S(1)} %bitcast.57, f32[1280,128]{1,0:T(8,128)} %bitcast.16.refs_3_, f32[1280,128]{1,0:T(8,128)} %bitcast.17.refs_4_, ...), custom_call_target="tpu_custom_call" | custom-call | tf_op jit(solution)/shard_map/gathered/pallas_call | solution.py:130
  84.5 1.7 collective-permute-start.5
  87.3 4.5 %crossing.2 = (f32[1280,128]{1,0:T(8,128)S(1)}, f32[1280,128]{1,0:T(8,128)}) custom-call(bf16[64,128]{1,0:T(8,128)(2,1)S(1)} %get-tuple-element.45.refs_0_, bf16[64,128]{1,0:T(8,128)(2,1)S(1)} %get-tuple-element.44.refs_1_, f32[1280,128]{1,0:T(8,128)} %bitcast.13.refs_2_, f32[1280,128]{1,0:T(8,128)S(1)} %bitcast.51, f32[1280,128]{1,0:T(8,128)S(1)} %bitcast.61, ...), custom_call_target="tpu_custom_call" | custom-call | tf_op jit(solution)/shard_map/crossing/pallas_call | solution.py:130
  92.6 2.5 %collective-permute-start.23 = (f32[5,32,8,128]{3,2,1,0:T(8,128)}, f32[5,32,8,128]{3,2,1,0:T(8,128)}, u32[]{:S(2)}, u32[]{:S(2)}) collective-permute-start(f32[5,32,8,128]{3,2,1,0:T(8,128)} %bitcast.29.refs_1_.refs_9_), channel_id=1, source_target_pairs={{0,2},{1,3},{2,0},{3,1},{4,6},{5,7},{6,4},{7,5},{8,10},{9,11},{10,... | collective-permute-start | bytes 1966088 | tf_op jit(solution)/shard_map/ppermute | solution.py:16
  95.1 2.1 %fusion.28 = (f32[5,8,8,128]{3,2,1,0:T(8,128)}, f32[5,8,8,128]{3,2,1,0:T(8,128)}, f32[5,8,8,128]{3,2,1,0:T(8,128)}, f32[5,8,8,128]{3,2,1,0:T(8,128)S(1)}) fusion(f32[5,32,8,128]{3,2,1,0:T(8,128)} %gate.7), kind=kLoop, calls=%fused_computation.96 | loop fusion | bytes 1310720 | tf_op jit(solution)/shard_map/slice | solution.py:304
  101.3 4.7 %crossing.3 = (f32[1280,128]{1,0:T(8,128)S(1)}, f32[1280,128]{1,0:T(8,128)}) custom-call(bf16[64,128]{1,0:T(8,128)(2,1)S(1)} %get-tuple-element.45.refs_0_, bf16[64,128]{1,0:T(8,128)(2,1)S(1)} %get-tuple-element.44.refs_1_, f32[1280,128]{1,0:T(8,128)} %bitcast.12.refs_2_, f32[1280,128]{1,0:T(8,128)S(1)} %bitcast.50, f32[1280,128]{1,0:T(8,128)} %bitcast.31.refs_4_, ...), custom_call_target="tpu_custom_call" | custom-call | tf_op jit(solution)/shard_map/crossing/pallas_call | solution.py:130
  107.6 6.1 %near.1.near_start.near_end = f32[16,5,2,32,128]{4,3,2,1,0:T(8,128)S(1)} custom-call(f32[4,5,5]{2,1,0:T(8,128)S(1)} %copy.38.cpl, f32[16,5,2,32,128]{4,3,2,1,0:T(8,128)S(1)} %copy-done.5, f32[16,5,2,1,128]{4,3,2,1,0:T(1,128)S(1)} %collective-permute-done.3.refs_9_.left, f32[16,5,2,1,128]{4,3,2,1,0:T(1,128)S(1)} %collective-permute-done.4.refs_10_.right, ...), custom_call_target="tpu_custom_call" | custom-call | tf_op jit(solution)/shard_map/near/pallas_call | solution.py:331
  115.2 3.2 %collective-permute-done.5 = f32[1312,128]{1,0:T(8,128)} collective-permute-done((f32[1312,128]{1,0:T(8,128)}, f32[1312,128]{1,0:T(8,128)}, u32[]{:S(2)}, u32[]{:S(2)}) %collective-permute-start.5) | collective-permute-done | bytes 671776 | tf_op jit(solution)/shard_map/ppermute | solution.py:16
  119.2 2.0 %slice.108 = f32[1280,128]{1,0:T(8,128)} slice(f32[1312,128]{1,0:T(8,128)} %collective-permute-done.5), slice={[0:1280], [0:128]} | slice | bytes 1310720 | tf_op jit(solution)/shard_map/slice | solution.py:319
  121.1 3.8 %collective-permute-done.23.after.rest_6_ = f32[5,32,8,128]{3,2,1,0:T(8,128)} collective-permute-done((f32[5,32,8,128]{3,2,1,0:T(8,128)}, f32[5,32,8,128]{3,2,1,0:T(8,128)}, u32[]{:S(2)}, u32[]{:S(2)}) %collective-permute-start.23) | collective-permute-done | bytes 655392 | tf_op jit(solution)/shard_map/ppermute | solution.py:16
  125.0 2.7 %edge.1 = f32[16,5,2,8,128]{4,3,2,1,0:T(8,128)} custom-call(f32[16,5]{1,0:T(8,128)} %copy-done.17, f32[5,32,8,128]{3,2,1,0:T(8,128)} %bitcast.52, f32[5,32,8,128]{3,2,1,0:T(8,128)} %bitcast.74, f32[16,5,2,32,128]{4,3,2,1,0:T(8,128)} %copy-done.1, f32[16,5,2,32,128]{4,3,2,1,0:T(8,128)} %copy-done.1, f32[5,32,128]{2,1,0:T(8,128)} %copy-done.11, ...), custom_call_target="tpu_custom_call" | custom-call | tf_op jit(solution)/shard_map/edge/pallas_call | solution.py:346
  130.4 4.6 %collective-permute-start.24 = (f32[16,5,2,1,128]{4,3,2,1,0:T(1,128)S(1)}, f32[16,5,2,1,128]{4,3,2,1,0:T(1,128)S(1)}, u32[]{:S(2)}, u32[]{:S(2)}) collective-permute-start(f32[16,5,2,1,128]{4,3,2,1,0:T(1,128)S(1)} %get-tuple-element.29), channel_id=1, source_target_pairs={{0,8},{8,16},{16,24},{1,9},{9,17},{17,25},{2,10},{10,18},{18,26},{... | collective-permute-start | bytes 245768 | tf_op jit(solution)/shard_map/ppermute | solution.py:21
  134.9 2.5 %fusion.2 = f32[2,2,8,1024]{3,1,2,0:T(2,128)S(1)} fusion(f32[8,2,128]{2,0,1:T(8,128)S(1)} %copy.40, f32[8,2,2,128]{3,0,2,1:T(8,128)S(1)} %bitcast.80), kind=kOutput, calls=%fused_computation.3 | convolution fusion | flops 52428800 | bytes 155648 | tf_op jit(solution)/shard_map/bmrf,bmfl->mrbl/dot_general | solution.py:363
  137.6 8.1 %collective-permute-done.26.rest_5_ = f32[5,32,8,128]{3,2,1,0:T(8,128)} collective-permute-done((f32[5,32,8,128]{3,2,1,0:T(8,128)}, f32[5,32,8,128]{3,2,1,0:T(8,128)}, u32[]{:S(2)}, u32[]{:S(2)}) %collective-permute-start.26) | collective-permute-done | bytes 655392 | tf_op jit(solution)/shard_map/ppermute | solution.py:16
  145.7 6.1 %collective-permute-done.27.rest_7_ = f32[5,32,8,128]{3,2,1,0:T(8,128)} collective-permute-done((f32[5,32,8,128]{3,2,1,0:T(8,128)}, f32[5,32,8,128]{3,2,1,0:T(8,128)}, u32[]{:S(2)}, u32[]{:S(2)}) %collective-permute-start.27) | collective-permute-done | bytes 655392 | tf_op jit(solution)/shard_map/ppermute | solution.py:16
  151.8 8.8 %last.1 = f32[16,5,2,32,128]{4,3,2,1,0:T(8,128)} custom-call(f32[4,5,5]{2,1,0:T(8,128)} %copy-done.16, f32[16,5]{1,0:T(8,128)} %copy-done.17, f32[16,5,2,1,128]{4,3,2,1,0:T(1,128)} %copy-done.19, f32[16,5,2,1,128]{4,3,2,1,0:T(1,128)} %copy-done.18, f32[5,32,128]{2,1,0:T(8,128)} %copy-done.11, f32[32,128]{1,0:T(8,128)} %copy-done.15, ...), custom_call_target="tpu_custom_call" | custom-call | tf_op jit(solution)/shard_map/last/pallas_call | solution.py:371
  163.7 3.6 %collective-permute-done.29 = f32[2,2]{1,0:T(2,128)S(1)} collective-permute-done((f32[2,2]{1,0:T(2,128)S(1)}, f32[2,2]{1,0:T(2,128)S(1)}, u32[]{:S(2)}, u32[]{:S(2)}) %collective-permute-start.29) | collective-permute-done | bytes 48 | tf_op jit(solution)/shard_map/ppermute | solution.py:16
  167.3 1.6 collective-permute-start.30
  168.9 2.8 %collective-permute-done.30 = f32[2,2]{1,0:T(2,128)S(1)} collective-permute-done((f32[2,2]{1,0:T(2,128)S(1)}, f32[2,2]{1,0:T(2,128)S(1)}, u32[]{:S(2)}, u32[]{:S(2)}) %collective-permute-start.30) | collective-permute-done | bytes 48 | tf_op jit(solution)/shard_map/ppermute | solution.py:16
  173.2 2.1 %collective-permute-done.31 = f32[2,2]{1,0:T(2,128)S(1)} collective-permute-done((f32[2,2]{1,0:T(2,128)S(1)}, f32[2,2]{1,0:T(2,128)S(1)}, u32[]{:S(2)}, u32[]{:S(2)}) %collective-permute-start.31) | collective-permute-done | bytes 48 | tf_op jit(solution)/shard_map/ppermute | solution.py:16
  176.8 2.1 %collective-permute-done.32 = f32[2,2]{1,0:T(2,128)S(1)} collective-permute-done((f32[2,2]{1,0:T(2,128)S(1)}, f32[2,2]{1,0:T(2,128)S(1)}, u32[]{:S(2)}, u32[]{:S(2)}) %collective-permute-start.32) | collective-permute-done | bytes 48 | tf_op jit(solution)/shard_map/ppermute | solution.py:16
  (165 shorter events, 35.9 us)
Async XLA Ops:
  7.3 40.9 %collective-permute-start.1 = (f32[161,8,128]{2,1,0:T(8,128)}, f32[161,8,128]{2,1,0:T(8,128)}, u32[]{:S(2)}, u32[]{:S(2)}) collective-permute-start(f32[161,8,128]{2,1,0:T(8,128)} %get-tuple-element.12), channel_id=1, source_target_pairs={{0,1},{1,0},{2,3},{3,2},{4,5},{5,4},{6,7},{7,6},{8,9},{9,8},{10,11... | collective-permute-start | bytes 1978376 | tf_op jit(solution)/shard_map/ppermute | solution.py:16
  7.8 32.4 %collective-permute-start = (f32[161,8,128]{2,1,0:T(8,128)}, f32[161,8,128]{2,1,0:T(8,128)}, u32[]{:S(2)}, u32[]{:S(2)}) collective-permute-start(f32[161,8,128]{2,1,0:T(8,128)} %get-tuple-element.12), channel_id=1, source_target_pairs={{0,2},{1,3},{2,0},{3,1},{4,6},{5,7},{6,4},{7,5},{8,10},{9,11},{10,... | collective-permute-start | bytes 1978376 | tf_op jit(solution)/shard_map/ppermute | solution.py:16
  10.3 62.7 %collective-permute-start.6 = (f32[5,32,16,128]{3,2,1,0:T(8,128)}, f32[5,32,16,128]{3,2,1,0:T(8,128)}, u32[]{:S(2)}, u32[]{:S(2)}) collective-permute-start(f32[5,32,16,128]{3,2,1,0:T(8,128)} %slice.81.after), channel_id=1, source_target_pairs={{0,4},{1,5},{2,6},{3,7},{4,0},{5,1},{6,2},{7,3},{8,12},{9,13},{10,... | collective-permute-start | bytes 3932168 | tf_op jit(solution)/shard_map/ppermute | solution.py:16
  14.3 25.9 %collective-permute-start.4 = (f32[16,5,2,1,128]{4,3,2,1,0:T(1,128)S(1)}, f32[16,5,2,1,128]{4,3,2,1,0:T(1,128)S(1)}, u32[]{:S(2)}, u32[]{:S(2)}) collective-permute-start(f32[16,5,2,1,128]{4,3,2,1,0:T(1,128)S(1)} %get-tuple-element.24), channel_id=1, source_target_pairs={{8,0},{16,8},{24,16},{9,1},{17,9},{25,17},{10,2},{18,10},{26,18},{... | collective-permute-start | bytes 245768 | tf_op jit(solution)/shard_map/ppermute | solution.py:22
  40.2 31.0 %collective-permute-start.7 = (f32[5,32,8,128]{3,2,1,0:T(8,128)}, f32[5,32,8,128]{3,2,1,0:T(8,128)}, u32[]{:S(2)}, u32[]{:S(2)}) collective-permute-start(f32[5,32,8,128]{3,2,1,0:T(8,128)} %gate.4), channel_id=1, source_target_pairs={{0,2},{1,3},{2,0},{3,1},{4,6},{5,7},{6,4},{7,5},{8,10},{9,11},{10,... | collective-permute-start | bytes 1966088 | tf_op jit(solution)/shard_map/ppermute | solution.py:16
  40.2 8.5 %collective-permute-start.2 = (f32[161,8,128]{2,1,0:T(8,128)}, f32[161,8,128]{2,1,0:T(8,128)}, u32[]{:S(2)}, u32[]{:S(2)}) collective-permute-start(f32[161,8,128]{2,1,0:T(8,128)} %collective-permute-done.refs_1_), channel_id=1, source_target_pairs={{0,1},{1,0},{2,3},{3,2},{4,5},{5,4},{6,7},{7,6},{8,9},{9,8},{10,11... | collective-permute-start | bytes 1978376 | tf_op jit(solution)/shard_map/ppermute | solution.py:16
  40.3 5.9 %collective-permute-start.3 = (f32[16,5,2,1,128]{4,3,2,1,0:T(1,128)S(1)}, f32[16,5,2,1,128]{4,3,2,1,0:T(1,128)S(1)}, u32[]{:S(2)}, u32[]{:S(2)}) collective-permute-start(f32[16,5,2,1,128]{4,3,2,1,0:T(1,128)S(1)} %get-tuple-element.25), channel_id=1, source_target_pairs={{0,8},{8,16},{16,24},{1,9},{9,17},{17,25},{2,10},{10,18},{18,26},{... | collective-permute-start | bytes 245768 | tf_op jit(solution)/shard_map/ppermute | solution.py:21
  46.2 26.8 %collective-permute-start.8 = (f32[5,32,8,128]{3,2,1,0:T(8,128)}, f32[5,32,8,128]{3,2,1,0:T(8,128)}, u32[]{:S(2)}, u32[]{:S(2)}) collective-permute-start(f32[5,32,8,128]{3,2,1,0:T(8,128)} %copy-done.9), channel_id=1, source_target_pairs={{0,1},{1,0},{2,3},{3,2},{4,5},{5,4},{6,7},{7,6},{8,9},{9,8},{10,11... | collective-permute-start | bytes 1966088 | tf_op jit(solution)/shard_map/ppermute | solution.py:16
  48.2 35.8 %collective-permute-start.13 = (f32[5,32,8,128]{3,2,1,0:T(8,128)}, f32[5,32,8,128]{3,2,1,0:T(8,128)S(1)}, u32[]{:S(2)}, u32[]{:S(2)}) collective-permute-start(f32[5,32,8,128]{3,2,1,0:T(8,128)} %get-tuple-element.22), channel_id=1, source_target_pairs={{0,1},{1,0},{2,3},{3,2},{4,5},{5,4},{6,7},{7,6},{8,9},{9,8},{10,11... | collective-permute-start | bytes 1966088 | tf_op jit(solution)/shard_map/ppermute | solution.py:16
  72.4 3.6 %collective-permute-start.12 = (f32[5,8,8,128]{3,2,1,0:T(8,128)S(1)}, f32[5,8,8,128]{3,2,1,0:T(8,128)S(1)}, u32[]{:S(2)}, u32[]{:S(2)}) collective-permute-start(f32[5,8,8,128]{3,2,1,0:T(8,128)S(1)} %get-tuple-element.38), channel_id=1, source_target_pairs={{0,1},{1,0},{2,3},{3,2},{4,5},{5,4},{6,7},{7,6},{8,9},{9,8},{10,11... | collective-permute-start | bytes 491528 | tf_op jit(solution)/shard_map/ppermute | solution.py:16
  72.5 3.6 %collective-permute-start.11 = (f32[5,8,8,128]{3,2,1,0:T(8,128)S(1)}, f32[5,8,8,128]{3,2,1,0:T(8,128)S(1)}, u32[]{:S(2)}, u32[]{:S(2)}) collective-permute-start(f32[5,8,8,128]{3,2,1,0:T(8,128)S(1)} %get-tuple-element.39), channel_id=1, source_target_pairs={{0,1},{1,0},{2,3},{3,2},{4,5},{5,4},{6,7},{7,6},{8,9},{9,8},{10,11... | collective-permute-start | bytes 491528 | tf_op jit(solution)/shard_map/ppermute | solution.py:16
  73.0 3.1 %collective-permute-start.10 = (f32[5,8,8,128]{3,2,1,0:T(8,128)S(1)}, f32[5,8,8,128]{3,2,1,0:T(8,128)S(1)}, u32[]{:S(2)}, u32[]{:S(2)}) collective-permute-start(f32[5,8,8,128]{3,2,1,0:T(8,128)S(1)} %get-tuple-element.40), channel_id=1, source_target_pairs={{0,1},{1,0},{2,3},{3,2},{4,5},{5,4},{6,7},{7,6},{8,9},{9,8},{10,11... | collective-permute-start | bytes 491528 | tf_op jit(solution)/shard_map/ppermute | solution.py:16
  73.1 3.0 %collective-permute-start.9 = (f32[5,8,8,128]{3,2,1,0:T(8,128)S(1)}, f32[5,8,8,128]{3,2,1,0:T(8,128)S(1)}, u32[]{:S(2)}, u32[]{:S(2)}) collective-permute-start(f32[5,8,8,128]{3,2,1,0:T(8,128)S(1)} %get-tuple-element.41), channel_id=1, source_target_pairs={{0,1},{1,0},{2,3},{3,2},{4,5},{5,4},{6,7},{7,6},{8,9},{9,8},{10,11... | collective-permute-start | bytes 491528 | tf_op jit(solution)/shard_map/ppermute | solution.py:16
  76.0 22.0 %collective-permute-start.18 = (f32[5,32,8,128]{3,2,1,0:T(8,128)}, f32[5,32,8,128]{3,2,1,0:T(8,128)}, u32[]{:S(2)}, u32[]{:S(2)}) collective-permute-start(f32[5,32,8,128]{3,2,1,0:T(8,128)} %get-tuple-element.23), channel_id=1, source_target_pairs={{0,1},{1,0},{2,3},{3,2},{4,5},{5,4},{6,7},{7,6},{8,9},{9,8},{10,11... | collective-permute-start | bytes 1966088 | tf_op jit(solution)/shard_map/ppermute | solution.py:16
  83.0 1.5 collective-permute-start.17
  83.5 2.7 %collective-permute-start.16 = (f32[5,8,8,128]{3,2,1,0:T(8,128)S(1)}, f32[5,8,8,128]{3,2,1,0:T(8,128)S(1)}, u32[]{:S(2)}, u32[]{:S(2)}) collective-permute-start(f32[5,8,8,128]{3,2,1,0:T(8,128)S(1)} %get-tuple-element.35), channel_id=1, source_target_pairs={{0,1},{1,0},{2,3},{3,2},{4,5},{5,4},{6,7},{7,6},{8,9},{9,8},{10,11... | collective-permute-start | bytes 491528 | tf_op jit(solution)/shard_map/ppermute | solution.py:16
  83.6 2.6 %collective-permute-start.15 = (f32[5,8,8,128]{3,2,1,0:T(8,128)S(1)}, f32[5,8,8,128]{3,2,1,0:T(8,128)S(1)}, u32[]{:S(2)}, u32[]{:S(2)}) collective-permute-start(f32[5,8,8,128]{3,2,1,0:T(8,128)S(1)} %get-tuple-element.36), channel_id=1, source_target_pairs={{0,1},{1,0},{2,3},{3,2},{4,5},{5,4},{6,7},{7,6},{8,9},{9,8},{10,11... | collective-permute-start | bytes 491528 | tf_op jit(solution)/shard_map/ppermute | solution.py:16
  84.0 2.2 %collective-permute-start.14 = (f32[5,8,8,128]{3,2,1,0:T(8,128)S(1)}, f32[5,8,8,128]{3,2,1,0:T(8,128)S(1)}, u32[]{:S(2)}, u32[]{:S(2)}) collective-permute-start(f32[5,8,8,128]{3,2,1,0:T(8,128)S(1)} %get-tuple-element.37), channel_id=1, source_target_pairs={{0,1},{1,0},{2,3},{3,2},{4,5},{5,4},{6,7},{7,6},{8,9},{9,8},{10,11... | collective-permute-start | bytes 491528 | tf_op jit(solution)/shard_map/ppermute | solution.py:16
  84.5 33.9 %collective-permute-start.5 = (f32[1312,128]{1,0:T(8,128)}, f32[1312,128]{1,0:T(8,128)}, u32[]{:S(2)}, u32[]{:S(2)}) collective-permute-start(f32[1312,128]{1,0:T(8,128)} %get-tuple-element.14.refs_1_), channel_id=1, source_target_pairs={{0,4},{1,5},{2,6},{3,7},{4,0},{5,1},{6,2},{7,3},{8,12},{9,13},{10,... | collective-permute-start | bytes 2015240 | tf_op jit(solution)/shard_map/ppermute | solution.py:16
  92.6 32.4 %collective-permute-start.23 = (f32[5,32,8,128]{3,2,1,0:T(8,128)}, f32[5,32,8,128]{3,2,1,0:T(8,128)}, u32[]{:S(2)}, u32[]{:S(2)}) collective-permute-start(f32[5,32,8,128]{3,2,1,0:T(8,128)} %bitcast.29.refs_1_.refs_9_), channel_id=1, source_target_pairs={{0,2},{1,3},{2,0},{3,1},{4,6},{5,7},{6,4},{7,5},{8,10},{9,11},{10,... | collective-permute-start | bytes 1966088 | tf_op jit(solution)/shard_map/ppermute | solution.py:16
  97.2 1.6 collective-permute-start.22
  97.5 1.8 collective-permute-start.21
  98.0 2.1 %collective-permute-start.20 = (f32[5,8,8,128]{3,2,1,0:T(8,128)}, f32[5,8,8,128]{3,2,1,0:T(8,128)S(1)}, u32[]{:S(2)}, u32[]{:S(2)}) collective-permute-start(f32[5,8,8,128]{3,2,1,0:T(8,128)} %get-tuple-element.32), channel_id=1, source_target_pairs={{0,1},{1,0},{2,3},{3,2},{4,5},{5,4},{6,7},{7,6},{8,9},{9,8},{10,11... | collective-permute-start | bytes 491528 | tf_op jit(solution)/shard_map/ppermute | solution.py:16
  98.8 1.4 collective-permute-start.19
  99.3 46.5 %collective-permute-start.26 = (f32[5,32,8,128]{3,2,1,0:T(8,128)}, f32[5,32,8,128]{3,2,1,0:T(8,128)}, u32[]{:S(2)}, u32[]{:S(2)}) collective-permute-start(f32[5,32,8,128]{3,2,1,0:T(8,128)} %bitcast.55), channel_id=1, source_target_pairs={{0,4},{1,5},{2,6},{3,7},{4,0},{5,1},{6,2},{7,3},{8,12},{9,13},{10,... | collective-permute-start | bytes 1966088 | tf_op jit(solution)/shard_map/ppermute | solution.py:16
  106.8 45.1 %collective-permute-start.27 = (f32[5,32,8,128]{3,2,1,0:T(8,128)}, f32[5,32,8,128]{3,2,1,0:T(8,128)}, u32[]{:S(2)}, u32[]{:S(2)}) collective-permute-start(f32[5,32,8,128]{3,2,1,0:T(8,128)} %bitcast.36.after), channel_id=1, source_target_pairs={{0,2},{1,3},{2,0},{3,1},{4,6},{5,7},{6,4},{7,5},{8,10},{9,11},{10,... | collective-permute-start | bytes 1966088 | tf_op jit(solution)/shard_map/ppermute | solution.py:16
  129.1 16.7 %collective-permute-start.25 = (f32[16,5,2,1,128]{4,3,2,1,0:T(1,128)S(1)}, f32[16,5,2,1,128]{4,3,2,1,0:T(1,128)S(1)}, u32[]{:S(2)}, u32[]{:S(2)}) collective-permute-start(f32[16,5,2,1,128]{4,3,2,1,0:T(1,128)S(1)} %get-tuple-element.28), channel_id=1, source_target_pairs={{8,0},{16,8},{24,16},{9,1},{17,9},{25,17},{10,2},{18,10},{26,18},{... | collective-permute-start | bytes 245768 | tf_op jit(solution)/shard_map/ppermute | solution.py:22
  130.4 15.4 %collective-permute-start.24 = (f32[16,5,2,1,128]{4,3,2,1,0:T(1,128)S(1)}, f32[16,5,2,1,128]{4,3,2,1,0:T(1,128)S(1)}, u32[]{:S(2)}, u32[]{:S(2)}) collective-permute-start(f32[16,5,2,1,128]{4,3,2,1,0:T(1,128)S(1)} %get-tuple-element.29), channel_id=1, source_target_pairs={{0,8},{8,16},{16,24},{1,9},{9,17},{17,25},{2,10},{10,18},{18,26},{... | collective-permute-start | bytes 245768 | tf_op jit(solution)/shard_map/ppermute | solution.py:21
  163.7 3.6 %collective-permute-start.29 = (f32[2,2]{1,0:T(2,128)S(1)}, f32[2,2]{1,0:T(2,128)S(1)}, u32[]{:S(2)}, u32[]{:S(2)}) collective-permute-start(f32[2,2]{1,0:T(2,128)S(1)} %add.367), channel_id=1, source_target_pairs={{0,2},{1,3},{2,0},{3,1},{4,6},{5,7},{6,4},{7,5},{8,10},{9,11},{10,... | collective-permute-start | bytes 56 | tf_op jit(solution)/shard_map/ppermute | solution.py:16
  167.3 4.5 %collective-permute-start.30 = (f32[2,2]{1,0:T(2,128)S(1)}, f32[2,2]{1,0:T(2,128)S(1)}, u32[]{:S(2)}, u32[]{:S(2)}) collective-permute-start(f32[2,2]{1,0:T(2,128)S(1)} %add.368), channel_id=1, source_target_pairs={{0,4},{1,5},{2,6},{3,7},{4,0},{5,1},{6,2},{7,3},{8,12},{9,13},{10,... | collective-permute-start | bytes 56 | tf_op jit(solution)/shard_map/ppermute | solution.py:16
  171.7 3.6 %collective-permute-start.31 = (f32[2,2]{1,0:T(2,128)S(1)}, f32[2,2]{1,0:T(2,128)S(1)}, u32[]{:S(2)}, u32[]{:S(2)}) collective-permute-start(f32[2,2]{1,0:T(2,128)S(1)} %add.369), channel_id=1, source_target_pairs={{0,8},{8,0},{16,24},{24,16},{1,9},{9,1},{17,25},{25,17},{2,10},{10... | collective-permute-start | bytes 56 | tf_op jit(solution)/shard_map/ppermute | solution.py:16
  175.3 3.6 %collective-permute-start.32 = (f32[2,2]{1,0:T(2,128)S(1)}, f32[2,2]{1,0:T(2,128)S(1)}, u32[]{:S(2)}, u32[]{:S(2)}) collective-permute-start(f32[2,2]{1,0:T(2,128)S(1)} %add.370), channel_id=1, source_target_pairs={{0,16},{8,24},{16,0},{24,8},{1,17},{9,25},{17,1},{25,9},{2,18},{10... | collective-permute-start | bytes 56 | tf_op jit(solution)/shard_map/ppermute | solution.py:16
  (24 other events, 183.6 us)

commit v3 on v2

--- a/solution.py
+++ b/solution.py
@@ -204,7 +204,8 @@
 
 
 def tile_sums(owns, fars, low, rows, c, at):
-    outer, between, *middle = [own[c, at] + far[c, at] for own, far in zip(owns, fars)]
+    outer, between, middle = [own[c, at] + far[c, at] for own, far in zip(owns, fars)]
+    middle = [middle[t : t + 8] for t in range(0, rows - 16, 8)]
     return [jnp.where(low, outer, between)] + middle + [jnp.where(low, between, outer)]
 
 
@@ -285,7 +286,6 @@
     ext_shape = (comps, 2, rows + 16, normal)
     top, quarter = half_span, half_span // 2
     lower = [d for d in reversed(inner) if d < quarter]
-    middle = [forcing[:, :, at : at + 8] for at in range(8, rows - 8, 8)]
     faces = [face_index.astype(jnp.float32), mode_shapes.reshape(2 * modes, -1)]
     faces = jnp.concatenate(faces + [jnp.zeros((8 - 3 * modes, face_index.shape[1]), jnp.float32)], axis=0)
     inner_rows = forcing[:, :, 8 : rows - 8]
@@ -318,16 +318,12 @@
     face_blocks = face_blocks + [b ^ top for b in face_blocks]
     e_far = e_far[:cut].reshape(e_own.shape)
 
-    def cross(n, hold):
-        raws, tab, _ = gather(middle[n], far_raw[:, :, 8 * n : 8 * n + 8], hold[:1], top, quarter)
-        own, out = transform(tab, raws, (lines, lines), hold, "crossing", comps)
-        return own, out, swap(out, "span", quarter)
-
     raws, tab, _ = gather(between, f_got, [e_out], quarter, top)
     f_own, f_out = transform(tab, raws, (lines, lines), [], "gathered", comps)
     f_far = swap(f_out, "span", top)
-    c_own, c_out, c_far = cross(0, [f_out])
-    d_own, d_out, d_far = cross(1, [c_out])
+    raws, tab, _ = gather(inner_rows, far_raw, [f_out], top, quarter)
+    m_own, m_out = transform(tab, raws, (lines, lines), [e_far], "crossing", comps)
+    m_far = swap(m_out, "span", quarter)
     near0 = pl.pallas_call(
         near_kernel,
         grid=grid,
@@ -338,8 +334,8 @@
         compiler_params=PARAMS,
         cost_estimate=FREE,
         name="near",
-    )(coupling, initial_state, left0, right0, d_out)
-    owns, fars = [e_own, f_own, c_own, d_own], [e_far, f_far, c_far, d_far]
+    )(coupling, initial_state, left0, right0, m_out)
+    owns, fars = [e_own, f_own, m_own], [e_far, f_far, m_far]
     pieces = len(owns)
 
     first_shape = (waves, comps, 2, 8, normal)
@@ -355,7 +351,7 @@
         compiler_params=LARGE,
         cost_estimate=FREE,
         name="edge",
-    )(speed, e_own, e_far, near0, near0, diag, keep, c_far)
+    )(speed, e_own, e_far, near0, near0, diag, keep, m_out)
     left1, right1 = halo(ends[:, :, :, :1], ends[:, :, :, 7:], "stream")
 
     hot = (face_sets[:, :modes, :, None] == jnp.arange(cells * rows, dtype=jnp.float32)).astype(jnp.float32)
@@ -374,7 +370,7 @@
         in_specs=[SMEM, SMEM]
         + [by_wave(side_shape, step)] * 2
         + [whole(diag.shape), whole(keep.shape), by_wave(state_shape, step)]
-        + [by_wave2(e_own.shape, step)] * (2 * pieces),
+        + [by_wave2(own.shape, step) for own in owns] * 2,
         out_specs=by_wave(state_shape, step),
         out_shape=jax.ShapeDtypeStruct(state_shape, jnp.float32),
         scratch_shapes=[pltpu.VMEM(ext_shape, jnp.float32)],

time: 181 us -> 179 us (0.989)
  waiting for transfers between devices: 74.6 us -> 83.7 us
  local copies, waits for them, and re-layouts: 30.3 us -> 21.5 us
  Pallas kernels: 37.8 us -> 33.7 us
  starting transfers between devices: 29.4 us -> 31.6 us
    ppermute x29 -> x23, waiting for transfers between devices: 72.2 us -> 81.3 us  [swap(): return lax.ppermute(value, axis, [(i, i ^ dist) for i in range(count)])]
    pallas_call x4 -> x3, Pallas kernels: 18 us -> 13.5 us  [transform(): pl.pallas_call(functools.partial(transform_kernel, len(raws), 2 + len(raw...]
    slice x2 -> x0, local copies, waits for them, and re-layouts: 3.68 us -> none  [the longest x1 2.49 us: cross(): far_raw[:, :, 8 * n:8 * n + 8]]
    ppermute x29 -> x23, starting transfers between devices: 18.7 us -> 21 us  [swap(): return lax.ppermute(value, axis, [(i, i ^ dist) for i in range(count)])]
    slice x3 -> x2, local copies, waits for them, and re-layouts: 4.63 us -> 2.59 us  [gather(): part = value[:, n * size:(n + 1) * size] if cuts > 1 else value]
  transfers between devices with their start and end apart: 33 -> 27, of which waited for: 16 -> 17; matrix products, arithmetic and copies ran while one was open for 12% -> 8% of each run, Pallas kernels for 15% -> 10%
where the time goes in v3:
time: 179 us; the launch traced here: 178 us
  waiting for transfers between devices  83.7 us (47%)
  Pallas kernels  33.7 us (19%)
  starting transfers between devices  31.6 us (18%)
  local copies, waits for them, and re-layouts  21.5 us (12%)
  other arithmetic  3.2 us (2%)
  matrix products  3 us (2%)
    ppermute x23, waiting for transfers between devices, swap(): return lax.ppermute(value, axis, [(i, i ^ dist) for i in range(count)])  81.3 us
    ppermute x23, starting transfers between devices, swap(): return lax.ppermute(value, axis, [(i, i ^ dist) for i in range(count)])  21 us
    pallas_call x3, Pallas kernels, transform(): pl.pallas_call(functools.partial(transform_kernel, len(raws), 2 + len(raw...  13.5 us
    unnamed x49, local copies, waits for them, and re-layouts  9.7 us
    pallas_call x1, Pallas kernels, shards(): pl.pallas_call(functools.partial(last_kernel, pieces), grid=grid, in_spec...  8.82 us
    ppermute x2, starting transfers between devices, halo(): left = lax.ppermute(tail, axis, [(i, i + 1) for i in range(ends)])  8.09 us
    pallas_call x1, Pallas kernels, shards(): pl.pallas_call(near_kernel, grid=grid, in_specs=[SMEM, by_wave(state_shap...  6.44 us
  transfers between devices with their start and end apart: 27, of which 17 were waited for; matrix products, arithmetic and copies ran while one was open for 8% of the time, Pallas kernels for 10%

profile of v3, /device:TPU:0, one launch (start us, length us, event | category | flops | bytes accessed | tf_op | source)
XLA Modules:
  0.0 177.8 jit_solution(11107915765184217637)
XLA Ops:
  1.5 1.5 slice.57.after
  3.2 2.3 %split.1 = (f32[161,8,128]{2,1,0:T(8,128)}, f32[5,32,8,128]{3,2,1,0:T(8,128)S(1)}) custom-call(f32[5,32,32,128]{3,2,1,0:T(8,128)S(1)} %copy-done.2, f32[5,32,32,128]{3,2,1,0:T(8,128)S(1)} %copy-done.2, f32[8,128]{1,0:T(8,128)S(1)} %maximum_maximum_fusion.faces, f32[5,32,16,128]{3,2,1,0:T(8,128)S(1)} %slice.57.after), custom_call_target="tpu_custom_call" | custom-call | tf_op jit(solution)/shard_map/split/pallas_call | solution.py:58
  5.9 2.6 %collective-permute-start = (f32[161,8,128]{2,1,0:T(8,128)}, f32[161,8,128]{2,1,0:T(8,128)S(1)}, u32[]{:S(2)}, u32[]{:S(2)}) collective-permute-start(f32[161,8,128]{2,1,0:T(8,128)} %get-tuple-element.10), channel_id=1, source_target_pairs={{0,2},{1,3},{2,0},{3,1},{4,6},{5,7},{6,4},{7,5},{8,10},{9,11},{10,... | collective-permute-start | bytes 1978376 | tf_op jit(solution)/shard_map/ppermute | solution.py:16
  8.5 2.6 %collective-permute-start.6 = (f32[5,32,16,128]{3,2,1,0:T(8,128)S(1)}, f32[5,32,16,128]{3,2,1,0:T(8,128)}, u32[]{:S(2)}, u32[]{:S(2)}) collective-permute-start(f32[5,32,16,128]{3,2,1,0:T(8,128)S(1)} %slice.57.after), channel_id=1, source_target_pairs={{0,4},{1,5},{2,6},{3,7},{4,0},{5,1},{6,2},{7,3},{8,12},{9,13},{10,... | collective-permute-start | bytes 3932168 | tf_op jit(solution)/shard_map/ppermute | solution.py:16
  11.1 1.4 fusion.24
  15.5 22.9 %collective-permute-done.refs_1_ = f32[161,8,128]{2,1,0:T(8,128)S(1)} collective-permute-done((f32[161,8,128]{2,1,0:T(8,128)}, f32[161,8,128]{2,1,0:T(8,128)S(1)}, u32[]{:S(2)}, u32[]{:S(2)}) %collective-permute-start) | collective-permute-done | bytes 659488 | tf_op jit(solution)/shard_map/ppermute | solution.py:16
  40.0 3.5 %collective-permute-start.3 = (f32[16,5,2,1,128]{4,3,2,1,0:T(1,128)S(1)}, f32[16,5,2,1,128]{4,3,2,1,0:T(1,128)S(1)}, u32[]{:S(2)}, u32[]{:S(2)}) collective-permute-start(f32[16,5,2,1,128]{4,3,2,1,0:T(1,128)S(1)} %get-tuple-element.19), channel_id=1, source_target_pairs={{0,8},{8,16},{16,24},{1,9},{9,17},{17,25},{2,10},{10,18},{18,26},{... | collective-permute-start | bytes 245768 | tf_op jit(solution)/shard_map/ppermute | solution.py:21
  43.6 2.3 %collective-permute-done.3.refs_9_.left = f32[16,5,2,1,128]{4,3,2,1,0:T(1,128)S(1)} collective-permute-done((f32[16,5,2,1,128]{4,3,2,1,0:T(1,128)S(1)}, f32[16,5,2,1,128]{4,3,2,1,0:T(1,128)S(1)}, u32[]{:S(2)}, u32[]{:S(2)}) %collective-permute-start.3) | collective-permute-done | bytes 81952 | tf_op jit(solution)/shard_map/ppermute | solution.py:21
  47.8 4.8 %gathered.2 = (f32[1280,128]{1,0:T(8,128)S(1)}, f32[1312,128]{1,0:T(8,128)}) custom-call(bf16[64,128]{1,0:T(8,128)(2,1)S(1)} %get-tuple-element.35.refs_0_, bf16[64,128]{1,0:T(8,128)(2,1)S(1)} %get-tuple-element.34.refs_1_, f32[1288,128]{1,0:T(8,128)} %bitcast.4.refs_2_, f32[1288,128]{1,0:T(8,128)S(1)} %bitcast.49, f32[1288,128]{1,0:T(8,128)} %bitcast.6.refs_4_, ...), custom_call_target="tpu_custom_call" | custom-call | tf_op jit(solution)/shard_map/gathered/pallas_call | solution.py:130
  54.1 3.0 %collective-permute-start.5 = (f32[1312,128]{1,0:T(8,128)}, f32[1312,128]{1,0:T(8,128)}, u32[]{:S(2)}, u32[]{:S(2)}) collective-permute-start(f32[1312,128]{1,0:T(8,128)} %get-tuple-element.12.refs_1_), channel_id=1, source_target_pairs={{0,4},{1,5},{2,6},{3,7},{4,0},{5,1},{6,2},{7,3},{8,12},{9,13},{10,... | collective-permute-start | bytes 2015240 | tf_op jit(solution)/shard_map/ppermute | solution.py:16
  57.2 13.0 %collective-permute-done.7.refs_0_ = f32[5,32,8,128]{3,2,1,0:T(8,128)S(1)} collective-permute-done((f32[5,32,8,128]{3,2,1,0:T(8,128)}, f32[5,32,8,128]{3,2,1,0:T(8,128)S(1)}, u32[]{:S(2)}, u32[]{:S(2)}) %collective-permute-start.7) | collective-permute-done | bytes 655392 | tf_op jit(solution)/shard_map/ppermute | solution.py:16
  76.4 3.7 %gathered.3 = (f32[1280,128]{1,0:T(8,128)S(1)}, f32[1280,128]{1,0:T(8,128)S(1)}) custom-call(bf16[64,128]{1,0:T(8,128)(2,1)S(1)} %get-tuple-element.31.refs_0_, bf16[64,128]{1,0:T(8,128)(2,1)S(1)} %get-tuple-element.30.refs_1_, f32[1280,128]{1,0:T(8,128)S(1)} %bitcast.52, f32[1280,128]{1,0:T(8,128)S(1)} %bitcast.45, f32[1280,128]{1,0:T(8,128)} %bitcast.16.refs_4_, ...), custom_call_target="tpu_custom_call" | custom-call | tf_op jit(solution)/shard_map/gathered/pallas_call | solution.py:130
  81.0 2.7 %collective-permute-done.6.refs_0_ = f32[5,32,16,128]{3,2,1,0:T(8,128)} collective-permute-done((f32[5,32,16,128]{3,2,1,0:T(8,128)S(1)}, f32[5,32,16,128]{3,2,1,0:T(8,128)}, u32[]{:S(2)}, u32[]{:S(2)}) %collective-permute-start.6) | collective-permute-done | bytes 1310752 | tf_op jit(solution)/shard_map/ppermute | solution.py:16
  85.7 11.6 %collective-permute-done.5 = f32[1312,128]{1,0:T(8,128)} collective-permute-done((f32[1312,128]{1,0:T(8,128)}, f32[1312,128]{1,0:T(8,128)}, u32[]{:S(2)}, u32[]{:S(2)}) %collective-permute-start.5) | collective-permute-done | bytes 671776 | tf_op jit(solution)/shard_map/ppermute | solution.py:16
  99.0 5.0 %crossing.1 = (f32[2560,128]{1,0:T(8,128)S(1)}, f32[2560,128]{1,0:T(8,128)S(1)}) custom-call(bf16[64,128]{1,0:T(8,128)(2,1)S(1)} %get-tuple-element.33.refs_0_, bf16[64,128]{1,0:T(8,128)(2,1)S(1)} %get-tuple-element.32.refs_1_, f32[2560,128]{1,0:T(8,128)S(1)} %bitcast.41, f32[2560,128]{1,0:T(8,128)} %bitcast.22.refs_3_, f32[2560,128]{1,0:T(8,128)} %bitcast.23.refs_4_, ...), custom_call_target="tpu_custom_call" | custom-call | tf_op jit(solution)/shard_map/crossing/pallas_call | solution.py:130
  105.5 3.1 %collective-permute-start.20 = (f32[5,32,8,128]{3,2,1,0:T(8,128)}, f32[5,32,8,128]{3,2,1,0:T(8,128)S(1)}, u32[]{:S(2)}, u32[]{:S(2)}) collective-permute-start(f32[5,32,8,128]{3,2,1,0:T(8,128)} %bitcast.56), channel_id=1, source_target_pairs={{0,4},{1,5},{2,6},{3,7},{4,0},{5,1},{6,2},{7,3},{8,12},{9,13},{10,... | collective-permute-start | bytes 1966088 | tf_op jit(solution)/shard_map/ppermute | solution.py:16
  110.2 6.4 %near.1.near_start.near_end = f32[16,5,2,32,128]{4,3,2,1,0:T(8,128)S(1)} custom-call(f32[4,5,5]{2,1,0:T(8,128)S(1)} %copy.37.cpl, f32[16,5,2,32,128]{4,3,2,1,0:T(8,128)} %state.1, f32[16,5,2,1,128]{4,3,2,1,0:T(1,128)S(1)} %collective-permute-done.3.refs_9_.left, f32[16,5,2,1,128]{4,3,2,1,0:T(1,128)S(1)} %collective-permute-done.4.refs_10_.right, ...), custom_call_target="tpu_custom_call" | custom-call | tf_op jit(solution)/shard_map/near/pallas_call | solution.py:327
  116.7 1.5 copy-done.1
  118.2 2.6 %edge.1 = f32[16,5,2,8,128]{4,3,2,1,0:T(8,128)} custom-call(f32[16,5]{1,0:T(8,128)} %copy-done.16, f32[5,32,8,128]{3,2,1,0:T(8,128)} %bitcast.50, f32[5,32,8,128]{3,2,1,0:T(8,128)} %bitcast.43, f32[16,5,2,32,128]{4,3,2,1,0:T(8,128)} %copy-done.1, f32[16,5,2,32,128]{4,3,2,1,0:T(8,128)} %copy-done.1, f32[5,32,128]{2,1,0:T(8,128)} %copy-done.10, ...), custom_call_target="tpu_custom_call" | custom-call | tf_op jit(solution)/shard_map/edge/pallas_call | solution.py:342
  123.6 4.6 %collective-permute-start.18 = (f32[16,5,2,1,128]{4,3,2,1,0:T(1,128)S(1)}, f32[16,5,2,1,128]{4,3,2,1,0:T(1,128)S(1)}, u32[]{:S(2)}, u32[]{:S(2)}) collective-permute-start(f32[16,5,2,1,128]{4,3,2,1,0:T(1,128)S(1)} %get-tuple-element.25), channel_id=1, source_target_pairs={{0,8},{8,16},{16,24},{1,9},{9,17},{17,25},{2,10},{10,18},{18,26},{... | collective-permute-start | bytes 245768 | tf_op jit(solution)/shard_map/ppermute | solution.py:21
  128.1 2.5 %fusion.2 = f32[2,2,8,1024]{3,1,2,0:T(2,128)S(1)} fusion(f32[8,2,128]{2,0,1:T(8,128)S(1)} %copy.39, f32[8,2,2,128]{3,0,2,1:T(8,128)S(1)} %bitcast.69), kind=kOutput, calls=%fused_computation.3 | convolution fusion | flops 52428800 | bytes 155648 | tf_op jit(solution)/shard_map/bmrf,bmfl->mrbl/dot_general | solution.py:359
  130.9 17.2 %collective-permute-done.20.rest_4_ = f32[5,32,8,128]{3,2,1,0:T(8,128)S(1)} collective-permute-done((f32[5,32,8,128]{3,2,1,0:T(8,128)}, f32[5,32,8,128]{3,2,1,0:T(8,128)S(1)}, u32[]{:S(2)}, u32[]{:S(2)}) %collective-permute-start.20) | collective-permute-done | bytes 655392 | tf_op jit(solution)/shard_map/ppermute | solution.py:16
  148.0 2.2 %collective-permute-done.21.rest_5_ = f32[5,32,16,128]{3,2,1,0:T(8,128)} collective-permute-done((f32[5,32,16,128]{3,2,1,0:T(8,128)S(1)}, f32[5,32,16,128]{3,2,1,0:T(8,128)}, u32[]{:S(2)}, u32[]{:S(2)}) %collective-permute-start.21) | collective-permute-done | bytes 1310752 | tf_op jit(solution)/shard_map/ppermute | solution.py:16
  150.2 8.8 %last.1 = f32[16,5,2,32,128]{4,3,2,1,0:T(8,128)} custom-call(f32[4,5,5]{2,1,0:T(8,128)} %copy-done.15, f32[16,5]{1,0:T(8,128)} %copy-done.16, f32[16,5,2,1,128]{4,3,2,1,0:T(1,128)} %copy-done.19, f32[16,5,2,1,128]{4,3,2,1,0:T(1,128)} %copy-done.18, f32[5,32,128]{2,1,0:T(8,128)} %copy-done.10, f32[32,128]{1,0:T(8,128)} %copy-done.14, ...), custom_call_target="tpu_custom_call" | custom-call | tf_op jit(solution)/shard_map/last/pallas_call | solution.py:367
  162.1 2.0 %collective-permute-start.23 = (f32[2,2]{1,0:T(2,128)S(1)}, f32[2,2]{1,0:T(2,128)S(1)}, u32[]{:S(2)}, u32[]{:S(2)}) collective-permute-start(f32[2,2]{1,0:T(2,128)S(1)} %add.341), channel_id=1, source_target_pairs={{0,2},{1,3},{2,0},{3,1},{4,6},{5,7},{6,4},{7,5},{8,10},{9,11},{10,... | collective-permute-start | bytes 56 | tf_op jit(solution)/shard_map/ppermute | solution.py:16
  164.1 1.5 collective-permute-done.23
  165.7 1.9 %collective-permute-start.24 = (f32[2,2]{1,0:T(2,128)S(1)}, f32[2,2]{1,0:T(2,128)S(1)}, u32[]{:S(2)}, u32[]{:S(2)}) collective-permute-start(f32[2,2]{1,0:T(2,128)S(1)} %add.342), channel_id=1, source_target_pairs={{0,4},{1,5},{2,6},{3,7},{4,0},{5,1},{6,2},{7,3},{8,12},{9,13},{10,... | collective-permute-start | bytes 56 | tf_op jit(solution)/shard_map/ppermute | solution.py:16
  167.6 2.6 %collective-permute-done.24 = f32[2,2]{1,0:T(2,128)S(1)} collective-permute-done((f32[2,2]{1,0:T(2,128)S(1)}, f32[2,2]{1,0:T(2,128)S(1)}, u32[]{:S(2)}, u32[]{:S(2)}) %collective-permute-start.24) | collective-permute-done | bytes 48 | tf_op jit(solution)/shard_map/ppermute | solution.py:16
  170.1 1.5 collective-permute-start.25
  171.6 2.1 %collective-permute-done.25 = f32[2,2]{1,0:T(2,128)S(1)} collective-permute-done((f32[2,2]{1,0:T(2,128)S(1)}, f32[2,2]{1,0:T(2,128)S(1)}, u32[]{:S(2)}, u32[]{:S(2)}) %collective-permute-start.25) | collective-permute-done | bytes 48 | tf_op jit(solution)/shard_map/ppermute | solution.py:16
  173.7 1.5 collective-permute-start.26
  175.2 2.0 %collective-permute-done.26 = f32[2,2]{1,0:T(2,128)S(1)} collective-permute-done((f32[2,2]{1,0:T(2,128)S(1)}, f32[2,2]{1,0:T(2,128)S(1)}, u32[]{:S(2)}, u32[]{:S(2)}) %collective-permute-start.26) | collective-permute-done | bytes 48 | tf_op jit(solution)/shard_map/ppermute | solution.py:16
  (148 shorter events, 29.5 us)
Async XLA Ops:
  0.6 14.7 %copy-start = (f32[5,128,128]{2,1,0:T(8,128)S(1)}, f32[5,128,128]{2,1,0:T(8,128)}, u32[]{:S(2)}) copy-start(f32[5,128,128]{2,1,0:T(8,128)} %param.10) | copy-start | bytes 983044
  5.4 40.5 %collective-permute-start.1 = (f32[161,8,128]{2,1,0:T(8,128)}, f32[161,8,128]{2,1,0:T(8,128)}, u32[]{:S(2)}, u32[]{:S(2)}) collective-permute-start(f32[161,8,128]{2,1,0:T(8,128)} %get-tuple-element.10), channel_id=1, source_target_pairs={{0,1},{1,0},{2,3},{3,2},{4,5},{5,4},{6,7},{7,6},{8,9},{9,8},{10,11... | collective-permute-start | bytes 1978376 | tf_op jit(solution)/shard_map/ppermute | solution.py:16
  5.9 32.5 %collective-permute-start = (f32[161,8,128]{2,1,0:T(8,128)}, f32[161,8,128]{2,1,0:T(8,128)S(1)}, u32[]{:S(2)}, u32[]{:S(2)}) collective-permute-start(f32[161,8,128]{2,1,0:T(8,128)} %get-tuple-element.10), channel_id=1, source_target_pairs={{0,2},{1,3},{2,0},{3,1},{4,6},{5,7},{6,4},{7,5},{8,10},{9,11},{10,... | collective-permute-start | bytes 1978376 | tf_op jit(solution)/shard_map/ppermute | solution.py:16
  8.5 75.2 %collective-permute-start.6 = (f32[5,32,16,128]{3,2,1,0:T(8,128)S(1)}, f32[5,32,16,128]{3,2,1,0:T(8,128)}, u32[]{:S(2)}, u32[]{:S(2)}) collective-permute-start(f32[5,32,16,128]{3,2,1,0:T(8,128)S(1)} %slice.57.after), channel_id=1, source_target_pairs={{0,4},{1,5},{2,6},{3,7},{4,0},{5,1},{6,2},{7,3},{8,12},{9,13},{10,... | collective-permute-start | bytes 3932168 | tf_op jit(solution)/shard_map/ppermute | solution.py:16
  12.5 27.6 %collective-permute-start.4 = (f32[16,5,2,1,128]{4,3,2,1,0:T(1,128)S(1)}, f32[16,5,2,1,128]{4,3,2,1,0:T(1,128)S(1)}, u32[]{:S(2)}, u32[]{:S(2)}) collective-permute-start(f32[16,5,2,1,128]{4,3,2,1,0:T(1,128)S(1)} %get-tuple-element.18), channel_id=1, source_target_pairs={{8,0},{16,8},{24,16},{9,1},{17,9},{25,17},{10,2},{18,10},{26,18},{... | collective-permute-start | bytes 245768 | tf_op jit(solution)/shard_map/ppermute | solution.py:22
  15.3 37.4 %copy-start.10 = (f32[5,32,128]{2,1,0:T(8,128)}, f32[5,32,128]{2,1,0:T(8,128)S(1)}, u32[]{:S(2)}) copy-start(f32[5,32,128]{2,1,0:T(8,128)S(1)} %constant_dynamic-slice_fusion.refs_7_.diag) | copy-start | bytes 245764
  39.2 30.9 %collective-permute-start.7 = (f32[5,32,8,128]{3,2,1,0:T(8,128)}, f32[5,32,8,128]{3,2,1,0:T(8,128)S(1)}, u32[]{:S(2)}, u32[]{:S(2)}) collective-permute-start(f32[5,32,8,128]{3,2,1,0:T(8,128)} %gate.3), channel_id=1, source_target_pairs={{0,2},{1,3},{2,0},{3,1},{4,6},{5,7},{6,4},{7,5},{8,10},{9,11},{10,... | collective-permute-start | bytes 1966088 | tf_op jit(solution)/shard_map/ppermute | solution.py:16
  39.2 7.5 %collective-permute-start.2 = (f32[161,8,128]{2,1,0:T(8,128)}, f32[161,8,128]{2,1,0:T(8,128)}, u32[]{:S(2)}, u32[]{:S(2)}) collective-permute-start(f32[161,8,128]{2,1,0:T(8,128)} %copy-done.7), channel_id=1, source_target_pairs={{0,1},{1,0},{2,3},{3,2},{4,5},{5,4},{6,7},{7,6},{8,9},{9,8},{10,11... | collective-permute-start | bytes 1978376 | tf_op jit(solution)/shard_map/ppermute | solution.py:16
  40.0 31.0 %copy-start.14 = (f32[32,128]{1,0:T(8,128)}, f32[32,128]{1,0:T(8,128)S(1)}, u32[]{:S(2)}) copy-start(f32[32,128]{1,0:T(8,128)S(1)} %fusion.18.refs_6_.keep) | copy-start | bytes 49156
  40.0 5.9 %collective-permute-start.3 = (f32[16,5,2,1,128]{4,3,2,1,0:T(1,128)S(1)}, f32[16,5,2,1,128]{4,3,2,1,0:T(1,128)S(1)}, u32[]{:S(2)}, u32[]{:S(2)}) collective-permute-start(f32[16,5,2,1,128]{4,3,2,1,0:T(1,128)S(1)} %get-tuple-element.19), channel_id=1, source_target_pairs={{0,8},{8,16},{16,24},{1,9},{9,17},{17,25},{2,10},{10,18},{18,26},{... | collective-permute-start | bytes 245768 | tf_op jit(solution)/shard_map/ppermute | solution.py:21
  45.9 26.4 %collective-permute-start.8 = (f32[5,32,8,128]{3,2,1,0:T(8,128)S(1)}, f32[5,32,8,128]{3,2,1,0:T(8,128)}, u32[]{:S(2)}, u32[]{:S(2)}) collective-permute-start(f32[5,32,8,128]{3,2,1,0:T(8,128)S(1)} %get-tuple-element.13), channel_id=1, source_target_pairs={{0,1},{1,0},{2,3},{3,2},{4,5},{5,4},{6,7},{7,6},{8,9},{9,8},{10,11... | collective-permute-start | bytes 1966088 | tf_op jit(solution)/shard_map/ppermute | solution.py:16
  46.0 52.6 %collective-permute-start.13 = (f32[5,32,16,128]{3,2,1,0:T(8,128)S(1)}, f32[5,32,16,128]{3,2,1,0:T(8,128)}, u32[]{:S(2)}, u32[]{:S(2)}) collective-permute-start(f32[5,32,16,128]{3,2,1,0:T(8,128)S(1)} %slice.57.after), channel_id=1, source_target_pairs={{0,1},{1,0},{2,3},{3,2},{4,5},{5,4},{6,7},{7,6},{8,9},{9,8},{10,11... | collective-permute-start | bytes 3932168 | tf_op jit(solution)/shard_map/ppermute | solution.py:16
  54.1 43.2 %collective-permute-start.5 = (f32[1312,128]{1,0:T(8,128)}, f32[1312,128]{1,0:T(8,128)}, u32[]{:S(2)}, u32[]{:S(2)}) collective-permute-start(f32[1312,128]{1,0:T(8,128)} %get-tuple-element.12.refs_1_), channel_id=1, source_target_pairs={{0,4},{1,5},{2,6},{3,7},{4,0},{5,1},{6,2},{7,3},{8,12},{9,13},{10,... | collective-permute-start | bytes 2015240 | tf_op jit(solution)/shard_map/ppermute | solution.py:16
  72.2 1.5 collective-permute-start.12
  72.3 1.6 collective-permute-start.11
  73.7 1.4 collective-permute-start.10
  73.9 1.4 collective-permute-start.9
  85.1 13.5 %collective-permute-start.17 = (f32[5,8,16,128]{3,2,1,0:T(8,128)S(1)}, f32[5,8,16,128]{3,2,1,0:T(8,128)S(1)}, u32[]{:S(2)}, u32[]{:S(2)}) collective-permute-start(f32[5,8,16,128]{3,2,1,0:T(8,128)S(1)} %get-tuple-element.20), channel_id=1, source_target_pairs={{0,1},{1,0},{2,3},{3,2},{4,5},{5,4},{6,7},{7,6},{8,9},{9,8},{10,11... | collective-permute-start | bytes 983048 | tf_op jit(solution)/shard_map/ppermute | solution.py:16
  85.1 13.5 %collective-permute-start.16 = (f32[5,8,16,128]{3,2,1,0:T(8,128)S(1)}, f32[5,8,16,128]{3,2,1,0:T(8,128)S(1)}, u32[]{:S(2)}, u32[]{:S(2)}) collective-permute-start(f32[5,8,16,128]{3,2,1,0:T(8,128)S(1)} %get-tuple-element.21), channel_id=1, source_target_pairs={{0,1},{1,0},{2,3},{3,2},{4,5},{5,4},{6,7},{7,6},{8,9},{9,8},{10,11... | collective-permute-start | bytes 983048 | tf_op jit(solution)/shard_map/ppermute | solution.py:16
  85.6 13.0 %collective-permute-start.15 = (f32[5,8,16,128]{3,2,1,0:T(8,128)S(1)}, f32[5,8,16,128]{3,2,1,0:T(8,128)S(1)}, u32[]{:S(2)}, u32[]{:S(2)}) collective-permute-start(f32[5,8,16,128]{3,2,1,0:T(8,128)S(1)} %get-tuple-element.22), channel_id=1, source_target_pairs={{0,1},{1,0},{2,3},{3,2},{4,5},{5,4},{6,7},{7,6},{8,9},{9,8},{10,11... | collective-permute-start | bytes 983048 | tf_op jit(solution)/shard_map/ppermute | solution.py:16
  97.4 1.6 collective-permute-start.14
  105.1 45.2 %collective-permute-start.21 = (f32[5,32,16,128]{3,2,1,0:T(8,128)S(1)}, f32[5,32,16,128]{3,2,1,0:T(8,128)}, u32[]{:S(2)}, u32[]{:S(2)}) collective-permute-start(f32[5,32,16,128]{3,2,1,0:T(8,128)S(1)} %bitcast.46), channel_id=1, source_target_pairs={{0,2},{1,3},{2,0},{3,1},{4,6},{5,7},{6,4},{7,5},{8,10},{9,11},{10,... | collective-permute-start | bytes 3932168 | tf_op jit(solution)/shard_map/ppermute | solution.py:16
  105.5 42.5 %collective-permute-start.20 = (f32[5,32,8,128]{3,2,1,0:T(8,128)}, f32[5,32,8,128]{3,2,1,0:T(8,128)S(1)}, u32[]{:S(2)}, u32[]{:S(2)}) collective-permute-start(f32[5,32,8,128]{3,2,1,0:T(8,128)} %bitcast.56), channel_id=1, source_target_pairs={{0,4},{1,5},{2,6},{3,7},{4,0},{5,1},{6,2},{7,3},{8,12},{9,13},{10,... | collective-permute-start | bytes 1966088 | tf_op jit(solution)/shard_map/ppermute | solution.py:16
  122.3 8.6 %collective-permute-start.19 = (f32[16,5,2,1,128]{4,3,2,1,0:T(1,128)S(1)}, f32[16,5,2,1,128]{4,3,2,1,0:T(1,128)S(1)}, u32[]{:S(2)}, u32[]{:S(2)}) collective-permute-start(f32[16,5,2,1,128]{4,3,2,1,0:T(1,128)S(1)} %get-tuple-element.24), channel_id=1, source_target_pairs={{8,0},{16,8},{24,16},{9,1},{17,9},{25,17},{10,2},{18,10},{26,18},{... | collective-permute-start | bytes 245768 | tf_op jit(solution)/shard_map/ppermute | solution.py:22
  123.6 7.3 %collective-permute-start.18 = (f32[16,5,2,1,128]{4,3,2,1,0:T(1,128)S(1)}, f32[16,5,2,1,128]{4,3,2,1,0:T(1,128)S(1)}, u32[]{:S(2)}, u32[]{:S(2)}) collective-permute-start(f32[16,5,2,1,128]{4,3,2,1,0:T(1,128)S(1)} %get-tuple-element.25), channel_id=1, source_target_pairs={{0,8},{8,16},{16,24},{1,9},{9,17},{17,25},{2,10},{10,18},{18,26},{... | collective-permute-start | bytes 245768 | tf_op jit(solution)/shard_map/ppermute | solution.py:21
  130.8 19.4 %copy-start.18 = (f32[16,5,2,1,128]{4,3,2,1,0:T(1,128)}, f32[16,5,2,1,128]{4,3,2,1,0:T(1,128)S(1)}, u32[]{:S(2)}) copy-start(f32[16,5,2,1,128]{4,3,2,1,0:T(1,128)S(1)} %collective-permute-done.19.right) | copy-start | bytes 245764
  130.9 19.4 %copy-start.19 = (f32[16,5,2,1,128]{4,3,2,1,0:T(1,128)}, f32[16,5,2,1,128]{4,3,2,1,0:T(1,128)S(1)}, u32[]{:S(2)}) copy-start(f32[16,5,2,1,128]{4,3,2,1,0:T(1,128)S(1)} %collective-permute-done.18.left) | copy-start | bytes 245764
  160.9 1.1 collective-permute-start.22
  162.1 3.6 %collective-permute-start.23 = (f32[2,2]{1,0:T(2,128)S(1)}, f32[2,2]{1,0:T(2,128)S(1)}, u32[]{:S(2)}, u32[]{:S(2)}) collective-permute-start(f32[2,2]{1,0:T(2,128)S(1)} %add.341), channel_id=1, source_target_pairs={{0,2},{1,3},{2,0},{3,1},{4,6},{5,7},{6,4},{7,5},{8,10},{9,11},{10,... | collective-permute-start | bytes 56 | tf_op jit(solution)/shard_map/ppermute | solution.py:16
  165.7 4.5 %collective-permute-start.24 = (f32[2,2]{1,0:T(2,128)S(1)}, f32[2,2]{1,0:T(2,128)S(1)}, u32[]{:S(2)}, u32[]{:S(2)}) collective-permute-start(f32[2,2]{1,0:T(2,128)S(1)} %add.342), channel_id=1, source_target_pairs={{0,4},{1,5},{2,6},{3,7},{4,0},{5,1},{6,2},{7,3},{8,12},{9,13},{10,... | collective-permute-start | bytes 56 | tf_op jit(solution)/shard_map/ppermute | solution.py:16
  170.1 3.6 %collective-permute-start.25 = (f32[2,2]{1,0:T(2,128)S(1)}, f32[2,2]{1,0:T(2,128)S(1)}, u32[]{:S(2)}, u32[]{:S(2)}) collective-permute-start(f32[2,2]{1,0:T(2,128)S(1)} %add.343), channel_id=1, source_target_pairs={{0,8},{8,0},{16,24},{24,16},{1,9},{9,1},{17,25},{25,17},{2,10},{10... | collective-permute-start | bytes 56 | tf_op jit(solution)/shard_map/ppermute | solution.py:16
  173.7 3.6 %collective-permute-start.26 = (f32[2,2]{1,0:T(2,128)S(1)}, f32[2,2]{1,0:T(2,128)S(1)}, u32[]{:S(2)}, u32[]{:S(2)}) collective-permute-start(f32[2,2]{1,0:T(2,128)S(1)} %add.344), channel_id=1, source_target_pairs={{0,16},{8,24},{16,0},{24,8},{1,17},{9,25},{17,1},{25,9},{2,18},{10... | collective-permute-start | bytes 56 | tf_op jit(solution)/shard_map/ppermute | solution.py:16
  (18 other events, 65.5 us)

commit v4 on v3

--- a/solution.py
+++ b/solution.py
@@ -318,12 +318,6 @@
     face_blocks = face_blocks + [b ^ top for b in face_blocks]
     e_far = e_far[:cut].reshape(e_own.shape)
 
-    raws, tab, _ = gather(between, f_got, [e_out], quarter, top)
-    f_own, f_out = transform(tab, raws, (lines, lines), [], "gathered", comps)
-    f_far = swap(f_out, "span", top)
-    raws, tab, _ = gather(inner_rows, far_raw, [f_out], top, quarter)
-    m_own, m_out = transform(tab, raws, (lines, lines), [e_far], "crossing", comps)
-    m_far = swap(m_out, "span", quarter)
     near0 = pl.pallas_call(
         near_kernel,
         grid=grid,
@@ -334,7 +328,13 @@
         compiler_params=PARAMS,
         cost_estimate=FREE,
         name="near",
-    )(coupling, initial_state, left0, right0, m_out)
+    )(coupling, initial_state, left0, right0, e_out)
+    raws, tab, _ = gather(between, f_got, [near0], quarter, top)
+    f_own, f_out = transform(tab, raws, (lines, lines), [], "gathered", comps)
+    f_far = swap(f_out, "span", top)
+    raws, tab, _ = gather(inner_rows, far_raw, [f_out], top, quarter)
+    m_own, m_out = transform(tab, raws, (lines, lines), [e_far], "crossing", comps)
+    m_far = swap(m_out, "span", quarter)
     owns, fars = [e_own, f_own, m_own], [e_far, f_far, m_far]
     pieces = len(owns)
 

time: 179 us -> 179 us (level)
    unnamed x49 -> x51, local copies, waits for them, and re-layouts: 9.7 us -> 9.83 us
where the time goes in v4:
time: 179 us; the launch traced here: 178 us
  waiting for transfers between devices  83.8 us (47%)
  Pallas kernels  33.3 us (19%)
  starting transfers between devices  31.6 us (18%)
  local copies, waits for them, and re-layouts  21.7 us (12%)
  other arithmetic  3.2 us (2%)
  matrix products  3 us (2%)
    ppermute x23, waiting for transfers between devices, swap(): return lax.ppermute(value, axis, [(i, i ^ dist) for i in range(count)])  81.5 us
    ppermute x23, starting transfers between devices, swap(): return lax.ppermute(value, axis, [(i, i ^ dist) for i in range(count)])  20.9 us
    pallas_call x3, Pallas kernels, transform(): pl.pallas_call(functools.partial(transform_kernel, len(raws), 2 + len(raw...  13.5 us
    unnamed x51, local copies, waits for them, and re-layouts  9.83 us
    pallas_call x1, Pallas kernels, shards(): pl.pallas_call(functools.partial(last_kernel, pieces), grid=grid, in_spec...  8.82 us
    ppermute x2, starting transfers between devices, halo(): left = lax.ppermute(tail, axis, [(i, i + 1) for i in range(ends)])  8.09 us
    pallas_call x1, Pallas kernels, shards(): pl.pallas_call(near_kernel, grid=grid, in_specs=[SMEM, by_wave(state_shap...  6.1 us
  transfers between devices with their start and end apart: 27, of which 17 were waited for; matrix products, arithmetic and copies ran while one was open for 8% of the time, Pallas kernels for 10%

profile of v4, /device:TPU:0, one launch (start us, length us, event | category | flops | bytes accessed | tf_op | source)
XLA Modules:
  0.0 177.8 jit_solution(1028092251661127857)
XLA Ops:
  1.5 1.5 slice.57.after
  3.2 2.3 %split.1 = (f32[161,8,128]{2,1,0:T(8,128)}, f32[5,32,8,128]{3,2,1,0:T(8,128)S(1)}) custom-call(f32[5,32,32,128]{3,2,1,0:T(8,128)S(1)} %copy-done.2, f32[5,32,32,128]{3,2,1,0:T(8,128)S(1)} %copy-done.2, f32[8,128]{1,0:T(8,128)S(1)} %maximum_maximum_fusion.faces, f32[5,32,16,128]{3,2,1,0:T(8,128)S(1)} %slice.57.after), custom_call_target="tpu_custom_call" | custom-call | tf_op jit(solution)/shard_map/split/pallas_call | solution.py:58
  5.9 2.6 %collective-permute-start = (f32[161,8,128]{2,1,0:T(8,128)}, f32[161,8,128]{2,1,0:T(8,128)S(1)}, u32[]{:S(2)}, u32[]{:S(2)}) collective-permute-start(f32[161,8,128]{2,1,0:T(8,128)} %get-tuple-element.10), channel_id=1, source_target_pairs={{0,2},{1,3},{2,0},{3,1},{4,6},{5,7},{6,4},{7,5},{8,10},{9,11},{10,... | collective-permute-start | bytes 1978376 | tf_op jit(solution)/shard_map/ppermute | solution.py:16
  8.5 2.6 %collective-permute-start.6 = (f32[5,32,16,128]{3,2,1,0:T(8,128)S(1)}, f32[5,32,16,128]{3,2,1,0:T(8,128)}, u32[]{:S(2)}, u32[]{:S(2)}) collective-permute-start(f32[5,32,16,128]{3,2,1,0:T(8,128)S(1)} %slice.57.after), channel_id=1, source_target_pairs={{0,4},{1,5},{2,6},{3,7},{4,0},{5,1},{6,2},{7,3},{8,12},{9,13},{10,... | collective-permute-start | bytes 3932168 | tf_op jit(solution)/shard_map/ppermute | solution.py:16
  11.1 1.4 fusion.24
  15.5 22.9 %collective-permute-done.refs_1_ = f32[161,8,128]{2,1,0:T(8,128)S(1)} collective-permute-done((f32[161,8,128]{2,1,0:T(8,128)}, f32[161,8,128]{2,1,0:T(8,128)S(1)}, u32[]{:S(2)}, u32[]{:S(2)}) %collective-permute-start) | collective-permute-done | bytes 659488 | tf_op jit(solution)/shard_map/ppermute | solution.py:16
  40.1 3.5 %collective-permute-start.3 = (f32[16,5,2,1,128]{4,3,2,1,0:T(1,128)S(1)}, f32[16,5,2,1,128]{4,3,2,1,0:T(1,128)S(1)}, u32[]{:S(2)}, u32[]{:S(2)}) collective-permute-start(f32[16,5,2,1,128]{4,3,2,1,0:T(1,128)S(1)} %get-tuple-element.19), channel_id=1, source_target_pairs={{0,8},{8,16},{16,24},{1,9},{9,17},{17,25},{2,10},{10,18},{18,26},{... | collective-permute-start | bytes 245768 | tf_op jit(solution)/shard_map/ppermute | solution.py:21
  43.6 2.3 %collective-permute-done.3.refs_9_.left = f32[16,5,2,1,128]{4,3,2,1,0:T(1,128)S(1)} collective-permute-done((f32[16,5,2,1,128]{4,3,2,1,0:T(1,128)S(1)}, f32[16,5,2,1,128]{4,3,2,1,0:T(1,128)S(1)}, u32[]{:S(2)}, u32[]{:S(2)}) %collective-permute-start.3) | collective-permute-done | bytes 81952 | tf_op jit(solution)/shard_map/ppermute | solution.py:21
  48.0 4.8 %gathered.2 = (f32[1280,128]{1,0:T(8,128)S(1)}, f32[1312,128]{1,0:T(8,128)}) custom-call(bf16[64,128]{1,0:T(8,128)(2,1)S(1)} %get-tuple-element.35.refs_0_, bf16[64,128]{1,0:T(8,128)(2,1)S(1)} %get-tuple-element.34.refs_1_, f32[1288,128]{1,0:T(8,128)} %bitcast.4.refs_2_, f32[1288,128]{1,0:T(8,128)S(1)} %bitcast.46, f32[1288,128]{1,0:T(8,128)} %bitcast.6.refs_4_, ...), custom_call_target="tpu_custom_call" | custom-call | tf_op jit(solution)/shard_map/gathered/pallas_call | solution.py:130
  54.3 3.0 %collective-permute-start.5 = (f32[1312,128]{1,0:T(8,128)}, f32[1312,128]{1,0:T(8,128)}, u32[]{:S(2)}, u32[]{:S(2)}) collective-permute-start(f32[1312,128]{1,0:T(8,128)} %get-tuple-element.12.after), channel_id=1, source_target_pairs={{0,4},{1,5},{2,6},{3,7},{4,0},{5,1},{6,2},{7,3},{8,12},{9,13},{10,... | collective-permute-start | bytes 2015240 | tf_op jit(solution)/shard_map/ppermute | solution.py:16
  57.3 6.1 %near.1.refs_1_.near_start.near_end = f32[16,5,2,32,128]{4,3,2,1,0:T(8,128)S(1)} custom-call(f32[4,5,5]{2,1,0:T(8,128)S(1)} %copy.37.cpl, f32[16,5,2,32,128]{4,3,2,1,0:T(8,128)S(1)} %copy-done.6, f32[16,5,2,1,128]{4,3,2,1,0:T(1,128)S(1)} %collective-permute-done.3.refs_9_.left, f32[16,5,2,1,128]{4,3,2,1,0:T(1,128)S(1)} %collective-permute-done.4.refs_10_.right, ...), custom_call_target="tpu_custom_call" | custom-call | tf_op jit(solution)/shard_map/near/pallas_call | solution.py:321
  63.5 1.5 copy-done.1
  64.9 5.2 %collective-permute-done.7.refs_0_ = f32[5,32,8,128]{3,2,1,0:T(8,128)S(1)} collective-permute-done((f32[5,32,8,128]{3,2,1,0:T(8,128)}, f32[5,32,8,128]{3,2,1,0:T(8,128)S(1)}, u32[]{:S(2)}, u32[]{:S(2)}) %collective-permute-start.7) | collective-permute-done | bytes 655392 | tf_op jit(solution)/shard_map/ppermute | solution.py:16
  76.4 3.7 %gathered.3 = (f32[1280,128]{1,0:T(8,128)S(1)}, f32[1280,128]{1,0:T(8,128)S(1)}) custom-call(bf16[64,128]{1,0:T(8,128)(2,1)S(1)} %get-tuple-element.31.refs_0_, bf16[64,128]{1,0:T(8,128)(2,1)S(1)} %get-tuple-element.30.refs_1_, f32[1280,128]{1,0:T(8,128)S(1)} %bitcast.49, f32[1280,128]{1,0:T(8,128)S(1)} %bitcast.45, f32[1280,128]{1,0:T(8,128)} %bitcast.16.refs_4_, ...), custom_call_target="tpu_custom_call" | custom-call | tf_op jit(solution)/shard_map/gathered/pallas_call | solution.py:130
  81.0 2.7 %collective-permute-done.6.refs_0_ = f32[5,32,16,128]{3,2,1,0:T(8,128)} collective-permute-done((f32[5,32,16,128]{3,2,1,0:T(8,128)S(1)}, f32[5,32,16,128]{3,2,1,0:T(8,128)}, u32[]{:S(2)}, u32[]{:S(2)}) %collective-permute-start.6) | collective-permute-done | bytes 1310752 | tf_op jit(solution)/shard_map/ppermute | solution.py:16
  85.7 11.6 %collective-permute-done.5 = f32[1312,128]{1,0:T(8,128)} collective-permute-done((f32[1312,128]{1,0:T(8,128)}, f32[1312,128]{1,0:T(8,128)}, u32[]{:S(2)}, u32[]{:S(2)}) %collective-permute-start.5) | collective-permute-done | bytes 671776 | tf_op jit(solution)/shard_map/ppermute | solution.py:16
  99.0 5.0 %crossing.1 = (f32[2560,128]{1,0:T(8,128)S(1)}, f32[2560,128]{1,0:T(8,128)S(1)}) custom-call(bf16[64,128]{1,0:T(8,128)(2,1)S(1)} %get-tuple-element.33.refs_0_, bf16[64,128]{1,0:T(8,128)(2,1)S(1)} %get-tuple-element.32.refs_1_, f32[2560,128]{1,0:T(8,128)S(1)} %bitcast.41, f32[2560,128]{1,0:T(8,128)} %bitcast.22.refs_3_, f32[2560,128]{1,0:T(8,128)} %bitcast.23.refs_4_, ...), custom_call_target="tpu_custom_call" | custom-call | tf_op jit(solution)/shard_map/crossing/pallas_call | solution.py:130
  105.5 3.1 %collective-permute-start.20 = (f32[5,32,8,128]{3,2,1,0:T(8,128)}, f32[5,32,8,128]{3,2,1,0:T(8,128)S(1)}, u32[]{:S(2)}, u32[]{:S(2)}) collective-permute-start(f32[5,32,8,128]{3,2,1,0:T(8,128)} %bitcast.55), channel_id=1, source_target_pairs={{0,4},{1,5},{2,6},{3,7},{4,0},{5,1},{6,2},{7,3},{8,12},{9,13},{10,... | collective-permute-start | bytes 1966088 | tf_op jit(solution)/shard_map/ppermute | solution.py:16
  110.1 2.7 %edge.1 = f32[16,5,2,8,128]{4,3,2,1,0:T(8,128)} custom-call(f32[16,5]{1,0:T(8,128)} %copy-done.17, f32[5,32,8,128]{3,2,1,0:T(8,128)} %bitcast.47, f32[5,32,8,128]{3,2,1,0:T(8,128)} %bitcast.43, f32[16,5,2,32,128]{4,3,2,1,0:T(8,128)} %copy-done.1, f32[16,5,2,32,128]{4,3,2,1,0:T(8,128)} %copy-done.1, f32[5,32,128]{2,1,0:T(8,128)} %copy-done.10, ...), custom_call_target="tpu_custom_call" | custom-call | tf_op jit(solution)/shard_map/edge/pallas_call | solution.py:342
  115.5 4.6 %collective-permute-start.18 = (f32[16,5,2,1,128]{4,3,2,1,0:T(1,128)S(1)}, f32[16,5,2,1,128]{4,3,2,1,0:T(1,128)S(1)}, u32[]{:S(2)}, u32[]{:S(2)}) collective-permute-start(f32[16,5,2,1,128]{4,3,2,1,0:T(1,128)S(1)} %get-tuple-element.25), channel_id=1, source_target_pairs={{0,8},{8,16},{16,24},{1,9},{9,17},{17,25},{2,10},{10,18},{18,26},{... | collective-permute-start | bytes 245768 | tf_op jit(solution)/shard_map/ppermute | solution.py:21
  120.1 2.5 %fusion.2 = f32[2,2,8,1024]{3,1,2,0:T(2,128)S(1)} fusion(f32[8,2,128]{2,0,1:T(8,128)S(1)} %copy.39, f32[8,2,2,128]{3,0,2,1:T(8,128)S(1)} %bitcast.68), kind=kOutput, calls=%fused_computation.3 | convolution fusion | flops 52428800 | bytes 155648 | tf_op jit(solution)/shard_map/bmrf,bmfl->mrbl/dot_general | solution.py:359
  122.8 25.2 %collective-permute-done.20.rest_4_ = f32[5,32,8,128]{3,2,1,0:T(8,128)S(1)} collective-permute-done((f32[5,32,8,128]{3,2,1,0:T(8,128)}, f32[5,32,8,128]{3,2,1,0:T(8,128)S(1)}, u32[]{:S(2)}, u32[]{:S(2)}) %collective-permute-start.20) | collective-permute-done | bytes 655392 | tf_op jit(solution)/shard_map/ppermute | solution.py:16
  148.0 2.2 %collective-permute-done.21.rest_5_ = f32[5,32,16,128]{3,2,1,0:T(8,128)} collective-permute-done((f32[5,32,16,128]{3,2,1,0:T(8,128)S(1)}, f32[5,32,16,128]{3,2,1,0:T(8,128)}, u32[]{:S(2)}, u32[]{:S(2)}) %collective-permute-start.21) | collective-permute-done | bytes 1310752 | tf_op jit(solution)/shard_map/ppermute | solution.py:16
  150.2 8.8 %last.1 = f32[16,5,2,32,128]{4,3,2,1,0:T(8,128)} custom-call(f32[4,5,5]{2,1,0:T(8,128)} %copy-done.16, f32[16,5]{1,0:T(8,128)} %copy-done.17, f32[16,5,2,1,128]{4,3,2,1,0:T(1,128)} %copy-done.20, f32[16,5,2,1,128]{4,3,2,1,0:T(1,128)} %copy-done.19, f32[5,32,128]{2,1,0:T(8,128)} %copy-done.10, f32[32,128]{1,0:T(8,128)} %copy-done.15, ...), custom_call_target="tpu_custom_call" | custom-call | tf_op jit(solution)/shard_map/last/pallas_call | solution.py:367
  162.0 2.0 %collective-permute-start.23 = (f32[2,2]{1,0:T(2,128)S(1)}, f32[2,2]{1,0:T(2,128)S(1)}, u32[]{:S(2)}, u32[]{:S(2)}) collective-permute-start(f32[2,2]{1,0:T(2,128)S(1)} %add.341), channel_id=1, source_target_pairs={{0,2},{1,3},{2,0},{3,1},{4,6},{5,7},{6,4},{7,5},{8,10},{9,11},{10,... | collective-permute-start | bytes 56 | tf_op jit(solution)/shard_map/ppermute | solution.py:16
  164.0 1.6 collective-permute-done.23
  165.6 1.9 %collective-permute-start.24 = (f32[2,2]{1,0:T(2,128)S(1)}, f32[2,2]{1,0:T(2,128)S(1)}, u32[]{:S(2)}, u32[]{:S(2)}) collective-permute-start(f32[2,2]{1,0:T(2,128)S(1)} %add.342), channel_id=1, source_target_pairs={{0,4},{1,5},{2,6},{3,7},{4,0},{5,1},{6,2},{7,3},{8,12},{9,13},{10,... | collective-permute-start | bytes 56 | tf_op jit(solution)/shard_map/ppermute | solution.py:16
  167.5 2.6 %collective-permute-done.24 = f32[2,2]{1,0:T(2,128)S(1)} collective-permute-done((f32[2,2]{1,0:T(2,128)S(1)}, f32[2,2]{1,0:T(2,128)S(1)}, u32[]{:S(2)}, u32[]{:S(2)}) %collective-permute-start.24) | collective-permute-done | bytes 48 | tf_op jit(solution)/shard_map/ppermute | solution.py:16
  170.1 1.5 collective-permute-start.25
  171.6 2.1 %collective-permute-done.25 = f32[2,2]{1,0:T(2,128)S(1)} collective-permute-done((f32[2,2]{1,0:T(2,128)S(1)}, f32[2,2]{1,0:T(2,128)S(1)}, u32[]{:S(2)}, u32[]{:S(2)}) %collective-permute-start.25) | collective-permute-done | bytes 48 | tf_op jit(solution)/shard_map/ppermute | solution.py:16
  173.7 1.5 collective-permute-start.26
  175.2 2.0 %collective-permute-done.26 = f32[2,2]{1,0:T(2,128)S(1)} collective-permute-done((f32[2,2]{1,0:T(2,128)S(1)}, f32[2,2]{1,0:T(2,128)S(1)}, u32[]{:S(2)}, u32[]{:S(2)}) %collective-permute-start.26) | collective-permute-done | bytes 48 | tf_op jit(solution)/shard_map/ppermute | solution.py:16
  (150 shorter events, 29.8 us)
Async XLA Ops:
  5.4 41.2 %copy-start.21 = (f32[4,5,5]{2,0,1:T(4,128)S(1)}, f32[4,5,5]{2,0,1:T(4,128)}, u32[]{:S(2)}) copy-start(f32[4,5,5]{2,0,1:T(4,128)} %param.12) | copy-start | bytes 1204
  5.4 40.5 %collective-permute-start.1 = (f32[161,8,128]{2,1,0:T(8,128)}, f32[161,8,128]{2,1,0:T(8,128)}, u32[]{:S(2)}, u32[]{:S(2)}) collective-permute-start(f32[161,8,128]{2,1,0:T(8,128)} %get-tuple-element.10), channel_id=1, source_target_pairs={{0,1},{1,0},{2,3},{3,2},{4,5},{5,4},{6,7},{7,6},{8,9},{9,8},{10,11... | collective-permute-start | bytes 1978376 | tf_op jit(solution)/shard_map/ppermute | solution.py:16
  5.9 32.5 %collective-permute-start = (f32[161,8,128]{2,1,0:T(8,128)}, f32[161,8,128]{2,1,0:T(8,128)S(1)}, u32[]{:S(2)}, u32[]{:S(2)}) collective-permute-start(f32[161,8,128]{2,1,0:T(8,128)} %get-tuple-element.10), channel_id=1, source_target_pairs={{0,2},{1,3},{2,0},{3,1},{4,6},{5,7},{6,4},{7,5},{8,10},{9,11},{10,... | collective-permute-start | bytes 1978376 | tf_op jit(solution)/shard_map/ppermute | solution.py:16
  8.5 75.2 %collective-permute-start.6 = (f32[5,32,16,128]{3,2,1,0:T(8,128)S(1)}, f32[5,32,16,128]{3,2,1,0:T(8,128)}, u32[]{:S(2)}, u32[]{:S(2)}) collective-permute-start(f32[5,32,16,128]{3,2,1,0:T(8,128)S(1)} %slice.57.after), channel_id=1, source_target_pairs={{0,4},{1,5},{2,6},{3,7},{4,0},{5,1},{6,2},{7,3},{8,12},{9,13},{10,... | collective-permute-start | bytes 3932168 | tf_op jit(solution)/shard_map/ppermute | solution.py:16
  12.5 27.6 %collective-permute-start.4 = (f32[16,5,2,1,128]{4,3,2,1,0:T(1,128)S(1)}, f32[16,5,2,1,128]{4,3,2,1,0:T(1,128)S(1)}, u32[]{:S(2)}, u32[]{:S(2)}) collective-permute-start(f32[16,5,2,1,128]{4,3,2,1,0:T(1,128)S(1)} %get-tuple-element.18), channel_id=1, source_target_pairs={{8,0},{16,8},{24,16},{9,1},{17,9},{25,17},{10,2},{18,10},{26,18},{... | collective-permute-start | bytes 245768 | tf_op jit(solution)/shard_map/ppermute | solution.py:22
  15.4 37.5 %copy-start.10 = (f32[5,32,128]{2,1,0:T(8,128)}, f32[5,32,128]{2,1,0:T(8,128)S(1)}, u32[]{:S(2)}) copy-start(f32[5,32,128]{2,1,0:T(8,128)S(1)} %constant_dynamic-slice_fusion.refs_7_.diag) | copy-start | bytes 245764
  39.3 30.9 %collective-permute-start.7 = (f32[5,32,8,128]{3,2,1,0:T(8,128)}, f32[5,32,8,128]{3,2,1,0:T(8,128)S(1)}, u32[]{:S(2)}, u32[]{:S(2)}) collective-permute-start(f32[5,32,8,128]{3,2,1,0:T(8,128)} %gate.3), channel_id=1, source_target_pairs={{0,2},{1,3},{2,0},{3,1},{4,6},{5,7},{6,4},{7,5},{8,10},{9,11},{10,... | collective-permute-start | bytes 1966088 | tf_op jit(solution)/shard_map/ppermute | solution.py:16
  39.3 7.5 %collective-permute-start.2 = (f32[161,8,128]{2,1,0:T(8,128)}, f32[161,8,128]{2,1,0:T(8,128)}, u32[]{:S(2)}, u32[]{:S(2)}) collective-permute-start(f32[161,8,128]{2,1,0:T(8,128)} %copy-done.7), channel_id=1, source_target_pairs={{0,1},{1,0},{2,3},{3,2},{4,5},{5,4},{6,7},{7,6},{8,9},{9,8},{10,11... | collective-permute-start | bytes 1978376 | tf_op jit(solution)/shard_map/ppermute | solution.py:16
  40.0 23.4 %copy-start.15 = (f32[32,128]{1,0:T(8,128)}, f32[32,128]{1,0:T(8,128)S(1)}, u32[]{:S(2)}) copy-start(f32[32,128]{1,0:T(8,128)S(1)} %fusion.18.refs_6_.keep) | copy-start | bytes 49156
  40.1 5.9 %collective-permute-start.3 = (f32[16,5,2,1,128]{4,3,2,1,0:T(1,128)S(1)}, f32[16,5,2,1,128]{4,3,2,1,0:T(1,128)S(1)}, u32[]{:S(2)}, u32[]{:S(2)}) collective-permute-start(f32[16,5,2,1,128]{4,3,2,1,0:T(1,128)S(1)} %get-tuple-element.19), channel_id=1, source_target_pairs={{0,8},{8,16},{16,24},{1,9},{9,17},{17,25},{2,10},{10,18},{18,26},{... | collective-permute-start | bytes 245768 | tf_op jit(solution)/shard_map/ppermute | solution.py:21
  46.0 26.4 %collective-permute-start.8 = (f32[5,32,8,128]{3,2,1,0:T(8,128)S(1)}, f32[5,32,8,128]{3,2,1,0:T(8,128)}, u32[]{:S(2)}, u32[]{:S(2)}) collective-permute-start(f32[5,32,8,128]{3,2,1,0:T(8,128)S(1)} %get-tuple-element.13), channel_id=1, source_target_pairs={{0,1},{1,0},{2,3},{3,2},{4,5},{5,4},{6,7},{7,6},{8,9},{9,8},{10,11... | collective-permute-start | bytes 1966088 | tf_op jit(solution)/shard_map/ppermute | solution.py:16
  46.0 52.6 %collective-permute-start.13 = (f32[5,32,16,128]{3,2,1,0:T(8,128)S(1)}, f32[5,32,16,128]{3,2,1,0:T(8,128)}, u32[]{:S(2)}, u32[]{:S(2)}) collective-permute-start(f32[5,32,16,128]{3,2,1,0:T(8,128)S(1)} %slice.57.after), channel_id=1, source_target_pairs={{0,1},{1,0},{2,3},{3,2},{4,5},{5,4},{6,7},{7,6},{8,9},{9,8},{10,11... | collective-permute-start | bytes 3932168 | tf_op jit(solution)/shard_map/ppermute | solution.py:16
  54.3 43.1 %collective-permute-start.5 = (f32[1312,128]{1,0:T(8,128)}, f32[1312,128]{1,0:T(8,128)}, u32[]{:S(2)}, u32[]{:S(2)}) collective-permute-start(f32[1312,128]{1,0:T(8,128)} %get-tuple-element.12.after), channel_id=1, source_target_pairs={{0,4},{1,5},{2,6},{3,7},{4,0},{5,1},{6,2},{7,3},{8,12},{9,13},{10,... | collective-permute-start | bytes 2015240 | tf_op jit(solution)/shard_map/ppermute | solution.py:16
  72.2 1.5 collective-permute-start.12
  72.3 1.6 collective-permute-start.11
  73.7 1.4 collective-permute-start.10
  73.9 1.4 collective-permute-start.9
  85.1 13.5 %collective-permute-start.17 = (f32[5,8,16,128]{3,2,1,0:T(8,128)S(1)}, f32[5,8,16,128]{3,2,1,0:T(8,128)S(1)}, u32[]{:S(2)}, u32[]{:S(2)}) collective-permute-start(f32[5,8,16,128]{3,2,1,0:T(8,128)S(1)} %get-tuple-element.20), channel_id=1, source_target_pairs={{0,1},{1,0},{2,3},{3,2},{4,5},{5,4},{6,7},{7,6},{8,9},{9,8},{10,11... | collective-permute-start | bytes 983048 | tf_op jit(solution)/shard_map/ppermute | solution.py:16
  85.1 13.5 %collective-permute-start.16 = (f32[5,8,16,128]{3,2,1,0:T(8,128)S(1)}, f32[5,8,16,128]{3,2,1,0:T(8,128)S(1)}, u32[]{:S(2)}, u32[]{:S(2)}) collective-permute-start(f32[5,8,16,128]{3,2,1,0:T(8,128)S(1)} %get-tuple-element.21), channel_id=1, source_target_pairs={{0,1},{1,0},{2,3},{3,2},{4,5},{5,4},{6,7},{7,6},{8,9},{9,8},{10,11... | collective-permute-start | bytes 983048 | tf_op jit(solution)/shard_map/ppermute | solution.py:16
  85.6 13.0 %collective-permute-start.15 = (f32[5,8,16,128]{3,2,1,0:T(8,128)S(1)}, f32[5,8,16,128]{3,2,1,0:T(8,128)S(1)}, u32[]{:S(2)}, u32[]{:S(2)}) collective-permute-start(f32[5,8,16,128]{3,2,1,0:T(8,128)S(1)} %get-tuple-element.22), channel_id=1, source_target_pairs={{0,1},{1,0},{2,3},{3,2},{4,5},{5,4},{6,7},{7,6},{8,9},{9,8},{10,11... | collective-permute-start | bytes 983048 | tf_op jit(solution)/shard_map/ppermute | solution.py:16
  97.4 1.6 collective-permute-start.14
  105.0 45.2 %collective-permute-start.21 = (f32[5,32,16,128]{3,2,1,0:T(8,128)S(1)}, f32[5,32,16,128]{3,2,1,0:T(8,128)}, u32[]{:S(2)}, u32[]{:S(2)}) collective-permute-start(f32[5,32,16,128]{3,2,1,0:T(8,128)S(1)} %bitcast.51), channel_id=1, source_target_pairs={{0,2},{1,3},{2,0},{3,1},{4,6},{5,7},{6,4},{7,5},{8,10},{9,11},{10,... | collective-permute-start | bytes 3932168 | tf_op jit(solution)/shard_map/ppermute | solution.py:16
  105.5 42.5 %collective-permute-start.20 = (f32[5,32,8,128]{3,2,1,0:T(8,128)}, f32[5,32,8,128]{3,2,1,0:T(8,128)S(1)}, u32[]{:S(2)}, u32[]{:S(2)}) collective-permute-start(f32[5,32,8,128]{3,2,1,0:T(8,128)} %bitcast.55), channel_id=1, source_target_pairs={{0,4},{1,5},{2,6},{3,7},{4,0},{5,1},{6,2},{7,3},{8,12},{9,13},{10,... | collective-permute-start | bytes 1966088 | tf_op jit(solution)/shard_map/ppermute | solution.py:16
  114.2 8.6 %collective-permute-start.19 = (f32[16,5,2,1,128]{4,3,2,1,0:T(1,128)S(1)}, f32[16,5,2,1,128]{4,3,2,1,0:T(1,128)S(1)}, u32[]{:S(2)}, u32[]{:S(2)}) collective-permute-start(f32[16,5,2,1,128]{4,3,2,1,0:T(1,128)S(1)} %get-tuple-element.24), channel_id=1, source_target_pairs={{8,0},{16,8},{24,16},{9,1},{17,9},{25,17},{10,2},{18,10},{26,18},{... | collective-permute-start | bytes 245768 | tf_op jit(solution)/shard_map/ppermute | solution.py:22
  115.5 7.3 %collective-permute-start.18 = (f32[16,5,2,1,128]{4,3,2,1,0:T(1,128)S(1)}, f32[16,5,2,1,128]{4,3,2,1,0:T(1,128)S(1)}, u32[]{:S(2)}, u32[]{:S(2)}) collective-permute-start(f32[16,5,2,1,128]{4,3,2,1,0:T(1,128)S(1)} %get-tuple-element.25), channel_id=1, source_target_pairs={{0,8},{8,16},{16,24},{1,9},{9,17},{17,25},{2,10},{10,18},{18,26},{... | collective-permute-start | bytes 245768 | tf_op jit(solution)/shard_map/ppermute | solution.py:21
  122.8 27.4 %copy-start.19 = (f32[16,5,2,1,128]{4,3,2,1,0:T(1,128)}, f32[16,5,2,1,128]{4,3,2,1,0:T(1,128)S(1)}, u32[]{:S(2)}) copy-start(f32[16,5,2,1,128]{4,3,2,1,0:T(1,128)S(1)} %collective-permute-done.19.right) | copy-start | bytes 245764
  122.8 27.4 %copy-start.20 = (f32[16,5,2,1,128]{4,3,2,1,0:T(1,128)}, f32[16,5,2,1,128]{4,3,2,1,0:T(1,128)S(1)}, u32[]{:S(2)}) copy-start(f32[16,5,2,1,128]{4,3,2,1,0:T(1,128)S(1)} %collective-permute-done.18.left) | copy-start | bytes 245764
  160.9 1.1 collective-permute-start.22
  162.0 3.6 %collective-permute-start.23 = (f32[2,2]{1,0:T(2,128)S(1)}, f32[2,2]{1,0:T(2,128)S(1)}, u32[]{:S(2)}, u32[]{:S(2)}) collective-permute-start(f32[2,2]{1,0:T(2,128)S(1)} %add.341), channel_id=1, source_target_pairs={{0,2},{1,3},{2,0},{3,1},{4,6},{5,7},{6,4},{7,5},{8,10},{9,11},{10,... | collective-permute-start | bytes 56 | tf_op jit(solution)/shard_map/ppermute | solution.py:16
  165.6 4.5 %collective-permute-start.24 = (f32[2,2]{1,0:T(2,128)S(1)}, f32[2,2]{1,0:T(2,128)S(1)}, u32[]{:S(2)}, u32[]{:S(2)}) collective-permute-start(f32[2,2]{1,0:T(2,128)S(1)} %add.342), channel_id=1, source_target_pairs={{0,4},{1,5},{2,6},{3,7},{4,0},{5,1},{6,2},{7,3},{8,12},{9,13},{10,... | collective-permute-start | bytes 56 | tf_op jit(solution)/shard_map/ppermute | solution.py:16
  170.1 3.6 %collective-permute-start.25 = (f32[2,2]{1,0:T(2,128)S(1)}, f32[2,2]{1,0:T(2,128)S(1)}, u32[]{:S(2)}, u32[]{:S(2)}) collective-permute-start(f32[2,2]{1,0:T(2,128)S(1)} %add.343), channel_id=1, source_target_pairs={{0,8},{8,0},{16,24},{24,16},{1,9},{9,1},{17,25},{25,17},{2,10},{10... | collective-permute-start | bytes 56 | tf_op jit(solution)/shard_map/ppermute | solution.py:16
  173.7 3.6 %collective-permute-start.26 = (f32[2,2]{1,0:T(2,128)S(1)}, f32[2,2]{1,0:T(2,128)S(1)}, u32[]{:S(2)}, u32[]{:S(2)}) collective-permute-start(f32[2,2]{1,0:T(2,128)S(1)} %add.344), channel_id=1, source_target_pairs={{0,16},{8,24},{16,0},{24,8},{1,17},{9,25},{17,1},{25,9},{2,18},{10... | collective-permute-start | bytes 56 | tf_op jit(solution)/shard_map/ppermute | solution.py:16
  (19 other events, 83.6 us)
